TPU v7x, 32 devices: a whole 2x2x4 slice. The times are simulated.
32 devices in a mesh: dp: 32 (over z, y, x, core).
Axes of the slice: x: 2, y: 2, z: 4, core: 2. Of those that a mesh axis runs over, the one named last changes fastest.
Arguments:
- tokens: bfloat16 [256, 128, 768], P('dp'), may hold values from -6 to 6
- segment_ids: int32 [256, 128], P('dp'), may hold values from 0 to 3, never falling along the last dimension, each value on 1 to 64 neighbouring positions
- time_embed: bfloat16 [256, 768], P('dp'), may hold values from -4 to 4
- norm1_gain: bfloat16 [768], P('dp'), may hold values from 0.25 to 1.75
- norm1_shift: bfloat16 [768], P('dp'), may hold values from -2 to 2
- w_qkv: bfloat16 [768, 2304], P('dp'), may hold values from -0.21875 to 0.21875
- b_query: bfloat16 [768], P('dp'), may hold values from -2 to 2
- b_value: bfloat16 [768], P('dp'), may hold values from -2 to 2
- w_proj: bfloat16 [768, 768], P('dp'), may hold values from -1.25 to 1.25
- b_proj: bfloat16 [768], P('dp'), may hold values from -2 to 2
- norm2_gain: bfloat16 [768], P('dp'), may hold values from 0.25 to 1.75
- norm2_shift: bfloat16 [768], P('dp'), may hold values from -2 to 2
- w_fc: bfloat16 [768, 3072], P('dp'), may hold values from -0.21875 to 0.21875
- b_fc: bfloat16 [3072], P('dp'), may hold values from -2 to 2
- w_out: bfloat16 [3072, 768], P('dp'), may hold values from -0.109375 to 0.109375
- b_out: bfloat16 [768], P('dp'), may hold values from -2 to 2
- cotangent: bfloat16 [256, 128, 768], P('dp'), may hold values from -6 to 6
Outputs:
- layer_out: bfloat16 [256, 128, 768], P('dp')
- d_tokens: float32 [256, 128, 768], P('dp')
- d_time: float32 [256, 768], P('dp')
- d_norm1_gain: float32 [768], P('dp')
- d_norm1_shift: float32 [768], P('dp')
- d_w_qkv: float32 [768, 2304], P('dp')
- d_b_query: float32 [768], P('dp')
- d_b_value: float32 [768], P('dp')
- d_w_proj: float32 [768, 768], P('dp')
- d_b_proj: float32 [768], P('dp')
- d_norm2_gain: float32 [768], P('dp')
- d_norm2_shift: float32 [768], P('dp')
- d_w_fc: float32 [768, 3072], P('dp')
- d_b_fc: float32 [3072], P('dp')
- d_w_out: float32 [3072, 768], P('dp')
- d_b_out: float32 [768], P('dp')
Inputs may be any that keep to these rules, and one draw needn't show every extreme that they name: `segment_ids`: within a row the ids never fall, and each id covers at most 64 consecutive tokens.
All inputs are finite; a program needn't handle non-finite values.
Results may differ from a plain program's by a relative error of at most 0.012.
Values may be sent and summed in bfloat16 or wider, within the bound.
No kernel may reach another device: no remote copies, remote signals or barrier semaphores. Data moves between devices by JAX's collectives and lax.ppermute only.
A program may use at most 192 MiB of HBM per device.

v0:
```python
import math

import jax
import jax.numpy as jnp
from jax import lax
from jax.sharding import PartitionSpec as P

HD = 64


norm_eps = 1e-05
masked_fill = -1e30


def scaled_norm(values, gain_vec):
    center_mean = jnp.mean(values, axis=-1, keepdims=True)
    centered = values - center_mean
    spread = jnp.mean(centered * centered, axis=-1, keepdims=True)
    return centered * lax.rsqrt(spread + norm_eps) * gain_vec


def exact_gelu(values):
    return jax.nn.gelu(values, approximate=False)


def masked_scores(queries, key_heads, same_doc, score_scale):
    raw_scores = (
        jnp.einsum("rqhe,rkhe->rhqk", queries, key_heads, preferred_element_type=jnp.float32)
        * score_scale
    )
    return jnp.where(same_doc[:, None, :, :], raw_scores, masked_fill)


def on_device(
    tokens,
    segment_ids,
    time_embed,
    norm1_gain,
    norm1_shift,
    w_qkv,
    b_query,
    b_value,
    w_proj,
    b_proj,
    norm2_gain,
    norm2_shift,
    w_fc,
    b_fc,
    w_out,
    b_out,
    cotangent,
):
    row_count, row_len, feat_width = tokens.shape
    head_count = feat_width // HD
    tok_count = row_count * row_len
    grad_scale = 1.0 / math.sqrt(tok_count * lax.axis_size("dp"))
    score_scale = HD ** (-0.5)
    attn_full = (
        lax.all_gather(w_qkv, "dp", axis=0, tiled=True),
        lax.all_gather(w_proj, "dp", axis=0, tiled=True),
        lax.all_gather(norm1_gain, "dp", axis=0, tiled=True),
        lax.all_gather(norm1_shift, "dp", axis=0, tiled=True),
        lax.all_gather(b_query, "dp", axis=0, tiled=True),
        lax.all_gather(b_value, "dp", axis=0, tiled=True),
        lax.all_gather(b_proj, "dp", axis=0, tiled=True),
    )
    mlp_full = (
        lax.all_gather(w_fc, "dp", axis=0, tiled=True),
        lax.all_gather(w_out, "dp", axis=0, tiled=True),
        lax.all_gather(norm2_gain, "dp", axis=0, tiled=True),
        lax.all_gather(norm2_shift, "dp", axis=0, tiled=True),
        lax.all_gather(b_fc, "dp", axis=0, tiled=True),
        lax.all_gather(b_out, "dp", axis=0, tiled=True),
    )
    qkv_w, proj_w, attn_gain, attn_shift, query_bias, value_bias, proj_bias = attn_full
    fc_w, out_w, mlp_gain, mlp_shift, fc_bias, out_bias = mlp_full
    inputs = (tokens.astype(jnp.float32) + time_embed.astype(jnp.float32)[:, None, :]).reshape(
        tok_count, feat_width
    )
    normed1 = (
        scaled_norm(inputs, attn_gain.astype(jnp.float32)) + attn_shift.astype(jnp.float32)
    ).astype(jnp.bfloat16)
    qkv_bias = jnp.concatenate([query_bias, jnp.zeros_like(query_bias), value_bias]).astype(
        jnp.float32
    )
    qkv_all = (jnp.dot(normed1, qkv_w, preferred_element_type=jnp.float32) + qkv_bias).astype(
        jnp.bfloat16
    )
    qkv_heads = qkv_all.reshape(row_count, row_len, 3, head_count, HD)
    queries = qkv_heads[:, :, 0]
    key_heads = qkv_heads[:, :, 1]
    value_heads = qkv_heads[:, :, 2]
    same_doc = segment_ids[:, :, None] == segment_ids[:, None, :]
    scores = masked_scores(queries, key_heads, same_doc, score_scale)
    row_top = jnp.max(scores, axis=-1, keepdims=True)
    shifted = jnp.exp(scores - row_top)
    row_sum = jnp.sum(shifted, axis=-1, keepdims=True)
    log_total = row_top + jnp.log(row_sum)
    weights = (shifted / row_sum).astype(jnp.bfloat16)
    attended = jnp.einsum(
        "rhqk,rkhe->rqhe", weights, value_heads, preferred_element_type=jnp.float32
    )
    attended = attended.reshape(tok_count, feat_width).astype(jnp.bfloat16)
    hidden = (
        inputs
        + jnp.dot(attended, proj_w, preferred_element_type=jnp.float32)
        + proj_bias.astype(jnp.float32)
    )
    normed2 = (
        scaled_norm(hidden, mlp_gain.astype(jnp.float32)) + mlp_shift.astype(jnp.float32)
    ).astype(jnp.bfloat16)
    pre_act = jnp.dot(normed2, fc_w, preferred_element_type=jnp.float32) + fc_bias.astype(
        jnp.float32
    )
    activated = exact_gelu(pre_act).astype(jnp.bfloat16)
    summed_out = (
        hidden
        + jnp.dot(activated, out_w, preferred_element_type=jnp.float32)
        + out_bias.astype(jnp.float32)
    )
    layer_out = summed_out.astype(jnp.bfloat16).reshape(row_count, row_len, feat_width)
    fc_w, out_w, mlp_gain = (
        lax.all_gather(w_fc, "dp", axis=0, tiled=True),
        lax.all_gather(w_out, "dp", axis=0, tiled=True),
        lax.all_gather(norm2_gain, "dp", axis=0, tiled=True),
    )
    grad_out = cotangent.reshape(tok_count, feat_width)
    d_w_out = jnp.einsum("nf,nd->fd", activated, grad_out, preferred_element_type=jnp.float32)
    d_b_out = jnp.sum(grad_out.astype(jnp.float32), axis=0)
    d_act = jnp.einsum("nd,fd->nf", grad_out, out_w, preferred_element_type=jnp.float32)
    unused_gelu, gelu_pull = jax.vjp(exact_gelu, pre_act)
    d_pre = gelu_pull(d_act)[0].astype(jnp.bfloat16)
    d_w_fc = jnp.einsum("nd,nf->df", normed2, d_pre, preferred_element_type=jnp.float32)
    d_b_fc = jnp.sum(d_pre.astype(jnp.float32), axis=0)
    d_normed2 = jnp.einsum("nf,df->nd", d_pre, fc_w, preferred_element_type=jnp.float32)
    unused_norm, norm2_pull = jax.vjp(scaled_norm, hidden, mlp_gain.astype(jnp.float32))
    d_hidden_norm, d_mlp_gain = norm2_pull(d_normed2)
    d_mlp_shift = jnp.sum(d_normed2, axis=0)
    d_hidden = grad_out.astype(jnp.float32) + d_hidden_norm
    mlp_owned = (
        lax.psum_scatter(d_w_fc, "dp", scatter_dimension=0, tiled=True),
        lax.psum_scatter(d_w_out, "dp", scatter_dimension=0, tiled=True),
        lax.psum_scatter(d_mlp_gain, "dp", scatter_dimension=0, tiled=True),
        lax.psum_scatter(d_mlp_shift, "dp", scatter_dimension=0, tiled=True),
        lax.psum_scatter(d_b_fc, "dp", scatter_dimension=0, tiled=True),
        lax.psum_scatter(d_b_out, "dp", scatter_dimension=0, tiled=True),
    )
    qkv_w, proj_w, attn_gain = (
        lax.all_gather(w_qkv, "dp", axis=0, tiled=True),
        lax.all_gather(w_proj, "dp", axis=0, tiled=True),
        lax.all_gather(norm1_gain, "dp", axis=0, tiled=True),
    )
    d_branch = d_hidden.astype(jnp.bfloat16)
    d_b_proj = jnp.sum(d_branch.astype(jnp.float32), axis=0)
    d_w_proj = jnp.einsum("nd,ne->de", attended, d_branch, preferred_element_type=jnp.float32)
    d_mixed = jnp.einsum("ne,de->nd", d_branch, proj_w, preferred_element_type=jnp.float32)
    d_mixed = d_mixed.astype(jnp.bfloat16).reshape(row_count, row_len, head_count, HD)
    scores = masked_scores(queries, key_heads, same_doc, score_scale)
    exact_probs = jnp.exp(scores - log_total)
    weights = exact_probs.astype(jnp.bfloat16)
    d_value = jnp.einsum("rhqk,rqhe->rkhe", weights, d_mixed, preferred_element_type=jnp.float32)
    d_probs = jnp.einsum(
        "rqhe,rkhe->rhqk", d_mixed, value_heads, preferred_element_type=jnp.float32
    )
    row_delta = jnp.sum(d_probs * exact_probs, axis=-1, keepdims=True)
    d_scores = (exact_probs * (d_probs - row_delta)).astype(jnp.bfloat16)
    d_query = (
        jnp.einsum("rhqk,rkhe->rqhe", d_scores, key_heads, preferred_element_type=jnp.float32)
        * score_scale
    )
    d_key = (
        jnp.einsum("rhqk,rqhe->rkhe", d_scores, queries, preferred_element_type=jnp.float32)
        * score_scale
    )
    d_qkv = jnp.concatenate(
        [
            d_query.reshape(tok_count, feat_width).astype(jnp.bfloat16),
            d_key.reshape(tok_count, feat_width).astype(jnp.bfloat16),
            d_value.reshape(tok_count, feat_width).astype(jnp.bfloat16),
        ],
        axis=1,
    )
    d_qkv_wide = d_qkv.astype(jnp.float32)
    d_b_query = jnp.sum(d_qkv_wide[:, :feat_width], axis=0)
    d_b_value = jnp.sum(d_qkv_wide[:, 2 * feat_width :], axis=0)
    d_w_qkv = jnp.einsum("nd,ne->de", normed1, d_qkv, preferred_element_type=jnp.float32)
    d_normed1 = jnp.einsum("ne,de->nd", d_qkv, qkv_w, preferred_element_type=jnp.float32)
    unused_first, norm1_pull = jax.vjp(scaled_norm, inputs, attn_gain.astype(jnp.float32))
    d_inputs_norm, d_attn_gain = norm1_pull(d_normed1)
    d_attn_shift = jnp.sum(d_normed1, axis=0)
    d_inputs = (d_hidden + d_inputs_norm).reshape(row_count, row_len, feat_width)
    d_time = jnp.sum(d_inputs, axis=1)
    attn_owned = (
        lax.psum_scatter(d_w_qkv, "dp", scatter_dimension=0, tiled=True),
        lax.psum_scatter(d_w_proj, "dp", scatter_dimension=0, tiled=True),
        lax.psum_scatter(d_attn_gain, "dp", scatter_dimension=0, tiled=True),
        lax.psum_scatter(d_attn_shift, "dp", scatter_dimension=0, tiled=True),
        lax.psum_scatter(d_b_query, "dp", scatter_dimension=0, tiled=True),
        lax.psum_scatter(d_b_value, "dp", scatter_dimension=0, tiled=True),
        lax.psum_scatter(d_b_proj, "dp", scatter_dimension=0, tiled=True),
    )
    own_qkv, own_proj, own_gain1, own_shift1, own_query, own_value, own_bproj = [
        member * grad_scale for member in attn_owned
    ]
    own_fc, own_out, own_gain2, own_shift2, own_bfc, own_bout = [
        member * grad_scale for member in mlp_owned
    ]
    return (
        layer_out,
        d_inputs,
        d_time,
        own_gain1,
        own_shift1,
        own_qkv,
        own_query,
        own_value,
        own_proj,
        own_bproj,
        own_gain2,
        own_shift2,
        own_fc,
        own_bfc,
        own_out,
        own_bout,
    )


def solution(mesh):
    in_specs = (
        P("dp", None, None),
        P("dp", None),
        P("dp", None),
        P("dp"),
        P("dp"),
        P("dp", None),
        P("dp"),
        P("dp"),
        P("dp", None),
        P("dp"),
        P("dp"),
        P("dp"),
        P("dp", None),
        P("dp"),
        P("dp", None),
        P("dp"),
        P("dp", None, None),
    )
    out_specs = (
        P("dp", None, None),
        P("dp", None, None),
        P("dp", None),
        P("dp"),
        P("dp"),
        P("dp", None),
        P("dp"),
        P("dp"),
        P("dp", None),
        P("dp"),
        P("dp"),
        P("dp"),
        P("dp", None),
        P("dp"),
        P("dp", None),
        P("dp"),
    )
    return jax.shard_map(
        on_device, mesh=mesh, in_specs=in_specs, out_specs=out_specs, check_vma=False
    )
```

profile of v0, /device:TPU:0, one launch (start us, length us, event | category | flops | bytes accessed | tf_op | source)
XLA Modules:
  0.0 826.8 jit_solution(16065974399056845671)
XLA Ops:
  17.6 42.8 %all-reduce.19 = (bf16[768]{0:T(1024)(128)(2,1)S(1)}, bf16[768]{0:T(1024)(128)(2,1)S(1)}, bf16[768]{0:T(1024)(128)(2,1)S(1)}, bf16[768]{0:T(1024)(128)(2,1)S(1)}...) all-reduce(bf16[768]{0:T(1024)(128)(2,1)S(1)} %dynamic-update-slice, ...), channel_id=1, replica_groups=mesh['dp'=32] {'dp'}, use_global_device_ids=true, to_apply=%add.4 | all-reduce | flops 9216 | bytes 36864
  66.9 7.0 all-gather.5.cloned.1.call-done
  73.9 7.5 add_convert_fusion.1
  81.4 6.9 copy.57
  100.3 29.6 %all-gather.7.cloned.1.call-done = bf16[768,768]{1,0:T(8,128)(2,1)} async-done(((bf16[24,768]{1,0:T(8,128)(2,1)}), bf16[768,768]{1,0:T(8,128)(2,1)}) %all-gather.7.cloned.1.call-update) | async-done | bytes 1179664 | tf_op jit(solution)/shard_map/all_gather | solution.py:60
  129.8 4.3 fusion.46
  134.7 60.7 %all-gather.9.cloned.1.call-done = bf16[768,3072]{1,0:T(8,128)(2,1)} async-done(((bf16[24,3072]{1,0:T(8,128)(2,1)}), bf16[768,3072]{1,0:T(8,128)(2,1)}) %all-gather.9.cloned.1.call-update) | async-done | bytes 4718608 | tf_op jit(solution)/shard_map/all_gather | solution.py:68
  195.4 36.0 %multiply_convert_fusion = (bf16[1024,3072]{1,0:T(8,128)(2,1)}, f32[1024,3072]{1,0:T(8,128)}, f32[1024,3072]{1,0:T(8,128)}) fusion(f32[3072]{0:T(1024)S(1)} %convert_element_type.136, bf16[768,3072]{1,0:T(8,128)(2,1)} %all-gather.9.cloned.1.call-done, f32[1024,768]{1,0:T(8,128)S(1)} %get-tuple-element.60, f32[768]{0:T(1024)S(1)} %convert_element_type.134, ...), kind=kOutput, calls=%fused_computation.4 | convolution fusion | flops 5043388416 | bytes 39348224 | tf_op jit(solution)/shard_map/dot_general | solution.py:112
  231.3 29.3 %all-gather.11.cloned.1.call-done = bf16[3072,768]{1,0:T(8,128)(2,1)} async-done(((bf16[96,768]{1,0:T(8,128)(2,1)}), bf16[3072,768]{1,0:T(8,128)(2,1)}) %all-gather.11.cloned.1.call-update) | async-done | bytes 4718608 | tf_op jit(solution)/shard_map/all_gather | solution.py:69
  260.6 18.1 %convert_reduce_fusion = (f32[3072]{0:T(1024)S(1)}, bf16[1024,3072]{1,0:T(8,128)(2,1)}) fusion(f32[1024,3072]{1,0:T(8,128)} %get-tuple-element.49, bf16[1024,768]{1,0:T(8,128)(2,1)} %bitcast.125, bf16[3072,768]{1,0:T(8,128)(2,1)} %all-gather.11.cloned.1.call-done, f32[1024,3072]{1,0:T(8,128)} %get-tuple-element.61, f32[3072]{0:T(1024)S(1)} %convert_element_type.136), kind=kOutput, calls=%fused_computation.2 | convolution fusion | flops 4885312512 | bytes 37773312 | tf_op jit(solution)/shard_map/nd,fd->nf/dot_general | solution.py:130
  278.7 9.2 %multiply_reduce_fusion.1 = (f32[768]{0:T(1024)S(1)}, f32[1024]{0:T(1024)S(1)}, f32[768]{0:T(1024)S(1)}, f32[1024,768]{1,0:T(8,128)S(1)}) fusion(f32[1024,768]{1,0:T(8,128)S(1)} %get-tuple-element.60, f32[1024]{0:T(1024)S(1)} %fusion.36, f32[1024]{0:T(1024)S(1)} %broadcast_multiply_fusion.4, f32[768]{0:T(1024)S(1)} %convert_element_type.133, ...), kind=kOutput, calls=%fused_computation.36 | convolution fusion | flops 4838126592 | bytes 17323008 | tf_op jit(solution)/shard_map/nf,df->nd/dot_general | solution.py:135
  302.4 6.3 fusion.24
  308.7 4.4 multiply_reduce_fusion
  315.8 6.7 multiply_convert_fusion.1
  331.7 6.0 fusion.47
  339.6 10.7 %fusion.38 = f32[768,3072]{1,0:T(8,128)} fusion(bf16[1024,3072]{1,0:T(8,128)(2,1)} %get-tuple-element.67, f32[1024,768]{1,0:T(8,128)S(1)} %copy-done.2, f32[768]{0:T(1024)S(1)} %convert_element_type.134, f32[768]{0:T(1024)S(1)} %convert_element_type.133, f32[1024]{0:T(1024)S(1)} %fusion.36, f32[1024]{0:T(1024)S(1)} %broadcast_multiply_fusion.4), kind=kOutput, calls=%fused_computation.106 | convolution fusion | flops 4835770368 | bytes 18888704 | tf_op jit(solution)/shard_map/nd,nf->df/dot_general | solution.py:133
  350.4 9.9 %fusion.48 = f32[3072,768]{1,0:T(8,128)} fusion(bf16[1024,3072]{1,0:T(8,128)(2,1)} %get-tuple-element.48, bf16[1024,768]{1,0:T(8,128)(2,1)} %bitcast.126), kind=kOutput, calls=%fused_computation.114 | convolution fusion | flops 4831838208 | bytes 17301504 | tf_op jit(solution)/shard_map/nf,nd->fd/dot_general | solution.py:128
  368.4 6.4 multiply_reduce_fusion.2
  374.8 40.7 %all-reduce.18 = (f32[768]{0:T(1024)S(1)}, f32[768]{0:T(1024)S(1)}, f32[768]{0:T(1024)S(1)}, f32[768]{0:T(1024)S(1)}, f32[768]{0:T(1024)S(1)}, /*index=5*/f32[76...) all-reduce(f32[768]{0:T(1024)S(1)} %get-tuple-element.20, ...), channel_id=2, replica_groups=mesh['dp'=32] {'dp'}, use_global_device_ids=true, to_apply=%region_13.14.clone | all-reduce | flops 9216 | bytes 73728
  418.5 3.7 fusion.41
  427.7 6.2 add_convert_fusion.2
  435.4 100.4 %reduce-scatter.5.cloned.1.call-done = f32[24,2304]{1,0:T(8,128)} async-done(((f32[768,2304]{1,0:T(8,128)}), f32[24,2304]{1,0:T(8,128)}) %reduce-scatter.5.cloned.1.call-update) | async-done | bytes 221200 | tf_op jit(solution)/shard_map/reduce_scatter | solution.py:194
  537.5 139.2 %reduce-scatter.9.cloned.1.call-done = f32[24,3072]{1,0:T(8,128)} async-done(((f32[768,3072]{1,0:T(8,128)}), f32[24,3072]{1,0:T(8,128)}) %reduce-scatter.9.cloned.1.call-update) | async-done | bytes 294928 | tf_op jit(solution)/shard_map/reduce_scatter | solution.py:141
  678.4 139.6 %reduce-scatter.11.cloned.1.call-done = f32[96,768]{1,0:T(8,128)} async-done(((f32[3072,768]{1,0:T(8,128)}), f32[96,768]{1,0:T(8,128)}) %reduce-scatter.11.cloned.1.call-update) | async-done | bytes 294928 | tf_op jit(solution)/shard_map/reduce_scatter | solution.py:142
  (179 shorter events, 80.3 us)
Async XLA Ops:
  7.2 56.8 %copy-start.16 = (bf16[8,128,768]{2,1,0:T(8,128)(2,1)S(1)}, bf16[8,128,768]{2,1,0:T(8,128)(2,1)}, u32[]{:S(2)}) copy-start(bf16[8,128,768]{2,1,0:T(8,128)(2,1)} %param.17) | copy-start | bytes 4718596
  7.2 66.7 %all-gather.5.cloned.1.call-start = ((), (), s32[]{:S(2)}) async-start(), calls=%async_computation.4 | async-start | bytes 3649536 | tf_op jit(solution)/shard_map/all_gather | solution.py:59
  7.9 121.9 %all-gather.7.cloned.1.call-start = ((), (), s32[]{:S(2)}) async-start(), calls=%async_computation.5 | async-start | bytes 1216512 | tf_op jit(solution)/shard_map/all_gather | solution.py:60
  8.7 186.7 %all-gather.9.cloned.1.call-start = ((), (), s32[]{:S(2)}) async-start(), calls=%async_computation.6 | async-start | bytes 4866048 | tf_op jit(solution)/shard_map/all_gather | solution.py:68
  9.4 251.2 %all-gather.11.cloned.1.call-start = ((), (), s32[]{:S(2)}) async-start(), calls=%async_computation.7 | async-start | bytes 4866048 | tf_op jit(solution)/shard_map/all_gather | solution.py:69
  10.0 423.9 %reduce-scatter.7.cloned.1.call-start = ((), (), s32[]{:S(2)}) async-start(), calls=%async_computation.9 | async-start | bytes 2433024 | tf_op jit(solution)/shard_map/reduce_scatter | solution.py:195
  60.4 4.3 copy-start.24
  64.6 16.7 %copy-start.28 = (f32[8,128]{1,0:T(8,128)}, f32[8,128]{1,0:T(8,128)S(1)}, u32[]{:S(2)}) copy-start(f32[8,128]{1,0:T(8,128)S(1)} %get-tuple-element.53) | copy-start | bytes 12292
  64.7 16.7 %copy-start.26 = (f32[1024]{0:T(1024)}, f32[1024]{0:T(1024)S(1)}, u32[]{:S(2)}) copy-start(f32[1024]{0:T(1024)S(1)} %bitcast_rsqrt_fusion) | copy-start | bytes 12292
  66.9 14.5 %copy-start.20 = (bf16[1024,768]{1,0:T(8,128)(2,1)}, bf16[1024,768]{1,0:T(8,128)(2,1)S(1)}, u32[]{:S(2)}) copy-start(bf16[1024,768]{1,0:T(8,128)(2,1)S(1)} %add_convert_fusion.4) | copy-start | bytes 4718596
  134.1 153.8 %copy-start.1 = (f32[1024,768]{1,0:T(8,128)}, f32[1024,768]{1,0:T(8,128)S(1)}, u32[]{:S(2)}) copy-start(f32[1024,768]{1,0:T(8,128)S(1)} %get-tuple-element.60) | copy-start | bytes 9437188
  297.8 11.0 %slice-start = ((s8[6291456]{0:T(1024)(128)(4,1)}), s8[2097152]{0:T(1024)(128)(4,1)S(1)}, s32[]{:S(2)}) async-start(s8[6291456]{0:T(1024)(128)(4,1)} %bitcast.121), calls=%async_computation.12 | async-start | bytes 4194304
  302.4 6.4 slice-start.1
  302.4 6.4 copy-start.18
  313.2 222.7 %reduce-scatter.5.cloned.1.call-start = ((), (), s32[]{:S(2)}) async-start(), calls=%async_computation.8 | async-start | bytes 7299072 | tf_op jit(solution)/shard_map/reduce_scatter | solution.py:194
  315.8 6.7 copy-start.14
  337.7 339.0 %reduce-scatter.9.cloned.1.call-start = ((), (), s32[]{:S(2)}) async-start(), calls=%async_computation.10 | async-start | bytes 9732096 | tf_op jit(solution)/shard_map/reduce_scatter | solution.py:141
  350.3 467.6 %reduce-scatter.11.cloned.1.call-start = ((), (), s32[]{:S(2)}) async-start(), calls=%async_computation.11 | async-start | bytes 9732096 | tf_op jit(solution)/shard_map/reduce_scatter | solution.py:142
  360.9 5.9 slice-start.2
  368.4 50.1 %copy-start.29 = (f32[8,128]{1,0:T(8,128)S(1)}, f32[8,128]{1,0:T(8,128)}, u32[]{:S(2)}) copy-start(f32[8,128]{1,0:T(8,128)} %copy-done.28) | copy-start | bytes 12292
  418.4 4.4 copy-start.8
  418.5 7.5 slice-start.4
  418.5 8.2 slice-start.6
  422.8 4.9 slice-start.7
  (25 other events, 59.7 us)
Sparse Core Ops, SparseCore 0:
  10.9 62.9 all-gather.4
  76.8 52.9 all-gather.6
  132.7 62.5 all-gather.8
  198.1 62.4 all-gather.10
  313.3 97.8 reduce-scatter.6
  417.7 118.1 reduce-scatter.4
  541.7 134.9 reduce-scatter.8
  683.6 134.3 reduce-scatter.10
where the time goes:
time: 833 us; the launch traced here: 827 us
  waiting for transfers between devices  508 us (61%)
  matrix products  136 us (16%)
  blocking collectives  83.5 us (10%)
  local copies, waits for them, and re-layouts  46.2 us (6%)
  other arithmetic  36.6 us (4%)
  between operations  15.1 us (2%)
    reduce_scatter x1, waiting for transfers between devices, on_device(): lax.psum_scatter(d_w_out, 'dp', scatter_dimension=0, tiled=True)  140 us
    reduce_scatter x1, waiting for transfers between devices, on_device(): lax.psum_scatter(d_w_fc, 'dp', scatter_dimension=0, tiled=True)  139 us
    reduce_scatter x1, waiting for transfers between devices, on_device(): lax.psum_scatter(d_w_qkv, 'dp', scatter_dimension=0, tiled=True)  100 us
    unnamed x2, blocking collectives  83.5 us
    all_gather x1, waiting for transfers between devices, on_device(): lax.all_gather(w_fc, 'dp', axis=0, tiled=True)  60.7 us
    dot_general x1, matrix products, on_device(): jnp.dot(normed2, fc_w, preferred_element_type=jnp.float32)  36 us
    unnamed x105, local copies, waits for them, and re-layouts  29.7 us
    all_gather x1, waiting for transfers between devices, on_device(): lax.all_gather(w_proj, 'dp', axis=0, tiled=True)  29.6 us
  transfers between devices with their start and end apart: 8, of which 7 were waited for; matrix products, arithmetic and copies ran while one was open for 18% of the time, Pallas kernels for 0%

commit v1 on v0

v1 whole, which is shorter than its diff:
```python
import functools
import math

import jax
import jax.numpy as jnp
from jax import lax
from jax.experimental import pallas as pl
from jax.experimental.pallas import tpu as pltpu
from jax.sharding import PartitionSpec as P

HD = 64
EPS = 1e-05
MASKED = -1e30
F32 = jnp.float32
BF16 = jnp.bfloat16
VMEM_LIMIT = 48 * 1024 * 1024


def dot(a, b, a_dim, b_dim):
    return lax.dot_general(a, b, (((a_dim,), (b_dim,)), ((), ())), preferred_element_type=F32)


def normalise(values):
    centered = values - jnp.mean(values, axis=-1, keepdims=True)
    spread = jnp.mean(centered * centered, axis=-1, keepdims=True)
    inv = lax.rsqrt(spread + EPS)
    return centered * inv, inv


def head_pair(block):
    lane = lax.broadcasted_iota(jnp.int32, block.shape, 1)
    zero = jnp.zeros_like(block)
    return jnp.concatenate([jnp.where(lane < HD, block, zero), jnp.where(lane >= HD, block, zero)], axis=0)


def own_lanes(stacked):
    half = stacked.shape[0] // 2
    lane = lax.broadcasted_iota(jnp.int32, (half, stacked.shape[1]), 1)
    return jnp.where(lane < HD, stacked[:half], stacked[half:])


def row_mask(seg_row):
    size = seg_row.shape[1]
    across = jnp.broadcast_to(seg_row.astype(F32), (size, size))
    return jnp.where(across == across.T, 0.0, MASKED)


def colsum(v):
    return jnp.sum(v, axis=0, keepdims=True)


Z, Y, X, CORES = 4, 2, 2, 2
PIECES = Z * Y * X * CORES


def merge_rows(blocks):
    count, rows, width = blocks.shape
    return blocks.astype(F32).reshape(count * rows, width).astype(BF16)


def slots(place, z, y, x):
    ys, xs = y ^ place[1], x ^ place[2]
    first = jnp.where(place[3] == 0, ys, xs)
    second = jnp.where(place[3] == 0, xs, ys)
    return first, second, (place[0] - z + Z) % Z


def put_blocks(place, z, y, x, even, odd, keep, send, tail=()):
    first, second, deep = slots(place, z, y, x)
    mine = place[3] == 0
    keep[(first, second, deep) + tail] = jnp.where(mine, even, odd)
    send[(second, first, deep) + tail] = jnp.where(mine, odd, even)


def attn_forward_body(
    place, tok, time, seg, mine0, mine1, other0, other1, n1, qkv, probs, att, hid, n2, weights, vec, *, rows
):
    size = tok.shape[0] // rows
    width = tok.shape[1]

    @pl.when(pl.program_id(0) == 0)
    def _():
        even = place[3] == 0
        for z in range(Z):
            for y in range(Y):
                for x in range(X):
                    first, second, deep = slots(place, z, y, x)
                    mine = jnp.where(first == 0, mine0[second, deep], mine1[second, deep])
                    other = jnp.where(second == 0, other0[first, deep], other1[first, deep])
                    both = [jnp.where(even, mine, other), jnp.where(even, other, mine)]
                    chip = (z * Y + y) * X + x
                    both = jnp.concatenate([b.astype(F32) for b in both], axis=0)
                    step = both.shape[0]
                    weights[chip * step : (chip + 1) * step, :] = both.astype(BF16)
        vec[...] = weights[:, 4 * width :].astype(F32).T[:16]

    x = tok[...].astype(F32)
    x = jnp.concatenate(
        [x[r * size : (r + 1) * size] + time[r].astype(F32) for r in range(rows)], axis=0
    )
    nhat, _ = normalise(x)
    normed = (nhat * vec[0:1, :] + vec[1:2, :]).astype(BF16)
    n1[...] = normed
    for part in range(3):
        cols = slice(part * width, (part + 1) * width)
        block = dot(normed, weights[:, cols], 1, 0)
        if part == 0:
            block = block + vec[2:3, :]
        if part == 2:
            block = block + vec[3:4, :]
        qkv[:, cols] = block.astype(BF16)
    pairs = width // (2 * HD)
    for r in range(rows):
        sl = slice(r * size, (r + 1) * size)
        mask = row_mask(seg[r])
        for p in range(pairs):
            c = 2 * HD * p
            q = qkv[sl, c : c + 2 * HD] * jnp.asarray(HD**-0.5, BF16)
            k = head_pair(qkv[sl, width + c : width + c + 2 * HD])
            v = head_pair(qkv[sl, 2 * width + c : 2 * width + c + 2 * HD])
            s = dot(q, k, 1, 1)
            halves = []
            for h in range(2):
                sh = s[:, h * size : (h + 1) * size] + mask
                e = jnp.exp(sh - jnp.max(sh, axis=-1, keepdims=True))
                halves.append((e / jnp.sum(e, axis=-1, keepdims=True)).astype(BF16))
            pr = jnp.concatenate(halves, axis=1)
            probs[r, p] = pr
            att[sl, c : c + 2 * HD] = dot(pr, v, 1, 0).astype(BF16)
    hidden = x + dot(att[...], weights[:, 3 * width : 4 * width], 1, 0) + vec[4:5, :]
    hid[...] = hidden
    nhat2, _ = normalise(hidden)
    n2[...] = (nhat2 * vec[5:6, :] + vec[6:7, :]).astype(BF16)


def attn_forward(place, tok, time, seg, gathered, rows=2):
    row_count = seg.shape[0]
    toks, width = tok.shape
    size = toks // row_count
    tm = rows * size
    pairs = width // (2 * HD)
    wide = gathered[0].shape[-1]
    full = lambda s: pl.BlockSpec(s, lambda i: (0,) * len(s))
    tile = lambda cols: pl.BlockSpec((tm, cols), lambda i: (i, 0))
    return pl.pallas_call(
        functools.partial(attn_forward_body, rows=rows),
        grid=(row_count // rows,),
        in_specs=[
            pl.BlockSpec(memory_space=pltpu.SMEM),
            tile(width),
            pl.BlockSpec((rows, 1, width), lambda i: (i, 0, 0)),
            pl.BlockSpec((rows, 1, size), lambda i: (i, 0, 0)),
        ]
        + [full(g.shape) for g in gathered],
        out_specs=[
            tile(width),
            tile(3 * width),
            pl.BlockSpec((rows, pairs, size, 2 * size), lambda i: (i, 0, 0, 0)),
            tile(width),
            tile(width),
            tile(width),
            full((width, wide)),
            full((16, width)),
        ],
        out_shape=[
            jax.ShapeDtypeStruct((toks, width), BF16),
            jax.ShapeDtypeStruct((toks, 3 * width), BF16),
            jax.ShapeDtypeStruct((row_count, pairs, size, 2 * size), BF16),
            jax.ShapeDtypeStruct((toks, width), BF16),
            jax.ShapeDtypeStruct((toks, width), F32),
            jax.ShapeDtypeStruct((toks, width), BF16),
            jax.ShapeDtypeStruct((width, wide), BF16),
            jax.ShapeDtypeStruct((16, width), F32),
        ],
        compiler_params=pltpu.CompilerParams(vmem_limit_bytes=VMEM_LIMIT),
        cost_estimate=pl.CostEstimate(flops=16 * 10**9, bytes_accessed=20 * 10**6, transcendentals=2 * 10**6),
        name="attn_forward",
    )(place, tok, time, seg, *gathered)


def ffn_body(
    place, n2, cot, fc, out, bfc, acc_out, acc_dn2, dbfc, keep, send, fc_s, out_s, act_s, dpre_s, *, tm, sub
):
    step = pl.program_id(0)
    width = n2.shape[1]

    @pl.when(step == 0)
    def _():
        acc_out[...] = jnp.zeros_like(acc_out)
        acc_dn2[...] = jnp.zeros_like(acc_dn2)

    fc_s[...] = merge_rows(fc[:, 0])
    out_s[...] = merge_rows(out[...].reshape((-1,) + out.shape[2:]))
    chunk = fc_s.shape[1]
    for part in range(chunk // sub):
        cols = slice(part * sub, (part + 1) * sub)
        bias = bfc[:, cols]
        db = jnp.zeros_like(bias)
        for m in range(n2.shape[0] // tm):
            sl = slice(m * tm, (m + 1) * tm)
            pre = dot(n2[sl, :], fc_s[:, cols], 1, 0) + bias
            d_act = dot(cot[sl, :], out_s[cols, :], 1, 1)
            cdf = 0.5 * lax.erf(pre * math.sqrt(0.5)) + 0.5
            density = jnp.exp(pre * pre * -0.5) * (1.0 / math.sqrt(2.0 * math.pi))
            act = (pre * cdf).astype(BF16)
            d_pre = (d_act * (cdf + pre * density)).astype(BF16)
            act_s[sl, cols] = act
            dpre_s[sl, cols] = d_pre
            db = db + jnp.sum(d_pre.astype(F32), axis=0, keepdims=True)
            acc_out[sl, :] += dot(act, out_s[cols, :], 1, 0)
            acc_dn2[sl, :] += dot(d_pre, fc_s[:, cols], 1, 1)
        dbfc[:, cols] = db
    grad = dot(act_s[...], cot[...], 0, 0)
    rows = out.shape[2]
    blocks = out.shape[1]
    for y in range(Y):
        for x in range(X):
            for b in range(blocks):
                at = ((y * X + x) * CORES * blocks + b) * rows
                even = grad[at : at + rows].astype(BF16)
                odd = grad[at + blocks * rows : at + (blocks + 1) * rows].astype(BF16)
                put_blocks(place, step, y, x, even, odd, keep, send, (blocks + b,))
    grad = dot(n2[...], dpre_s[...], 0, 0)
    for z in range(Z):
        for y in range(Y):
            for x in range(X):
                at = ((z * Y + y) * X + x) * CORES * rows
                even = grad[at : at + rows].astype(BF16)
                odd = grad[at + rows : at + 2 * rows].astype(BF16)
                put_blocks(place, z, y, x, even, odd, keep, send, (step,))


def ffn(place, n2, cot, gathered, bfc, tm=512, sub=256):
    toks, width = n2.shape
    pieces, count, rows, _ = gathered.shape
    blocks = count // 2
    hidden = width * blocks
    chunk = hidden // Z
    full = lambda s: pl.BlockSpec(s, lambda j: (0,) * len(s))
    parted = (Y, X, Z, count, rows, width)
    return pl.pallas_call(
        functools.partial(ffn_body, tm=tm, sub=sub),
        grid=(Z,),
        in_specs=[
            pl.BlockSpec(memory_space=pltpu.SMEM),
            full((toks, width)),
            full((toks, width)),
            pl.BlockSpec((pieces, 1, rows, width), lambda j: (0, j, 0, 0)),
            pl.BlockSpec((pieces // Z, blocks, rows, width), lambda j: (j, 1, 0, 0)),
            pl.BlockSpec((1, chunk), lambda j: (0, j)),
        ],
        out_specs=[
            full((toks, width)),
            full((toks, width)),
            pl.BlockSpec((1, chunk), lambda j: (0, j)),
            full(parted),
            full(parted),
        ],
        out_shape=[
            jax.ShapeDtypeStruct((toks, width), F32),
            jax.ShapeDtypeStruct((toks, width), F32),
            jax.ShapeDtypeStruct((1, hidden), F32),
            jax.ShapeDtypeStruct(parted, BF16),
            jax.ShapeDtypeStruct(parted, BF16),
        ],
        scratch_shapes=[
            pltpu.VMEM((width, chunk), BF16),
            pltpu.VMEM((chunk, width), BF16),
            pltpu.VMEM((toks, chunk), BF16),
            pltpu.VMEM((toks, chunk), BF16),
        ],
        compiler_params=pltpu.CompilerParams(vmem_limit_bytes=VMEM_LIMIT),
        cost_estimate=pl.CostEstimate(flops=30 * 10**9, bytes_accessed=30 * 10**6, transcendentals=6 * 10**6),
        name="ffn",
    )(place, n2, cot, gathered, gathered, bfc)


def attn_backward_body(
    hid, acc_out, acc_dn2, cot, qkv, probs, wproj, vec, layer_out, dhid, dbr, dqkv, sums, *, rows
):
    width = hid.shape[1]
    size = hid.shape[0] // rows

    @pl.when(pl.program_id(0) == 0)
    def _():
        sums[...] = jnp.zeros_like(sums)

    hidden = hid[...]
    layer_out[...] = (hidden + acc_out[...] + vec[7:8, :]).astype(BF16)
    nhat, inv = normalise(hidden)
    dn2 = acc_dn2[...]
    cotangent = cot[...].astype(F32)
    q = dn2 * vec[5:6, :]
    mean_q = jnp.mean(q, axis=-1, keepdims=True)
    mean_qn = jnp.mean(q * nhat, axis=-1, keepdims=True)
    d_hidden = cotangent + (q - mean_q - nhat * mean_qn) * inv
    dhid[...] = d_hidden
    branch = d_hidden.astype(BF16)
    dbr[...] = branch
    sums[0:1, :] += colsum(dn2 * nhat)
    sums[1:2, :] += colsum(dn2)
    sums[2:3, :] += colsum(branch.astype(F32))
    sums[3:4, :] += colsum(cotangent)
    d_mixed = dot(branch, wproj[...], 1, 1).astype(BF16)
    pairs = width // (2 * HD)
    for r in range(rows):
        sl = slice(r * size, (r + 1) * size)
        for p in range(pairs):
            c = 2 * HD * p
            qb = qkv[sl, c : c + 2 * HD] * jnp.asarray(HD**-0.5, BF16)
            k = head_pair(qkv[sl, width + c : width + c + 2 * HD])
            v = head_pair(qkv[sl, 2 * width + c : 2 * width + c + 2 * HD])
            dm = d_mixed[sl, c : c + 2 * HD]
            pr = probs[r, p]
            dp = dot(dm, v, 1, 1)
            pf = pr.astype(F32)
            prod = dp * pf
            ds = jnp.concatenate(
                [
                    prod[:, h * size : (h + 1) * size]
                    - pf[:, h * size : (h + 1) * size]
                    * jnp.sum(prod[:, h * size : (h + 1) * size], axis=-1, keepdims=True)
                    for h in range(2)
                ],
                axis=1,
            ).astype(BF16)
            dv = own_lanes(dot(pr, dm, 0, 0))
            dk = own_lanes(dot(ds, qb, 0, 0))
            dq = dot(ds, k, 1, 0) * HD**-0.5
            dqkv[sl, c : c + 2 * HD] = dq.astype(BF16)
            dqkv[sl, width + c : width + c + 2 * HD] = dk.astype(BF16)
            dqkv[sl, 2 * width + c : 2 * width + c + 2 * HD] = dv.astype(BF16)
    sums[4:5, :] += colsum(dqkv[:, :width].astype(F32))
    sums[5:6, :] += colsum(dqkv[:, 2 * width :].astype(F32))


def attn_backward(hid, acc_out, acc_dn2, cot, qkv, probs, wproj, vec, rows=2):
    row_count, pairs, size, _ = probs.shape
    toks, width = hid.shape
    tm = rows * size
    full = lambda s: pl.BlockSpec(s, lambda i: (0,) * len(s))
    tile = lambda cols: pl.BlockSpec((tm, cols), lambda i: (i, 0))
    return pl.pallas_call(
        functools.partial(attn_backward_body, rows=rows),
        grid=(row_count // rows,),
        in_specs=[
            tile(width),
            tile(width),
            tile(width),
            tile(width),
            tile(3 * width),
            pl.BlockSpec((rows, pairs, size, 2 * size), lambda i: (i, 0, 0, 0)),
            pl.BlockSpec((width, width), lambda i: (0, 3)),
            full(vec.shape),
        ],
        out_specs=[tile(width), tile(width), tile(width), tile(3 * width), full((8, width))],
        out_shape=[
            jax.ShapeDtypeStruct((toks, width), BF16),
            jax.ShapeDtypeStruct((toks, width), F32),
            jax.ShapeDtypeStruct((toks, width), BF16),
            jax.ShapeDtypeStruct((toks, 3 * width), BF16),
            jax.ShapeDtypeStruct((8, width), F32),
        ],
        compiler_params=pltpu.CompilerParams(vmem_limit_bytes=VMEM_LIMIT),
        cost_estimate=pl.CostEstimate(flops=20 * 10**9, bytes_accessed=30 * 10**6, transcendentals=0),
        name="attn_backward",
    )(hid, acc_out, acc_dn2, cot, qkv, probs, wproj, vec)


def weight_grad_body(place, n1, dqkv, att, dbr, keep, send):
    rows = keep.shape[3]

    def emit(grad):
        for z in range(Z):
            for y in range(Y):
                for x in range(X):
                    at = ((z * Y + y) * X + x) * CORES * rows
                    even = grad[at : at + rows].astype(BF16)
                    odd = grad[at + rows : at + 2 * rows].astype(BF16)
                    put_blocks(place, z, y, x, even, odd, keep, send)

    @pl.when(pl.program_id(0) == 0)
    def _():
        emit(dot(att[...], dbr[...], 0, 0))

    @pl.when(pl.program_id(0) > 0)
    def _():
        emit(dot(n1[...], dqkv[...], 0, 0))


def weight_grad(place, n1, dqkv, att, dbr):
    toks, width = n1.shape
    rows = width // PIECES
    full = pl.BlockSpec((toks, width), lambda j: (0, 0))
    parted = pl.BlockSpec((Y, X, Z, rows, width), lambda j: (0, 0, 0, 0, (j + 3) % 4))
    shape = jax.ShapeDtypeStruct((Y, X, Z, rows, 4 * width), BF16)
    return pl.pallas_call(
        weight_grad_body,
        grid=(4,),
        in_specs=[
            pl.BlockSpec(memory_space=pltpu.SMEM),
            full,
            pl.BlockSpec((toks, width), lambda j: (0, jnp.maximum(j - 1, 0))),
            full,
            full,
        ],
        out_specs=[parted, parted],
        out_shape=[shape, shape],
        compiler_params=pltpu.CompilerParams(vmem_limit_bytes=VMEM_LIMIT),
        cost_estimate=pl.CostEstimate(flops=5 * 10**9, bytes_accessed=15 * 10**6, transcendentals=0),
        name="weight_grad",
    )(place, n1, dqkv, att, dbr)


def input_grad_body(tok, time, dhid, dqkv, wqkv, vec, dtok, dtime, sums, *, rows):
    width = tok.shape[1]
    size = tok.shape[0] // rows

    @pl.when(pl.program_id(0) == 0)
    def _():
        sums[...] = jnp.zeros_like(sums)

    x = tok[...].astype(F32)
    x = jnp.concatenate(
        [x[r * size : (r + 1) * size] + time[r].astype(F32) for r in range(rows)], axis=0
    )
    nhat, inv = normalise(x)
    dn1 = dot(dqkv[...], wqkv[...], 1, 1)
    sums[0:1, :] += colsum(dn1 * nhat)
    sums[1:2, :] += colsum(dn1)
    q = dn1 * vec[0:1, :]
    mean_q = jnp.mean(q, axis=-1, keepdims=True)
    mean_qn = jnp.mean(q * nhat, axis=-1, keepdims=True)
    d_tok = dhid[...] + (q - mean_q - nhat * mean_qn) * inv
    dtok[...] = d_tok
    for r in range(rows):
        dtime[r] = colsum(d_tok[r * size : (r + 1) * size])


def input_grad(tok, time, dhid, dqkv, wqkv, vec, rows=2):
    row_count = time.shape[0]
    toks, width = tok.shape
    tm = toks // row_count * rows
    full = lambda s: pl.BlockSpec(s, lambda i: (0,) * len(s))
    tile = lambda cols: pl.BlockSpec((tm, cols), lambda i: (i, 0))
    per_row = pl.BlockSpec((rows, 1, width), lambda i: (i, 0, 0))
    return pl.pallas_call(
        functools.partial(input_grad_body, rows=rows),
        grid=(row_count // rows,),
        in_specs=[
            tile(width),
            per_row,
            tile(width),
            tile(3 * width),
            pl.BlockSpec((width, 3 * width), lambda i: (0, 0)),
            full(vec.shape),
        ],
        out_specs=[tile(width), per_row, full((8, width))],
        out_shape=[
            jax.ShapeDtypeStruct((toks, width), F32),
            jax.ShapeDtypeStruct((row_count, 1, width), F32),
            jax.ShapeDtypeStruct((8, width), F32),
        ],
        compiler_params=pltpu.CompilerParams(vmem_limit_bytes=VMEM_LIMIT),
        cost_estimate=pl.CostEstimate(flops=8 * 10**9, bytes_accessed=18 * 10**6, transcendentals=0),
        name="input_grad",
    )(tok, time, dhid, dqkv, wqkv, vec)


def flip(position):
    return lambda i: i ^ position


def exchange(array, partner):
    return lax.ppermute(array, "dp", [(i, partner(i)) for i in range(PIECES)])


def plane_partner(stage):
    def partner(i):
        along_y = (i % 2 == 0) == (stage == "first")
        return i ^ (4 if along_y else 2)

    return partner


def gather_cube(block):
    ring = [block] + [exchange(block, lambda i, k=k: (i + 8 * k) % PIECES) for k in range(1, Z)]
    line = jnp.stack(ring)
    half = jnp.stack([line, exchange(line, plane_partner("second"))])
    rest = exchange(half, plane_partner("first"))
    return half, rest, exchange(half, flip(1)), exchange(rest, flip(1))


def sum_cube(keep, send):
    came = exchange(send, flip(1))
    wide = lambda v: v.astype(F32)
    away = (wide(keep[1]) + wide(came[1])).astype(BF16)
    first = exchange(away, plane_partner("first"))
    away = (wide(keep[0, 1]) + wide(came[0, 1]) + wide(first[1])).astype(BF16)
    second = exchange(away, plane_partner("second"))
    here = lambda k: wide(keep[0, 0, k]) + wide(came[0, 0, k]) + wide(first[0, k]) + wide(second[k])
    total = here(0)
    for k in range(1, Z):
        total = total + wide(exchange(here(k).astype(BF16), lambda i, k=k: (i - 8 * k) % PIECES))
    return total


def sum_everywhere(values):
    for bit in (1, 2, 4, 8, 16):
        values = values + exchange(values, flip(bit))
    return values


def gather_any(block):
    every = lax.all_gather(block, "dp", axis=0, tiled=True)
    every = every.reshape((Z, Y, X, CORES, every.shape[0] // PIECES) + every.shape[1:])
    deep = [0, 3, 2, 1]
    even = jnp.transpose(every[:, :, :, 0], (1, 2, 0, 3, 4))[:, :, jnp.array(deep)]
    odd = jnp.transpose(every[:, :, :, 1], (2, 1, 0, 3, 4))[:, :, jnp.array(deep)]
    return even[0], even[1], odd[0], odd[1]


def natural_blocks(keep, send):
    deep = jnp.array([0, 3, 2, 1])
    rest = tuple(range(3, keep.ndim))
    even = jnp.transpose(keep[:, :, deep], (2, 0, 1) + rest)
    odd = jnp.transpose(send[:, :, deep], (2, 1, 0) + rest)
    both = jnp.stack([even, odd], axis=3)
    return both.reshape((PIECES,) + both.shape[4:])


def on_device(
    tokens,
    segment_ids,
    time_embed,
    norm1_gain,
    norm1_shift,
    w_qkv,
    b_query,
    b_value,
    w_proj,
    b_proj,
    norm2_gain,
    norm2_shift,
    w_fc,
    b_fc,
    w_out,
    b_out,
    cotangent,
):
    row_count, row_len, width = tokens.shape
    toks = row_count * row_len
    devices = lax.axis_size("dp")
    cube = devices == PIECES
    rank = lax.axis_index("dp")
    grad_scale = 1.0 / math.sqrt(toks * devices)
    own = w_proj.shape[0]
    ratio = b_fc.shape[0] // own
    if cube:
        place = jnp.stack([rank // 8, (rank // 4) % 2, (rank // 2) % 2, rank % 2]).astype(jnp.int32)
    else:
        place = jnp.zeros((4,), jnp.int32)

    small = jnp.stack(
        [norm1_gain, norm1_shift, b_query, b_value, b_proj, norm2_gain, norm2_shift, b_out], axis=1
    )
    small = jnp.concatenate([small, b_fc.reshape(ratio, own).T], axis=1)
    small = jnp.pad(small, ((0, 0), (0, 128 - small.shape[1])))
    attn_block = jnp.concatenate([w_qkv, w_proj, small], axis=1)
    ffn_block = jnp.concatenate(
        [w_fc.reshape(own, ratio, width).transpose(1, 0, 2), w_out.reshape(ratio, own, width)], axis=0
    )
    if cube:
        ffn_full = lax.all_gather(ffn_block, "dp", axis=0)
        attn_full = gather_cube(attn_block)
    else:
        fc_full = lax.all_gather(w_fc, "dp", axis=0, tiled=True)
        out_full = lax.all_gather(w_out, "dp", axis=0, tiled=True)
        cut = width // PIECES
        ffn_full = jnp.concatenate(
            [
                fc_full.reshape(PIECES, cut, ratio, width).transpose(0, 2, 1, 3),
                out_full.reshape(PIECES, ratio, cut, width),
            ],
            axis=1,
        )
        attn_full = gather_any(attn_block)

    flat = tokens.reshape(toks, width)
    times = time_embed.reshape(row_count, 1, width)
    segments = segment_ids.reshape(row_count, 1, row_len)
    cot = cotangent.reshape(toks, width)
    n1, qkv, probs, att, hid, n2, attn_w, vec = attn_forward(place, flat, times, segments, attn_full)
    bfc = vec[8 : 8 + ratio].reshape(ratio, devices, own).transpose(1, 0, 2).reshape(1, ratio * width)
    acc_out, acc_dn2, dbfc, ffn_keep, ffn_send = ffn(place, n2, cot, ffn_full, bfc)
    layer_out, dhid, dbr, dqkv, sums = attn_backward(hid, acc_out, acc_dn2, cot, qkv, probs, attn_w, vec)
    attn_keep, attn_send = weight_grad(place, n1, dqkv, att, dbr)
    d_tokens, d_time, sums1 = input_grad(flat, times, dhid, dqkv, attn_w, vec)

    vectors = jnp.concatenate([sums[:6], sums1[:2], dbfc.reshape(ratio, width)], axis=0)
    if cube:
        vectors = sum_everywhere(vectors)
        own_ffn = sum_cube(ffn_keep, ffn_send)
        own_attn = sum_cube(attn_keep, attn_send)
        own_out = own_ffn[ratio:].reshape(ratio * own, width)
        own_fc = own_ffn[:ratio].transpose(1, 0, 2).reshape(own, ratio * width)
    else:
        vectors = lax.psum(vectors, "dp")
        grads = natural_blocks(attn_keep, attn_send).astype(F32)
        own_attn = lax.psum_scatter(grads.reshape(width, -1), "dp", scatter_dimension=0, tiled=True)
        grads = natural_blocks(ffn_keep, ffn_send).astype(F32)
        fc_grad = grads[:, :ratio].transpose(0, 2, 1, 3).reshape(width, ratio * width)
        own_fc = lax.psum_scatter(fc_grad, "dp", scatter_dimension=0, tiled=True)
        out_grad = grads[:, ratio:].reshape(ratio * width, width)
        own_out = lax.psum_scatter(out_grad, "dp", scatter_dimension=0, tiled=True)
    vectors = vectors * grad_scale
    mine = lax.dynamic_slice(vectors[:8], (0, rank * own), (8, own))
    own_bfc = lax.dynamic_slice(vectors[8:].reshape(-1), (rank * own * ratio,), (own * ratio,))
    own_attn = own_attn * grad_scale
    return (
        layer_out.reshape(tokens.shape),
        d_tokens.reshape(tokens.shape),
        d_time.reshape(time_embed.shape),
        mine[6],
        mine[7],
        own_attn[:, : 3 * width],
        mine[4],
        mine[5],
        own_attn[:, 3 * width :],
        mine[2],
        mine[0],
        mine[1],
        own_fc * grad_scale,
        own_bfc,
        own_out * grad_scale,
        mine[3],
    )


def solution(mesh):
    in_specs = (
        P("dp", None, None),
        P("dp", None),
        P("dp", None),
        P("dp"),
        P("dp"),
        P("dp", None),
        P("dp"),
        P("dp"),
        P("dp", None),
        P("dp"),
        P("dp"),
        P("dp"),
        P("dp", None),
        P("dp"),
        P("dp", None),
        P("dp"),
        P("dp", None, None),
    )
    out_specs = (
        P("dp", None, None),
        P("dp", None, None),
        P("dp", None),
        P("dp"),
        P("dp"),
        P("dp", None),
        P("dp"),
        P("dp"),
        P("dp", None),
        P("dp"),
        P("dp"),
        P("dp"),
        P("dp", None),
        P("dp"),
        P("dp", None),
        P("dp"),
    )
    return jax.shard_map(
        on_device, mesh=mesh, in_specs=in_specs, out_specs=out_specs, check_vma=False
    )
```

time: 833 us -> 302 us (0.36)
  waiting for transfers between devices: 508 us -> 116 us
  matrix products: 136 us -> 0 us
  Pallas kernels: 0 us -> 103 us
  blocking collectives: 83.5 us -> 0 us
  starting transfers between devices: 0.7 us -> 29 us
  local copies, waits for them, and re-layouts: 46.2 us -> 21 us
  other arithmetic: 36.6 us -> 17.5 us
    reduce_scatter x4 -> x0, waiting for transfers between devices: 379 us -> none  [the longest x1 140 us: on_device(): lax.psum_scatter(d_w_out, 'dp', scatter_dimension=0, tiled=True)]
    dot_general x18 -> x0, matrix products: 136 us -> none  [the longest x1 36 us: on_device(): jnp.dot(normed2, fc_w, preferred_element_type=jnp.float32)]
    all_gather x4 -> x1, waiting for transfers between devices: 127 us -> 13.1 us  [on_device(): ffn_full = lax.all_gather(ffn_block, 'dp', axis=0)]
    pallas_call x0 -> x5, Pallas kernels: none -> 103 us  [the longest x1 42 us: ffn(): pl.pallas_call(functools.partial(ffn_body, tm=tm, sub=sub), grid=(Z,), in...]
    ppermute x0 -> x24, waiting for transfers between devices: none -> 103 us  [exchange(): return lax.ppermute(array, 'dp', [(i, partner(i)) for i in range(PIECES)])]
    unnamed x2 -> x0, blocking collectives: 83.5 us -> none
    ppermute x0 -> x24, starting transfers between devices: none -> 29 us  [exchange(): return lax.ppermute(array, 'dp', [(i, partner(i)) for i in range(PIECES)])]
    unnamed x105 -> x27, local copies, waits for them, and re-layouts: 29.7 us -> 4.68 us
  transfers between devices with their start and end apart: 8 -> 25, of which waited for: 7 -> 15; matrix products, arithmetic and copies ran while one was open for 18% -> 10% of each run, Pallas kernels for 0% -> 20%
where the time goes in v1:
time: 302 us
  waiting for transfers between devices  116 us (38%)
  Pallas kernels  103 us (34%)
  starting transfers between devices  29 us (10%)
  local copies, waits for them, and re-layouts  21 us (7%)
  other arithmetic  17.5 us (6%)
  between operations  14.3 us (5%)
    ppermute x24, waiting for transfers between devices, exchange(): return lax.ppermute(array, 'dp', [(i, partner(i)) for i in range(PIECES)])  103 us
    pallas_call x1, Pallas kernels, ffn(): pl.pallas_call(functools.partial(ffn_body, tm=tm, sub=sub), grid=(Z,), in...  42 us
    ppermute x24, starting transfers between devices, exchange(): return lax.ppermute(array, 'dp', [(i, partner(i)) for i in range(PIECES)])  29 us
    pallas_call x1, Pallas kernels, attn_backward(): pl.pallas_call(functools.partial(attn_backward_body, rows=rows), grid=(ro...  23.3 us
    pallas_call x1, Pallas kernels, attn_forward(): pl.pallas_call(functools.partial(attn_forward_body, rows=rows), grid=(row...  19.9 us
    all_gather x1, waiting for transfers between devices, on_device(): ffn_full = lax.all_gather(ffn_block, 'dp', axis=0)  13.1 us
    pallas_call x1, Pallas kernels, weight_grad(): pl.pallas_call(weight_grad_body, grid=(4,), in_specs=[pl.BlockSpec(memory...  9.15 us
    pallas_call x1, Pallas kernels, input_grad(): pl.pallas_call(functools.partial(input_grad_body, rows=rows), grid=(row_c...  9.07 us
  transfers between devices with their start and end apart: 25, of which 15 were waited for; matrix products, arithmetic and copies ran while one was open for 10% of the time, Pallas kernels for 20%

profile of v1, /device:TPU:0, one launch (start us, length us, event | category | flops | bytes accessed | tf_op | source)
XLA Modules:
  0.0 301.6 jit_solution(17703448553439787693)
XLA Ops:
  18.1 3.1 %collective-permute-start = (bf16[24,3200]{1,0:T(8,128)(2,1)S(1)}, bf16[24,3200]{1,0:T(8,128)(2,1)S(1)}, u32[]{:S(2)}, u32[]{:S(2)}) collective-permute-start(bf16[24,3200]{1,0:T(8,128)(2,1)S(1)} %get-tuple-element.73), channel_id=1, source_target_pairs={{0,8},{1,9},{2,10},{3,11},{4,12},{5,13},{6,14},{7,15},{8,16},{9,17... | collective-permute-start | bytes 460808 | tf_op jit(solution)/shard_map/ppermute | solution.py:475
  21.1 2.6 collective-permute-start.1
  25.1 3.3 %collective-permute-done = bf16[24,3200]{1,0:T(8,128)(2,1)S(1)} collective-permute-done((bf16[24,3200]{1,0:T(8,128)(2,1)S(1)}, bf16[24,3200]{1,0:T(8,128)(2,1)S(1)}, u32[]{:S(2)}, u32[]{:S(2)}) %collective-permute-start) | collective-permute-done | bytes 153632 | tf_op jit(solution)/shard_map/ppermute | solution.py:475
  28.3 10.3 %collective-permute-done.1 = bf16[24,3200]{1,0:T(8,128)(2,1)S(1)} collective-permute-done((bf16[24,3200]{1,0:T(8,128)(2,1)S(1)}, bf16[24,3200]{1,0:T(8,128)(2,1)S(1)}, u32[]{:S(2)}, u32[]{:S(2)}) %collective-permute-start.1) | collective-permute-done | bytes 153632 | tf_op jit(solution)/shard_map/ppermute | solution.py:475
  41.1 10.2 %collective-permute-done.3 = bf16[4,24,3200]{2,1,0:T(8,128)(2,1)S(1)} collective-permute-done((bf16[4,24,3200]{2,1,0:T(8,128)(2,1)S(1)}, bf16[4,24,3200]{2,1,0:T(8,128)(2,1)S(1)}, u32[]{:S(2)}, u32[]{:S(2)}) %collective-permute-start.3) | collective-permute-done | bytes 614432 | tf_op jit(solution)/shard_map/ppermute | solution.py:475
  51.8 16.5 %collective-permute-done.4.mine1 = bf16[2,4,24,3200]{3,2,1,0:T(8,128)(2,1)S(1)} collective-permute-done((bf16[2,4,24,3200]{3,2,1,0:T(8,128)(2,1)S(1)}, bf16[2,4,24,3200]{3,2,1,0:T(8,128)(2,1)S(1)}, u32[]{:S(2)}, u32[]{:S(2)}) %collective-permute-start.4) | collective-permute-done | bytes 1228832 | tf_op jit(solution)/shard_map/ppermute | solution.py:475
  68.3 2.9 collective-permute-start.6
  75.1 19.9 %attn_forward.1 = (bf16[1024,768]{1,0:T(8,128)(2,1)}, bf16[1024,2304]{1,0:T(8,128)(2,1)}, bf16[8,6,128,256]{3,2,1,0:T(8,128)(2,1)}, bf16[1024,768]{1,0:T(8,128)(...) custom-call(s32[4]{0:T(128)S(1)} %pad_add_fusion.place, ...), custom_call_target="tpu_custom_call" | custom-call | flops 16000000000 | bytes 20000000 | tf_op jit(solution)/shard_map/attn_forward/pallas_call | solution.py:145
  95.3 13.1 %all-gather.3.cloned.1.call-done = bf16[256,24,768]{2,1,0:T(8,128)(2,1)} async-done(((bf16[8,24,768]{2,1,0:T(8,128)(2,1)}), bf16[256,24,768]{2,1,0:T(8,128)(2,1)}) %all-gather.3.cloned.1.call-update) | async-done | bytes 9437200 | tf_op jit(solution)/shard_map/all_gather | solution.py:574
  109.8 42.0 %ffn.1 = (f32[1024,768]{1,0:T(8,128)}, f32[1024,768]{1,0:T(8,128)}, f32[1,3072]{1,0:T(1,128)S(1)}, bf16[2,2,4,8,24,768]{5,4,3,2,1,0:T(8,128)(2,1)}, bf16[2,2,4,8,24,768]{5,4,3,2,1,0:T(8,128)(2,1)}) custom-call(s32[4]{0:T(128)S(1)} %pad_add_fusion.place, bf16[1024,768]{1,0:T(8,128)(2,1)S(1)} %copy-done.8, bf16[1024,768]{1,0:T(8,128)(2,1)S(1)} %bitcast.172, ...), custom_call_target="tpu_custom_call" | custom-call | flops 30000001024 | bytes 30000000 | tf_op jit(solution)/shard_map/ffn/pallas_call | solution.py:241
  152.0 23.3 %attn_backward.1 = (bf16[1024,768]{1,0:T(8,128)(2,1)}, f32[1024,768]{1,0:T(8,128)}, bf16[1024,768]{1,0:T(8,128)(2,1)S(1)}, bf16[1024,2304]{1,0:T(8,128)(2,1)}, f32[8,768]{1,0:T(8,128)S(1)}) custom-call(f32[1024,768]{1,0:T(8,128)} %get-tuple-element.39.hid, f32[1024,768]{1,0:T(8,128)} %get-tuple-element.42.acc_out, f32[1024,768]{1,0:T(8,128)} %get-tuple-element.43.acc_dn2, ...), custom_call_target="tpu_custom_call" | custom-call | flops 20000000000 | bytes 30000000 | tf_op jit(solution)/shard_map/attn_backward/pallas_call | solution.py:343
  175.4 9.2 %weight_grad.1 = (bf16[2,2,4,24,3072]{4,3,2,1,0:T(8,128)(2,1)}, bf16[2,2,4,24,3072]{4,3,2,1,0:T(8,128)(2,1)}) custom-call(s32[4]{0:T(128)S(1)} %pad_add_fusion.place, bf16[1024,768]{1,0:T(8,128)(2,1)S(1)} %copy-done.5, bf16[1024,2304]{1,0:T(8,128)(2,1)} %get-tuple-element.49.dqkv, bf16[1024,768]{1,0:T(8,128)(2,1)S(1)} %copy-done.6, ...), custom_call_target="tpu_custom_call" | custom-call | flops 5000000000 | bytes 15000000 | tf_op jit(solution)/shard_map/weight_grad/pallas_call | solution.py:397
  184.8 3.8 %fusion = bf16[2,4,8,24,768]{4,3,2,1,0:T(8,128)(2,1)} fusion(bf16[2,2,4,8,24,768]{5,4,3,2,1,0:T(8,128)(2,1)} %collective-permute-done.18, bf16[2,2,4,8,24,768]{5,4,3,2,1,0:T(8,128)(2,1)S(1)} %copy-done.9), kind=kLoop, calls=%fused_computation.1 | loop fusion | flops 4718592 | bytes 7077888 | tf_op jit(solution)/shard_map/convert_element_type | solution.py:497
  191.5 9.1 %input_grad.1 = (f32[1024,768]{1,0:T(8,128)}, f32[8,1,768]{2,1,0:T(1,128)S(1)}, f32[8,768]{1,0:T(8,128)S(1)}) custom-call(bf16[1024,768]{1,0:T(8,128)(2,1)S(1)} %bitcast.175, bf16[8,1,768]{2,1,0:T(2,128)(2,1)S(1)} %copy.94.time, f32[1024,768]{1,0:T(8,128)S(1)} %copy-done.7, bf16[1024,2304]{1,0:T(8,128)(2,1)} %get-tuple-element.49.dqkv, ...), custom_call_target="tpu_custom_call" | custom-call | flops 8000000000 | bytes 18000000 | tf_op jit(solution)/shard_map/input_grad/pallas_call | solution.py:447
  204.3 3.6 %collective-permute-done.8 = f32[12,768]{1,0:T(8,128)S(1)} collective-permute-done((f32[12,768]{1,0:T(8,128)S(1)}, f32[12,768]{1,0:T(8,128)S(1)}, u32[]{:S(2)}, u32[]{:S(2)}) %collective-permute-start.8) | collective-permute-done | bytes 36896 | tf_op jit(solution)/shard_map/ppermute | solution.py:475
  209.0 21.8 %collective-permute-done.9 = f32[12,768]{1,0:T(8,128)S(1)} collective-permute-done((f32[12,768]{1,0:T(8,128)S(1)}, f32[12,768]{1,0:T(8,128)S(1)}, u32[]{:S(2)}, u32[]{:S(2)}) %collective-permute-start.9) | collective-permute-done | bytes 36896 | tf_op jit(solution)/shard_map/ppermute | solution.py:475
  233.0 2.0 collective-permute-done.10
  240.1 2.4 fusion.1
  250.2 2.0 collective-permute-start.15
  253.3 7.9 %collective-permute-done.20 = bf16[4,8,24,768]{3,2,1,0:T(8,128)(2,1)S(1)} collective-permute-done((bf16[4,8,24,768]{3,2,1,0:T(8,128)(2,1)S(1)}, bf16[4,8,24,768]{3,2,1,0:T(8,128)(2,1)S(1)}, u32[]{:S(2)}, u32[]{:S(2)}) %collective-permute-start.20) | collective-permute-done | bytes 1179680 | tf_op jit(solution)/shard_map/ppermute | solution.py:475
  261.2 2.1 fusion.6
  263.3 2.0 collective-permute-start.21
  269.0 4.2 %collective-permute-done.21 = bf16[8,24,768]{2,1,0:T(8,128)(2,1)S(1)} collective-permute-done((bf16[8,24,768]{2,1,0:T(8,128)(2,1)S(1)}, bf16[8,24,768]{2,1,0:T(8,128)(2,1)S(1)}, u32[]{:S(2)}, u32[]{:S(2)}) %collective-permute-start.21) | collective-permute-done | bytes 294944 | tf_op jit(solution)/shard_map/ppermute | solution.py:475
  273.2 18.7 %collective-permute-done.22 = bf16[8,24,768]{2,1,0:T(8,128)(2,1)S(1)} collective-permute-done((bf16[8,24,768]{2,1,0:T(8,128)(2,1)S(1)}, bf16[8,24,768]{2,1,0:T(8,128)(2,1)S(1)}, u32[]{:S(2)}, u32[]{:S(2)}) %collective-permute-start.22) | collective-permute-done | bytes 294944 | tf_op jit(solution)/shard_map/ppermute | solution.py:475
  (111 shorter events, 51.6 us)
Async XLA Ops:
  7.2 101.2 %all-gather.3.cloned.1.call-start = ((), (), s32[]{:S(2)}) async-start(), calls=%async_computation | async-start | bytes 9732096 | tf_op jit(solution)/shard_map/all_gather | solution.py:574
  18.1 10.3 %collective-permute-start = (bf16[24,3200]{1,0:T(8,128)(2,1)S(1)}, bf16[24,3200]{1,0:T(8,128)(2,1)S(1)}, u32[]{:S(2)}, u32[]{:S(2)}) collective-permute-start(bf16[24,3200]{1,0:T(8,128)(2,1)S(1)} %get-tuple-element.73), channel_id=1, source_target_pairs={{0,8},{1,9},{2,10},{3,11},{4,12},{5,13},{6,14},{7,15},{8,16},{9,17... | collective-permute-start | bytes 460808 | tf_op jit(solution)/shard_map/ppermute | solution.py:475
  21.1 17.5 %collective-permute-start.1 = (bf16[24,3200]{1,0:T(8,128)(2,1)S(1)}, bf16[24,3200]{1,0:T(8,128)(2,1)S(1)}, u32[]{:S(2)}, u32[]{:S(2)}) collective-permute-start(bf16[24,3200]{1,0:T(8,128)(2,1)S(1)} %get-tuple-element.73), channel_id=1, source_target_pairs={{0,16},{1,17},{2,18},{3,19},{4,20},{5,21},{6,22},{7,23},{8,24},{9,... | collective-permute-start | bytes 460808 | tf_op jit(solution)/shard_map/ppermute | solution.py:475
  23.7 15.5 %collective-permute-start.2 = (bf16[24,3200]{1,0:T(8,128)(2,1)S(1)}, bf16[24,3200]{1,0:T(8,128)(2,1)S(1)}, u32[]{:S(2)}, u32[]{:S(2)}) collective-permute-start(bf16[24,3200]{1,0:T(8,128)(2,1)S(1)} %get-tuple-element.73), channel_id=1, source_target_pairs={{0,24},{1,25},{2,26},{3,27},{4,28},{5,29},{6,30},{7,31},{8,0},{9,1... | collective-permute-start | bytes 460808 | tf_op jit(solution)/shard_map/ppermute | solution.py:475
  39.3 12.0 %collective-permute-start.3 = (bf16[4,24,3200]{2,1,0:T(8,128)(2,1)S(1)}, bf16[4,24,3200]{2,1,0:T(8,128)(2,1)S(1)}, u32[]{:S(2)}, u32[]{:S(2)}) collective-permute-start(bf16[4,24,3200]{2,1,0:T(8,128)(2,1)S(1)} %get-tuple-element.69), channel_id=1, source_target_pairs={{0,2},{1,5},{2,0},{3,7},{4,6},{5,1},{6,4},{7,3},{8,10},{9,13},{10,... | collective-permute-start | bytes 1843208 | tf_op jit(solution)/shard_map/ppermute | solution.py:475
  51.5 16.8 %collective-permute-start.4 = (bf16[2,4,24,3200]{3,2,1,0:T(8,128)(2,1)S(1)}, bf16[2,4,24,3200]{3,2,1,0:T(8,128)(2,1)S(1)}, u32[]{:S(2)}, u32[]{:S(2)}) collective-permute-start(bf16[2,4,24,3200]{3,2,1,0:T(8,128)(2,1)S(1)} %pad_maximum_fusion.mine0), channel_id=1, source_target_pairs={{0,4},{1,3},{2,6},{3,1},{4,0},{5,7},{6,2},{7,5},{8,12},{9,11},{10,... | collective-permute-start | bytes 3686408 | tf_op jit(solution)/shard_map/ppermute | solution.py:475
  51.7 20.6 %collective-permute-start.5 = (bf16[2,4,24,3200]{3,2,1,0:T(8,128)(2,1)S(1)}, bf16[2,4,24,3200]{3,2,1,0:T(8,128)(2,1)}, u32[]{:S(2)}, u32[]{:S(2)}) collective-permute-start(bf16[2,4,24,3200]{3,2,1,0:T(8,128)(2,1)S(1)} %pad_maximum_fusion.mine0), channel_id=1, source_target_pairs={{0,1},{1,0},{2,3},{3,2},{4,5},{5,4},{6,7},{7,6},{8,9},{9,8},{10,11... | collective-permute-start | bytes 3686408 | tf_op jit(solution)/shard_map/ppermute | solution.py:475
  68.3 5.6 %collective-permute-start.6 = (bf16[2,4,24,3200]{3,2,1,0:T(8,128)(2,1)S(1)}, bf16[2,4,24,3200]{3,2,1,0:T(8,128)(2,1)}, u32[]{:S(2)}, u32[]{:S(2)}) collective-permute-start(bf16[2,4,24,3200]{3,2,1,0:T(8,128)(2,1)S(1)} %collective-permute-done.4.mine1), channel_id=1, source_target_pairs={{0,1},{1,0},{2,3},{3,2},{4,5},{5,4},{6,7},{7,6},{8,9},{9,8},{10,11... | collective-permute-start | bytes 3686408 | tf_op jit(solution)/shard_map/ppermute | solution.py:475
  151.8 33.0 %collective-permute-start.18 = (bf16[2,2,4,8,24,768]{5,4,3,2,1,0:T(8,128)(2,1)}, bf16[2,2,4,8,24,768]{5,4,3,2,1,0:T(8,128)(2,1)}, u32[]{:S(2)}, u32[]{:S(2)}) collective-permute-start(bf16[2,2,4,8,24,768]{5,4,3,2,1,0:T(8,128)(2,1)} %get-tuple-element.61), channel_id=1, source_target_pairs={{0,1},{1,0},{2,3},{3,2},{4,5},{5,4},{6,7},{7,6},{8,9},{9,8},{10,11... | collective-permute-start | bytes 14155784 | tf_op jit(solution)/shard_map/ppermute | solution.py:475
  184.5 5.6 %collective-permute-start.12 = (bf16[2,2,4,24,3072]{4,3,2,1,0:T(8,128)(2,1)}, bf16[2,2,4,24,3072]{4,3,2,1,0:T(8,128)(2,1)S(1)}, u32[]{:S(2)}, u32[]{:S(2)}) collective-permute-start(bf16[2,2,4,24,3072]{4,3,2,1,0:T(8,128)(2,1)} %get-tuple-element.59), channel_id=1, source_target_pairs={{0,1},{1,0},{2,3},{3,2},{4,5},{5,4},{6,7},{7,6},{8,9},{9,8},{10,11... | collective-permute-start | bytes 7077896 | tf_op jit(solution)/shard_map/ppermute | solution.py:475
  188.6 51.5 %collective-permute-start.19 = (bf16[2,4,8,24,768]{4,3,2,1,0:T(8,128)(2,1)}, bf16[2,4,8,24,768]{4,3,2,1,0:T(8,128)(2,1)}, u32[]{:S(2)}, u32[]{:S(2)}) collective-permute-start(bf16[2,4,8,24,768]{4,3,2,1,0:T(8,128)(2,1)} %fusion), channel_id=1, source_target_pairs={{0,4},{1,3},{2,6},{3,1},{4,0},{5,7},{6,2},{7,5},{8,12},{9,11},{10,... | collective-permute-start | bytes 7077896 | tf_op jit(solution)/shard_map/ppermute | solution.py:475
  190.5 46.5 %collective-permute-start.13 = (bf16[2,4,24,3072]{3,2,1,0:T(8,128)(2,1)S(1)}, bf16[2,4,24,3072]{3,2,1,0:T(8,128)(2,1)}, u32[]{:S(2)}, u32[]{:S(2)}) collective-permute-start(bf16[2,4,24,3072]{3,2,1,0:T(8,128)(2,1)S(1)} %fusion.2), channel_id=1, source_target_pairs={{0,4},{1,3},{2,6},{3,1},{4,0},{5,7},{6,2},{7,5},{8,12},{9,11},{10,... | collective-permute-start | bytes 3538952 | tf_op jit(solution)/shard_map/ppermute | solution.py:475
  203.2 4.7 %collective-permute-start.8 = (f32[12,768]{1,0:T(8,128)S(1)}, f32[12,768]{1,0:T(8,128)S(1)}, u32[]{:S(2)}, u32[]{:S(2)}) collective-permute-start(f32[12,768]{1,0:T(8,128)S(1)} %fusion.20), channel_id=1, source_target_pairs={{0,2},{1,3},{2,0},{3,1},{4,6},{5,7},{6,4},{7,5},{8,10},{9,11},{10,... | collective-permute-start | bytes 110600 | tf_op jit(solution)/shard_map/ppermute | solution.py:475
  207.9 22.9 %collective-permute-start.9 = (f32[12,768]{1,0:T(8,128)S(1)}, f32[12,768]{1,0:T(8,128)S(1)}, u32[]{:S(2)}, u32[]{:S(2)}) collective-permute-start(f32[12,768]{1,0:T(8,128)S(1)} %add.180), channel_id=1, source_target_pairs={{0,4},{1,5},{2,6},{3,7},{4,0},{5,1},{6,2},{7,3},{8,12},{9,13},{10,... | collective-permute-start | bytes 110600 | tf_op jit(solution)/shard_map/ppermute | solution.py:475
  230.8 4.2 %collective-permute-start.10 = (f32[12,768]{1,0:T(8,128)S(1)}, f32[12,768]{1,0:T(8,128)S(1)}, u32[]{:S(2)}, u32[]{:S(2)}) collective-permute-start(f32[12,768]{1,0:T(8,128)S(1)} %add.181), channel_id=1, source_target_pairs={{0,8},{1,9},{2,10},{3,11},{4,12},{5,13},{6,14},{7,15},{8,0},{9,1},... | collective-permute-start | bytes 110600 | tf_op jit(solution)/shard_map/ppermute | solution.py:475
  235.0 8.2 %collective-permute-start.11 = (f32[12,768]{1,0:T(8,128)S(1)}, f32[12,768]{1,0:T(8,128)S(1)}, u32[]{:S(2)}, u32[]{:S(2)}) collective-permute-start(f32[12,768]{1,0:T(8,128)S(1)} %add.182), channel_id=1, source_target_pairs={{0,16},{1,17},{2,18},{3,19},{4,20},{5,21},{6,22},{7,23},{8,24},{9,... | collective-permute-start | bytes 110600 | tf_op jit(solution)/shard_map/ppermute | solution.py:475
  238.6 9.9 %collective-permute-start.14 = (bf16[4,24,3072]{2,1,0:T(8,128)(2,1)S(1)}, bf16[4,24,3072]{2,1,0:T(8,128)(2,1)S(1)}, u32[]{:S(2)}, u32[]{:S(2)}) collective-permute-start(bf16[4,24,3072]{2,1,0:T(8,128)(2,1)S(1)} %fusion.3), channel_id=1, source_target_pairs={{0,2},{1,5},{2,0},{3,7},{4,6},{5,1},{6,4},{7,3},{8,10},{9,13},{10,... | collective-permute-start | bytes 1769480 | tf_op jit(solution)/shard_map/ppermute | solution.py:475
  242.5 18.7 %collective-permute-start.20 = (bf16[4,8,24,768]{3,2,1,0:T(8,128)(2,1)S(1)}, bf16[4,8,24,768]{3,2,1,0:T(8,128)(2,1)S(1)}, u32[]{:S(2)}, u32[]{:S(2)}) collective-permute-start(bf16[4,8,24,768]{3,2,1,0:T(8,128)(2,1)S(1)} %fusion.1), channel_id=1, source_target_pairs={{0,2},{1,5},{2,0},{3,7},{4,6},{5,1},{6,4},{7,3},{8,10},{9,13},{10,... | collective-permute-start | bytes 3538952 | tf_op jit(solution)/shard_map/ppermute | solution.py:475
  250.2 15.2 %collective-permute-start.15 = (bf16[24,3072]{1,0:T(8,128)(2,1)S(1)}, bf16[24,3072]{1,0:T(8,128)(2,1)S(1)}, u32[]{:S(2)}, u32[]{:S(2)}) collective-permute-start(bf16[24,3072]{1,0:T(8,128)(2,1)S(1)} %get-tuple-element.65), channel_id=1, source_target_pairs={{0,24},{1,25},{2,26},{3,27},{4,28},{5,29},{6,30},{7,31},{8,0},{9,1... | collective-permute-start | bytes 442376 | tf_op jit(solution)/shard_map/ppermute | solution.py:475
  252.1 14.3 %collective-permute-start.16 = (bf16[24,3072]{1,0:T(8,128)(2,1)S(1)}, bf16[24,3072]{1,0:T(8,128)(2,1)S(1)}, u32[]{:S(2)}, u32[]{:S(2)}) collective-permute-start(bf16[24,3072]{1,0:T(8,128)(2,1)S(1)} %get-tuple-element.67), channel_id=1, source_target_pairs={{0,16},{1,17},{2,18},{3,19},{4,20},{5,21},{6,22},{7,23},{8,24},{9,... | collective-permute-start | bytes 442376 | tf_op jit(solution)/shard_map/ppermute | solution.py:475
  252.2 14.2 %collective-permute-start.17 = (bf16[24,3072]{1,0:T(8,128)(2,1)S(1)}, bf16[24,3072]{1,0:T(8,128)(2,1)S(1)}, u32[]{:S(2)}, u32[]{:S(2)}) collective-permute-start(bf16[24,3072]{1,0:T(8,128)(2,1)S(1)} %get-tuple-element.66), channel_id=1, source_target_pairs={{0,8},{1,9},{2,10},{3,11},{4,12},{5,13},{6,14},{7,15},{8,16},{9,17... | collective-permute-start | bytes 442376 | tf_op jit(solution)/shard_map/ppermute | solution.py:475
  263.3 9.9 %collective-permute-start.21 = (bf16[8,24,768]{2,1,0:T(8,128)(2,1)S(1)}, bf16[8,24,768]{2,1,0:T(8,128)(2,1)S(1)}, u32[]{:S(2)}, u32[]{:S(2)}) collective-permute-start(bf16[8,24,768]{2,1,0:T(8,128)(2,1)S(1)} %get-tuple-element.62), channel_id=1, source_target_pairs={{0,24},{1,25},{2,26},{3,27},{4,28},{5,29},{6,30},{7,31},{8,0},{9,1... | collective-permute-start | bytes 884744 | tf_op jit(solution)/shard_map/ppermute | solution.py:475
  265.3 26.6 %collective-permute-start.22 = (bf16[8,24,768]{2,1,0:T(8,128)(2,1)S(1)}, bf16[8,24,768]{2,1,0:T(8,128)(2,1)S(1)}, u32[]{:S(2)}, u32[]{:S(2)}) collective-permute-start(bf16[8,24,768]{2,1,0:T(8,128)(2,1)S(1)} %get-tuple-element.64), channel_id=1, source_target_pairs={{0,16},{1,17},{2,18},{3,19},{4,20},{5,21},{6,22},{7,23},{8,24},{9,... | collective-permute-start | bytes 884744 | tf_op jit(solution)/shard_map/ppermute | solution.py:475
  265.4 26.5 %collective-permute-start.23 = (bf16[8,24,768]{2,1,0:T(8,128)(2,1)S(1)}, bf16[8,24,768]{2,1,0:T(8,128)(2,1)S(1)}, u32[]{:S(2)}, u32[]{:S(2)}) collective-permute-start(bf16[8,24,768]{2,1,0:T(8,128)(2,1)S(1)} %get-tuple-element.63), channel_id=1, source_target_pairs={{0,8},{1,9},{2,10},{3,11},{4,12},{5,13},{6,14},{7,15},{8,16},{9,17... | collective-permute-start | bytes 884744 | tf_op jit(solution)/shard_map/ppermute | solution.py:475
  (14 other events, 221.7 us)
Sparse Core Ops, SparseCore 0:
  11.5 96.8 all-gather.2

commit v2 on v1

v2 whole, which is shorter than its diff:
```python
import functools
import math

import jax
import jax.numpy as jnp
from jax import lax
from jax.experimental import pallas as pl
from jax.experimental.pallas import tpu as pltpu
from jax.sharding import PartitionSpec as P

HD = 64
EPS = 1e-05
MASKED = -1e30
F32 = jnp.float32
BF16 = jnp.bfloat16
VMEM_LIMIT = 48 * 1024 * 1024


def dot(a, b, a_dim, b_dim):
    return lax.dot_general(a, b, (((a_dim,), (b_dim,)), ((), ())), preferred_element_type=F32)


def normalise(values):
    centered = values - jnp.mean(values, axis=-1, keepdims=True)
    spread = jnp.mean(centered * centered, axis=-1, keepdims=True)
    inv = lax.rsqrt(spread + EPS)
    return centered * inv, inv


def head_pair(block):
    lane = lax.broadcasted_iota(jnp.int32, block.shape, 1)
    zero = jnp.zeros_like(block)
    return jnp.concatenate([jnp.where(lane < HD, block, zero), jnp.where(lane >= HD, block, zero)], axis=0)


def own_lanes(stacked):
    half = stacked.shape[0] // 2
    lane = lax.broadcasted_iota(jnp.int32, (half, stacked.shape[1]), 1)
    return jnp.where(lane < HD, stacked[:half], stacked[half:])


def row_mask(seg_row):
    size = seg_row.shape[1]
    across = jnp.broadcast_to(seg_row.astype(F32), (size, size))
    return jnp.where(across == across.T, 0.0, MASKED)


def colsum(v):
    return jnp.sum(v, axis=0, keepdims=True)


Z, Y, X, CORES = 4, 2, 2, 2
PIECES = Z * Y * X * CORES


def merge_rows(blocks):
    count, rows, width = blocks.shape
    return blocks.astype(F32).reshape(count * rows, width).astype(BF16)


def slots(place, z, y, x):
    ys, xs = y ^ place[1], x ^ place[2]
    first = jnp.where(place[3] == 0, ys, xs)
    second = jnp.where(place[3] == 0, xs, ys)
    return first, second, (place[0] - z + Z) % Z


def put_blocks(place, z, y, x, even, odd, keep, send, tail=()):
    first, second, deep = slots(place, z, y, x)
    mine = place[3] == 0
    keep[(first, second, deep) + tail] = jnp.where(mine, even, odd)
    send[(second, first, deep) + tail] = jnp.where(mine, odd, even)


def pick(place, parts, z, y, x):
    mine0, mine1, other0, other1 = parts
    first, second, deep = slots(place, z, y, x)
    mine = jnp.where(first == 0, mine0[second, deep], mine1[second, deep])
    other = jnp.where(second == 0, other0[first, deep], other1[first, deep])
    even = place[3] == 0
    return jnp.where(even, mine, other), jnp.where(even, other, mine)


def spread(small, cut, row, stride, start, length):
    lane = lax.broadcasted_iota(jnp.int32, (8, 128), 1)
    tiles = [jnp.zeros((8, 128), F32) for _ in range(length // 128)]
    for i in range(PIECES):
        at = start + i * stride
        tile, shift = at // 128, at % 128
        block = small[i * cut + row : i * cut + row + 8]
        if shift:
            block = pltpu.roll(block, shift, 1)
        if shift + cut <= 128:
            tiles[tile] = tiles[tile] + block
        else:
            tiles[tile] = tiles[tile] + jnp.where(lane >= shift, block, 0.0)
            tiles[tile + 1] = tiles[tile + 1] + jnp.where(lane < shift, block, 0.0)
    return jnp.concatenate(tiles, axis=1)


def attn_forward_body(
    place, tok, time, seg, mine0, mine1, other0, other1, n1, qkv, probs, att, hid, n2, weights, vec, bfc, *, rows
):
    size = tok.shape[0] // rows
    width = tok.shape[1]

    @pl.when(pl.program_id(0) == 0)
    def _():
        for z in range(Z):
            for y in range(Y):
                for x in range(X):
                    both = pick(place, (mine0, mine1, other0, other1), z, y, x)
                    both = jnp.concatenate([b.astype(F32) for b in both], axis=0)
                    step = both.shape[0]
                    at = ((z * Y + y) * X + x) * step
                    weights[at : at + step, :] = both.astype(BF16)
        small = weights[:, 4 * width :].astype(F32)
        cut = width // PIECES
        vec[...] = spread(small, cut, 0, cut, 0, width)
        early = spread(small, cut, 8, 2 * cut, 0, bfc.shape[1])
        late = spread(small, cut, 8, 2 * cut, cut, bfc.shape[1])
        bfc[...] = early[0:2] + late[2:4]

    x = tok[...].astype(F32)
    x = jnp.concatenate(
        [x[r * size : (r + 1) * size] + time[r].astype(F32) for r in range(rows)], axis=0
    )
    nhat, _ = normalise(x)
    normed = (nhat * vec[0:1, :] + vec[1:2, :]).astype(BF16)
    n1[...] = normed
    for part in range(3):
        cols = slice(part * width, (part + 1) * width)
        block = dot(normed, weights[:, cols], 1, 0)
        if part == 0:
            block = block + vec[2:3, :]
        if part == 2:
            block = block + vec[3:4, :]
        qkv[:, cols] = block.astype(BF16)
    pairs = width // (2 * HD)
    for r in range(rows):
        sl = slice(r * size, (r + 1) * size)
        mask = row_mask(seg[r])
        for p in range(pairs):
            c = 2 * HD * p
            q = qkv[sl, c : c + 2 * HD] * jnp.asarray(HD**-0.5, BF16)
            k = head_pair(qkv[sl, width + c : width + c + 2 * HD])
            v = head_pair(qkv[sl, 2 * width + c : 2 * width + c + 2 * HD])
            s = dot(q, k, 1, 1)
            halves = []
            for h in range(2):
                sh = s[:, h * size : (h + 1) * size] + mask
                e = jnp.exp(sh - jnp.max(sh, axis=-1, keepdims=True))
                halves.append((e / jnp.sum(e, axis=-1, keepdims=True)).astype(BF16))
            pr = jnp.concatenate(halves, axis=1)
            probs[r, p] = pr
            att[sl, c : c + 2 * HD] = dot(pr, v, 1, 0).astype(BF16)
    hidden = x + dot(att[...], weights[:, 3 * width : 4 * width], 1, 0) + vec[4:5, :]
    hid[...] = hidden
    nhat2, _ = normalise(hidden)
    n2[...] = (nhat2 * vec[5:6, :] + vec[6:7, :]).astype(BF16)


def attn_forward(place, tok, time, seg, gathered, rows=2):
    row_count = seg.shape[0]
    toks, width = tok.shape
    size = toks // row_count
    tm = rows * size
    pairs = width // (2 * HD)
    wide = gathered[0].shape[-1]
    full = lambda s: pl.BlockSpec(s, lambda i: (0,) * len(s))
    tile = lambda cols: pl.BlockSpec((tm, cols), lambda i: (i, 0))
    return pl.pallas_call(
        functools.partial(attn_forward_body, rows=rows),
        grid=(row_count // rows,),
        in_specs=[
            pl.BlockSpec(memory_space=pltpu.SMEM),
            tile(width),
            pl.BlockSpec((rows, 1, width), lambda i: (i, 0, 0)),
            pl.BlockSpec((rows, 1, size), lambda i: (i, 0, 0)),
        ]
        + [full(g.shape) for g in gathered],
        out_specs=[
            tile(width),
            tile(3 * width),
            pl.BlockSpec((rows, pairs, size, 2 * size), lambda i: (i, 0, 0, 0)),
            tile(width),
            tile(width),
            tile(width),
            full((width, wide)),
            full((8, width)),
            full((2, 2 * width)),
        ],
        out_shape=[
            jax.ShapeDtypeStruct((toks, width), BF16),
            jax.ShapeDtypeStruct((toks, 3 * width), BF16),
            jax.ShapeDtypeStruct((row_count, pairs, size, 2 * size), BF16),
            jax.ShapeDtypeStruct((toks, width), BF16),
            jax.ShapeDtypeStruct((toks, width), F32),
            jax.ShapeDtypeStruct((toks, width), BF16),
            jax.ShapeDtypeStruct((width, wide), BF16),
            jax.ShapeDtypeStruct((8, width), F32),
            jax.ShapeDtypeStruct((2, 2 * width), F32),
        ],
        compiler_params=pltpu.CompilerParams(vmem_limit_bytes=VMEM_LIMIT),
        cost_estimate=pl.CostEstimate(flops=16 * 10**9, bytes_accessed=20 * 10**6, transcendentals=2 * 10**6),
        name="attn_forward",
    )(place, tok, time, seg, *gathered)


def ffn_body(place, n2, cot, fc, out, bfc, acc_out, acc_dn2, dbfc, keep, send, fc_s, out_s, act_s, dpre_s, *, tm, sub, half):
    step = pl.program_id(0)

    @pl.when(step == 0)
    def _():
        acc_out[...] = jnp.zeros_like(acc_out)
        acc_dn2[...] = jnp.zeros_like(acc_dn2)

    fc_s[...] = merge_rows(fc[:, 0])
    out_s[...] = merge_rows(out[...].reshape((-1,) + out.shape[2:]))
    chunk = fc_s.shape[1]
    for part in range(chunk // sub):
        cols = slice(part * sub, (part + 1) * sub)
        bias = bfc[half : half + 1, cols]
        db = jnp.zeros_like(bias)
        for m in range(n2.shape[0] // tm):
            sl = slice(m * tm, (m + 1) * tm)
            pre = dot(n2[sl, :], fc_s[:, cols], 1, 0) + bias
            d_act = dot(cot[sl, :], out_s[cols, :], 1, 1)
            cdf = 0.5 * lax.erf(pre * math.sqrt(0.5)) + 0.5
            density = jnp.exp(pre * pre * -0.5) * (1.0 / math.sqrt(2.0 * math.pi))
            act = (pre * cdf).astype(BF16)
            d_pre = (d_act * (cdf + pre * density)).astype(BF16)
            act_s[sl, cols] = act
            dpre_s[sl, cols] = d_pre
            db = db + jnp.sum(d_pre.astype(F32), axis=0, keepdims=True)
            acc_out[sl, :] += dot(act, out_s[cols, :], 1, 0)
            acc_dn2[sl, :] += dot(d_pre, fc_s[:, cols], 1, 1)
        dbfc[:, cols] = db
    grad = dot(act_s[...], cot[...], 0, 0)
    blocks, rows = out.shape[1:3]
    planes = out.shape[0] // (Y * X * CORES)
    for z in range(planes):
        for y in range(Y):
            for x in range(X):
                for b in range(blocks):
                    at = (((z * Y + y) * X + x) * CORES * blocks + b) * rows
                    even = grad[at : at + rows].astype(BF16)
                    odd = grad[at + blocks * rows : at + (blocks + 1) * rows].astype(BF16)
                    put_blocks(place, step * planes + z, y, x, even, odd, keep, send, (blocks + b,))
    grad = dot(n2[...], dpre_s[...], 0, 0)
    for z in range(Z):
        for y in range(Y):
            for x in range(X):
                at = ((z * Y + y) * X + x) * CORES * rows
                even = grad[at : at + rows].astype(BF16)
                odd = grad[at + rows : at + 2 * rows].astype(BF16)
                put_blocks(place, z, y, x, even, odd, keep, send, (step,))


def ffn(place, n2, cot, gathered, bfc, half, tm=512, sub=256):
    toks, width = n2.shape
    pieces, _, rows, _ = gathered.shape
    blocks = 2
    count = 2 * blocks
    once = pl.Buffered(buffer_count=1)
    full = lambda s: pl.BlockSpec(s, lambda j: (0,) * len(s), pipeline_mode=once)
    whole = lambda s: pl.BlockSpec(s, lambda j: (0,) * len(s))
    parted = (Y, X, Z, count, rows, width)
    return pl.pallas_call(
        functools.partial(ffn_body, tm=tm, sub=sub, half=half),
        grid=(blocks,),
        in_specs=[
            pl.BlockSpec(memory_space=pltpu.SMEM),
            full((toks, width)),
            full((toks, width)),
            pl.BlockSpec((pieces, 1, rows, width), lambda j: (0, count * half + j, 0, 0)),
            pl.BlockSpec((pieces // blocks, blocks, rows, width), lambda j: (j, 2 * half + 1, 0, 0)),
            pl.BlockSpec((2, width), lambda j: (0, j)),
        ],
        out_specs=[
            whole((toks, width)),
            whole((toks, width)),
            pl.BlockSpec((1, width), lambda j: (0, j)),
            whole(parted),
            whole(parted),
        ],
        out_shape=[
            jax.ShapeDtypeStruct((toks, width), F32),
            jax.ShapeDtypeStruct((toks, width), F32),
            jax.ShapeDtypeStruct((1, blocks * width), F32),
            jax.ShapeDtypeStruct(parted, BF16),
            jax.ShapeDtypeStruct(parted, BF16),
        ],
        scratch_shapes=[
            pltpu.VMEM((width, width), BF16),
            pltpu.VMEM((width, width), BF16),
            pltpu.VMEM((toks, width), BF16),
            pltpu.VMEM((toks, width), BF16),
        ],
        compiler_params=pltpu.CompilerParams(vmem_limit_bytes=VMEM_LIMIT),
        cost_estimate=pl.CostEstimate(flops=15 * 10**9, bytes_accessed=20 * 10**6, transcendentals=3 * 10**6),
        name="ffn",
    )(place, n2, cot, gathered, gathered, bfc)


def attn_backward_body(
    tok, time, hid, out0, out1, dn20, dn21, cot, qkv, probs, weights, vec, *refs, rows
):
    layer_out, dtok, dtime, dbr, dqkv, sums = refs[-6:]
    width = hid.shape[1]
    size = hid.shape[0] // rows

    @pl.when(pl.program_id(0) == 0)
    def _():
        sums[...] = jnp.zeros_like(sums)

    hidden = hid[...]
    layer_out[...] = (hidden + (out0[...] + out1[...]) + vec[7:8, :]).astype(BF16)
    nhat, inv = normalise(hidden)
    dn2 = dn20[...] + dn21[...]
    cotangent = cot[...].astype(F32)
    q = dn2 * vec[5:6, :]
    mean_q = jnp.mean(q, axis=-1, keepdims=True)
    mean_qn = jnp.mean(q * nhat, axis=-1, keepdims=True)
    d_hidden = cotangent + (q - mean_q - nhat * mean_qn) * inv
    dtok[...] = d_hidden
    branch = d_hidden.astype(BF16)
    dbr[...] = branch
    sums[0:1, :] += colsum(dn2 * nhat)
    sums[1:2, :] += colsum(dn2)
    sums[2:3, :] += colsum(branch.astype(F32))
    sums[3:4, :] += colsum(cotangent)
    d_mixed = dot(branch, weights[:, 3 * width : 4 * width], 1, 1).astype(BF16)
    pairs = width // (2 * HD)
    for r in range(rows):
        sl = slice(r * size, (r + 1) * size)
        for p in range(pairs):
            c = 2 * HD * p
            qb = qkv[sl, c : c + 2 * HD] * jnp.asarray(HD**-0.5, BF16)
            k = head_pair(qkv[sl, width + c : width + c + 2 * HD])
            v = head_pair(qkv[sl, 2 * width + c : 2 * width + c + 2 * HD])
            dm = d_mixed[sl, c : c + 2 * HD]
            pr = probs[r, p]
            dp = dot(dm, v, 1, 1)
            pf = pr.astype(F32)
            prod = dp * pf
            ds = jnp.concatenate(
                [
                    prod[:, h * size : (h + 1) * size]
                    - pf[:, h * size : (h + 1) * size]
                    * jnp.sum(prod[:, h * size : (h + 1) * size], axis=-1, keepdims=True)
                    for h in range(2)
                ],
                axis=1,
            ).astype(BF16)
            dv = own_lanes(dot(pr, dm, 0, 0))
            dk = own_lanes(dot(ds, qb, 0, 0))
            dq = dot(ds, k, 1, 0) * HD**-0.5
            dqkv[sl, c : c + 2 * HD] = dq.astype(BF16)
            dqkv[sl, width + c : width + c + 2 * HD] = dk.astype(BF16)
            dqkv[sl, 2 * width + c : 2 * width + c + 2 * HD] = dv.astype(BF16)
    sums[4:5, :] += colsum(dqkv[:, :width].astype(F32))
    sums[5:6, :] += colsum(dqkv[:, 2 * width :].astype(F32))

    x = tok[...].astype(F32)
    x = jnp.concatenate(
        [x[r * size : (r + 1) * size] + time[r].astype(F32) for r in range(rows)], axis=0
    )
    nhat, inv = normalise(x)
    dn1 = dot(dqkv[...], weights[:, : 3 * width], 1, 1)
    sums[6:7, :] += colsum(dn1 * nhat)
    sums[7:8, :] += colsum(dn1)
    q = dn1 * vec[0:1, :]
    mean_q = jnp.mean(q, axis=-1, keepdims=True)
    mean_qn = jnp.mean(q * nhat, axis=-1, keepdims=True)
    d_tok = dtok[...] + (q - mean_q - nhat * mean_qn) * inv
    dtok[...] = d_tok
    for r in range(rows):
        dtime[r] = colsum(d_tok[r * size : (r + 1) * size])


def attn_backward(tok, time, hid, outs, dn2s, cot, qkv, probs, weights, vec, base, steps, before=(), rows=2):
    row_count, pairs, size, _ = probs.shape
    width = hid.shape[1]
    tm = rows * size
    toks = row_count * size
    once = pl.Buffered(buffer_count=1)
    full = lambda s: pl.BlockSpec(s, lambda i: (0,) * len(s), pipeline_mode=once)
    tile = lambda cols: pl.BlockSpec((tm, cols), lambda i: (i + base, 0))
    per_row = pl.BlockSpec((rows, 1, width), lambda i: (i + base, 0, 0))
    return pl.pallas_call(
        functools.partial(attn_backward_body, rows=rows),
        grid=(steps,),
        in_specs=[tile(width), per_row]
        + [tile(width)] * 6
        + [
            tile(3 * width),
            pl.BlockSpec((rows, pairs, size, 2 * size), lambda i: (i + base, 0, 0, 0)),
            full(weights.shape),
            full(vec.shape),
        ]
        + [pl.BlockSpec(memory_space=pl.ANY)] * len(before),
        out_specs=[
            tile(width),
            tile(width),
            per_row,
            tile(width),
            tile(3 * width),
            pl.BlockSpec((8, width), lambda i: (0, 0)),
        ],
        input_output_aliases={12 + k: k for k in range(len(before))},
        out_shape=[
            jax.ShapeDtypeStruct((toks, width), BF16),
            jax.ShapeDtypeStruct((toks, width), F32),
            jax.ShapeDtypeStruct((row_count, 1, width), F32),
            jax.ShapeDtypeStruct((toks, width), BF16),
            jax.ShapeDtypeStruct((toks, 3 * width), BF16),
            jax.ShapeDtypeStruct((8, width), F32),
        ],
        compiler_params=pltpu.CompilerParams(vmem_limit_bytes=VMEM_LIMIT),
        cost_estimate=pl.CostEstimate(flops=6 * 10**9 * steps, bytes_accessed=10 * 10**6 * steps, transcendentals=0),
        name="attn_backward",
    )(tok, time, hid, *outs, *dn2s, cot, qkv, probs, weights, vec, *before)


def collect(vectors, cut, stride, start, piece):
    at = start + piece * stride
    tile, shift = at // 128, at % 128
    lane = lax.broadcasted_iota(jnp.int32, (vectors.shape[0], 128), 1)
    block = vectors[:, tile * 128 : (tile + 1) * 128]
    if shift + cut > 128:
        block = jnp.where(lane >= shift, block, vectors[:, (tile + 1) * 128 : (tile + 2) * 128])
    if shift:
        block = pltpu.roll(block, 128 - shift, 1)
    return jnp.where(lane < cut, block, 0.0)


def weight_grad_body(place, *refs, columns, with_vectors):
    keep, send = refs[-2:]
    rows = keep.shape[3]
    width = refs[0].shape[1]
    step = pl.program_id(0)

    def emit(grad, tail):
        for z in range(Z):
            for y in range(Y):
                for x in range(X):
                    at = ((z * Y + y) * X + x) * CORES * rows
                    even = grad[at : at + rows].astype(BF16)
                    odd = grad[at + rows : at + 2 * rows].astype(BF16)
                    put_blocks(place, z, y, x, even, odd, keep, send, tail)

    for k in range(columns):

        @pl.when(step == k)
        def _(k=k):
            emit(dot(refs[0][...], refs[1][...], 0, 0), (slice(None), slice(k * width, (k + 1) * width)))

    if with_vectors:

        @pl.when(step == columns)
        def _():
            att, dbr, sums0, sums1, dbfc0, dbfc1 = refs[2:8]
            emit(dot(att[...], dbr[...], 0, 0), (slice(None), slice(columns * width, (columns + 1) * width)))
            vectors = sums0[...] + sums1[...]
            pad = jnp.zeros((6, dbfc0.shape[1]), F32)
            hidden = jnp.concatenate([dbfc0[...], dbfc1[...], pad], axis=0)

            def block(piece):
                early = collect(hidden, rows, 2 * rows, 0, piece)
                late = collect(hidden, rows, 2 * rows, rows, piece)
                top = collect(vectors, rows, rows, 0, piece)
                rest = [early[:2], late[:2], jnp.zeros((rows - 12, 128), F32)]
                return jnp.concatenate([top] + rest, axis=0).astype(BF16)

            for z in range(Z):
                for y in range(Y):
                    for x in range(X):
                        piece = ((z * Y + y) * X + x) * CORES
                        tail = (slice(None), slice((columns + 1) * width, (columns + 1) * width + 128))
                        put_blocks(place, z, y, x, block(piece), block(piece + 1), keep, send, tail)


def weight_grad(place, n1, dqkv, first, columns, extra=()):
    toks, width = n1.shape
    rows = width // PIECES
    once = pl.Buffered(buffer_count=1)
    full = lambda a: pl.BlockSpec(a.shape, lambda j: (0, 0), pipeline_mode=once)
    parted = (Y, X, Z, rows, columns * width + (width + 128 if extra else 0))
    whole = pl.BlockSpec(parted, lambda j: (0,) * 5)
    shape = jax.ShapeDtypeStruct(parted, BF16)
    return pl.pallas_call(
        functools.partial(weight_grad_body, columns=columns, with_vectors=bool(extra)),
        grid=(columns + bool(extra),),
        in_specs=[
            pl.BlockSpec(memory_space=pltpu.SMEM),
            full(n1),
            pl.BlockSpec((toks, width), lambda j: (0, first + jnp.minimum(j, columns - 1))),
        ]
        + [full(e) for e in extra],
        out_specs=[whole, whole],
        out_shape=[shape, shape],
        compiler_params=pltpu.CompilerParams(vmem_limit_bytes=VMEM_LIMIT),
        cost_estimate=pl.CostEstimate(flops=25 * 10**8, bytes_accessed=8 * 10**6, transcendentals=0),
        name="weight_grad",
    )(place, n1, dqkv, *extra)


def flip(position):
    return lambda i: i ^ position


def exchange(array, partner):
    return lax.ppermute(array, "dp", [(i, partner(i)) for i in range(PIECES)])


def plane_partner(stage):
    def partner(i):
        along_y = (i % 2 == 0) == (stage == "first")
        return i ^ (4 if along_y else 2)

    return partner


class CubeGather:
    def __init__(self, block):
        self.ready, self.step, self.mine, self.parts = block, 0, None, None

    def send(self):
        if self.step == 0:
            ring = [exchange(self.ready, lambda i, k=k: (i + 8 * k) % PIECES) for k in range(1, Z)]
            self.ready = jnp.stack([self.ready] + ring)
        elif self.step == 1:
            self.ready = jnp.stack([self.ready, exchange(self.ready, plane_partner("second"))])
        elif self.step == 2:
            self.ready = (self.ready, exchange(self.ready, plane_partner("first")))
        else:
            self.parts = self.ready + tuple(exchange(half, flip(1)) for half in self.ready)
        self.step += 1


class CubeSum:
    def __init__(self, keep, send):
        self.grads, self.keep, self.ahead = (keep, send), keep, send
        self.came, self.first, self.second, self.rest = None, None, None, None

    def part(self, *at):
        total = self.keep[at].astype(F32) + self.came[at].astype(F32)
        if self.first is not None:
            total = total + self.first[at[1:]].astype(F32)
        if self.second is not None:
            total = total + self.second[at[2:]].astype(F32)
        return total

    def send(self):
        if self.came is None:
            self.came = exchange(self.ahead, flip(1))
        elif self.first is None:
            self.ahead = self.part(1).astype(BF16)
            self.first = exchange(self.ahead, plane_partner("first"))
        elif self.second is None:
            self.ahead = self.part(0, 1).astype(BF16)
            self.second = exchange(self.ahead, plane_partner("second"))
        else:
            self.ahead = [self.part(0, 0, k).astype(BF16) for k in range(1, Z)]
            self.rest = [
                exchange(block, lambda i, k=k: (i - 8 * k) % PIECES) for k, block in enumerate(self.ahead, 1)
            ]

    def total(self):
        return self.part(0, 0, 0) + sum(block.astype(F32) for block in self.rest)


def hold(first, *then):
    return tuple(lax.optimization_barrier((first, one))[1] for one in then)


def sum_over(values, *bits):
    for bit in bits:
        values = values + exchange(values, flip(bit))
    return values


def cut_any(every):
    every = every.reshape((Z, Y, X, CORES, every.shape[0] // PIECES) + every.shape[1:])
    deep = jnp.array([0, 3, 2, 1])
    even = jnp.transpose(every[:, :, :, 0], (1, 2, 0, 3, 4))[:, :, deep]
    odd = jnp.transpose(every[:, :, :, 1], (2, 1, 0, 3, 4))[:, :, deep]
    return even[0], even[1], odd[0], odd[1]


def natural_blocks(keep, send):
    deep = jnp.array([0, 3, 2, 1])
    rest = tuple(range(3, keep.ndim))
    even = jnp.transpose(keep[:, :, deep], (2, 0, 1) + rest)
    odd = jnp.transpose(send[:, :, deep], (2, 1, 0) + rest)
    both = jnp.stack([even, odd], axis=3)
    return both.reshape((PIECES,) + both.shape[4:])


def on_device(
    tokens,
    segment_ids,
    time_embed,
    norm1_gain,
    norm1_shift,
    w_qkv,
    b_query,
    b_value,
    w_proj,
    b_proj,
    norm2_gain,
    norm2_shift,
    w_fc,
    b_fc,
    w_out,
    b_out,
    cotangent,
):
    row_count, row_len, width = tokens.shape
    toks = row_count * row_len
    devices = lax.axis_size("dp")
    cube = devices == PIECES
    rank = lax.axis_index("dp")
    grad_scale = 1.0 / math.sqrt(toks * devices)
    own = w_proj.shape[0]
    ratio = b_fc.shape[0] // own
    if cube:
        place = jnp.stack([rank // 8, (rank // 4) % 2, (rank // 2) % 2, rank % 2]).astype(jnp.int32)
    else:
        place = jnp.zeros((4,), jnp.int32)

    small = jnp.concatenate(
        [norm1_gain, norm1_shift, b_query, b_value, b_proj, norm2_gain, norm2_shift, b_out, b_fc]
    ).reshape(8 + ratio, own)
    order = list(range(8)) + [8 + 2 * h + k for k in range(ratio // 2) for h in range(2)]
    small = jnp.concatenate([small[v : v + 1] for v in order], axis=0)
    cut = width // PIECES
    halves = 2
    blocks = ratio // halves
    ffn_fc = lambda w: w.reshape(-1, PIECES, halves, blocks * cut).transpose(2, 0, 1, 3).reshape(halves, -1, blocks, width)
    if cube:
        ffn_block = jnp.concatenate(
            [ffn_fc(w_fc).transpose(0, 2, 1, 3), w_out.reshape(halves, blocks, own, width)], axis=1
        )
        ffn_full = lax.all_gather(ffn_block.reshape(-1, own, width), "dp", axis=0)
        small = jnp.pad(small, ((0, own - small.shape[0]), (0, 128 - own)))
        attn_gather = CubeGather(jnp.concatenate([w_qkv, w_proj, small], axis=1))
        for _ in range(4):
            attn_gather.send()
        attn_full = attn_gather.parts
    else:
        whole = lambda w: lax.all_gather(w, "dp", axis=0, tiled=True)
        natural = whole(small.T.reshape(own, -1))
        vectors = natural[:, :8].T
        hidden_bias = whole(b_fc).reshape(PIECES, ratio, cut)
        small = jnp.concatenate(
            [vectors.reshape(8, PIECES, cut).transpose(1, 0, 2), hidden_bias[:, jnp.array([0, 2, 1, 3])]], axis=1
        )
        small = jnp.pad(small, ((0, 0), (0, cut - small.shape[1]), (0, 128 - cut))).reshape(width, 128)
        attn_full = cut_any(jnp.concatenate([whole(w_qkv), whole(w_proj), small], axis=1))
        fc_full = ffn_fc(whole(w_fc)).reshape(halves, PIECES, cut, blocks, width).transpose(1, 0, 3, 2, 4)
        out_full = whole(w_out).reshape(PIECES, halves, blocks, cut, width)
        ffn_full = jnp.concatenate([fc_full, out_full], axis=2).reshape(PIECES, -1, cut, width)

    flat = tokens.reshape(toks, width)
    times = time_embed.reshape(row_count, 1, width)
    segments = segment_ids.reshape(row_count, 1, row_len)
    cot = cotangent.reshape(toks, width)
    n1, qkv, probs, att, hid, n2, attn_w, vec, bfc = attn_forward(place, flat, times, segments, attn_full)

    out0, dn20, dbfc0, *grads0 = ffn(place, n2, cot, ffn_full, bfc, 0)
    sum0 = CubeSum(*grads0)
    if cube:
        sum0.send()
    bfc, out0 = lax.optimization_barrier((bfc, out0))
    out1, dn21, dbfc1, *grads1 = ffn(place, n2, cot, ffn_full, bfc, 1)
    sum1 = CubeSum(*grads1)
    backward = lambda hid, base, steps, before: attn_backward(
        flat, times, hid, (out0, out1), (dn20, dn21), cot, qkv, probs, attn_w, vec, base, steps, before
    )
    steps = row_count // 2
    if cube:
        sum0.send()
        sum1.send()
        (hid,) = hold(sum0.ahead, hid)
    *before, sums0 = backward(hid, 0, 1, ())
    if cube:
        sum1.send()
        sum0.send()
        (hid,) = hold(sum1.ahead, *hold(sum0.ahead, hid))
    layer_out, d_tokens, d_time, dbr, dqkv, sums1 = backward(hid, 1, steps - 1, before)
    if cube:
        sum0.send()
        sum1.send()
        (dqkv,) = hold(sum1.ahead, *hold(sum0.ahead[0], dqkv))
    attn0 = CubeSum(*weight_grad(place, n1, dqkv, 0, 2))
    if cube:
        attn0.send()
        attn0.keep, dbr = lax.optimization_barrier((attn0.keep, dbr))
    attn1 = CubeSum(*weight_grad(place, n1, dqkv, 2, 1, (att, dbr, sums0, sums1, dbfc0, dbfc1)))
    if cube:
        attn0.send()
        attn1.send()
        attn1.send()
        sum1.second, *sum0.rest = hold(attn1.ahead, sum1.second, *sum0.rest)
        sum1.send()
        attn0.send()
        attn1.send()
        sum1.rest = hold(attn1.ahead, *sum1.rest)
        attn0.send()
        attn1.send()
        own_ffn = jnp.stack([sum0.total(), sum1.total()])
        (own_ffn,) = hold(attn1.ahead[0], own_ffn)
        own_attn = jnp.concatenate([attn0.total(), attn1.total()], axis=1)
        own_out = own_ffn[:, blocks:].reshape(ratio * own, width)
        own_fc = own_ffn[:, :blocks].transpose(2, 0, 1, 3).reshape(own, halves, PIECES, blocks * own)
        own_fc = own_fc.transpose(0, 2, 1, 3).reshape(own, ratio * width)
        vectors = own_attn[:, 4 * width :]
        mine = vectors[:8, :own]
        own_bfc = jnp.concatenate([vectors[8 + v, :own] for v in (0, 2, 1, 3)])
    else:
        scatter = lambda g: lax.psum_scatter(g, "dp", scatter_dimension=0, tiled=True)
        grads = jnp.concatenate([natural_blocks(*a.grads) for a in (attn0, attn1)], axis=-1).astype(F32)
        own_attn = scatter(grads[:, :, : 4 * width].reshape(width, -1))
        vectors = lax.psum(grads[:, :, 4 * width : 4 * width + cut], "dp")
        mine = lax.dynamic_slice(
            vectors[:, :8].transpose(1, 0, 2).reshape(8, width), (0, rank * own), (8, own)
        )
        hidden_grad = vectors[:, jnp.array([8, 10, 9, 11])].reshape(-1)
        own_bfc = lax.dynamic_slice(hidden_grad, (rank * own * ratio,), (own * ratio,))
        grads = jnp.stack([natural_blocks(*s.grads) for s in (sum0, sum1)], axis=1).astype(F32)
        out_grad = grads[:, :, blocks:].reshape(ratio * width, width)
        own_out = scatter(out_grad)
        fc_grad = grads[:, :, :blocks].transpose(0, 3, 1, 2, 4).reshape(width, halves, PIECES, blocks * cut)
        own_fc = scatter(fc_grad.transpose(0, 2, 1, 3).reshape(width, ratio * width))
    mine, own_bfc = mine * grad_scale, own_bfc * grad_scale
    own_attn = own_attn * grad_scale
    return (
        layer_out.reshape(tokens.shape),
        d_tokens.reshape(tokens.shape),
        d_time.reshape(time_embed.shape),
        mine[6],
        mine[7],
        own_attn[:, : 3 * width],
        mine[4],
        mine[5],
        own_attn[:, 3 * width : 4 * width],
        mine[2],
        mine[0],
        mine[1],
        own_fc * grad_scale,
        own_bfc,
        own_out * grad_scale,
        mine[3],
    )


def solution(mesh):
    in_specs = (
        P("dp", None, None),
        P("dp", None),
        P("dp", None),
        P("dp"),
        P("dp"),
        P("dp", None),
        P("dp"),
        P("dp"),
        P("dp", None),
        P("dp"),
        P("dp"),
        P("dp"),
        P("dp", None),
        P("dp"),
        P("dp", None),
        P("dp"),
        P("dp", None, None),
    )
    out_specs = (
        P("dp", None, None),
        P("dp", None, None),
        P("dp", None),
        P("dp"),
        P("dp"),
        P("dp", None),
        P("dp"),
        P("dp"),
        P("dp", None),
        P("dp"),
        P("dp"),
        P("dp"),
        P("dp", None),
        P("dp"),
        P("dp", None),
        P("dp"),
    )
    return jax.shard_map(
        on_device, mesh=mesh, in_specs=in_specs, out_specs=out_specs, check_vma=False
    )
```

time: 302 us -> 278 us (0.921)
  waiting for transfers between devices: 116 us -> 80.9 us
  Pallas kernels: 103 us -> 112 us
  starting transfers between devices: 29 us -> 37.9 us
  local copies, waits for them, and re-layouts: 21 us -> 13.9 us
    ppermute x24 -> x31, waiting for transfers between devices: 103 us -> 67.8 us  [exchange(): return lax.ppermute(array, 'dp', [(i, partner(i)) for i in range(PIECES)])]
    ppermute x24 -> x31, starting transfers between devices: 29 us -> 37.9 us  [exchange(): return lax.ppermute(array, 'dp', [(i, partner(i)) for i in range(PIECES)])]
    pallas_call x4 -> x6, Pallas kernels: 83.5 us -> 91.9 us  [the longest x2 44.1 us: ffn(): pl.pallas_call(functools.partial(ffn_body, tm=tm, sub=sub, half=half), gr...]
    another operation x8 -> x0, local copies, waits for them, and re-layouts: 5.98 us -> none  [on_device(): jnp.stack([norm1_gain, norm1_shift, b_query, b_value, b_proj, norm2_gain,...]
    convert_element_type x6 -> x12, other arithmetic: 12 us -> 9.31 us  [the longest x4 4.25 us: send(): self.ahead = self.part(0, 1).astype(BF16)]
  transfers between devices with their start and end apart: 25 -> 32, of which waited for: 15 -> 14; matrix products, arithmetic and copies ran while one was open for 10% -> 5% of each run, Pallas kernels for 20% -> 31%
where the time goes in v2:
time: 278 us; the launch traced here: 275 us
  Pallas kernels  112 us (40%)
  waiting for transfers between devices  80.9 us (29%)
  starting transfers between devices  37.9 us (14%)
  other arithmetic  15.5 us (6%)
  between operations  14.7 us (5%)
  local copies, waits for them, and re-layouts  13.9 us (5%)
    ppermute x31, waiting for transfers between devices, exchange(): return lax.ppermute(array, 'dp', [(i, partner(i)) for i in range(PIECES)])  67.8 us
    pallas_call x2, Pallas kernels, ffn(): pl.pallas_call(functools.partial(ffn_body, tm=tm, sub=sub, half=half), gr...  44.1 us
    pallas_call x2, Pallas kernels, attn_backward(): pl.pallas_call(functools.partial(attn_backward_body, rows=rows), grid=(st...  38.3 us
    ppermute x31, starting transfers between devices, exchange(): return lax.ppermute(array, 'dp', [(i, partner(i)) for i in range(PIECES)])  37.9 us
    pallas_call x1, Pallas kernels, attn_forward(): pl.pallas_call(functools.partial(attn_forward_body, rows=rows), grid=(row...  20.3 us
    all_gather x1, waiting for transfers between devices, on_device(): ffn_full = lax.all_gather(ffn_block.reshape(-1, own, width), 'dp', axis=0)  13.1 us
    pallas_call x2, Pallas kernels, weight_grad(): pl.pallas_call(functools.partial(weight_grad_body, columns=columns, with_...  9.49 us
  transfers between devices with their start and end apart: 32, of which 14 were waited for; matrix products, arithmetic and copies ran while one was open for 5% of the time, Pallas kernels for 31%

profile of v2, /device:TPU:0, one launch (start us, length us, event | category | flops | bytes accessed | tf_op | source)
XLA Modules:
  0.0 275.2 jit_solution(2918415777870696267)
XLA Ops:
  11.6 5.1 %collective-permute-start.2 = (bf16[24,3200]{1,0:T(8,128)(2,1)S(1)}, bf16[24,3200]{1,0:T(8,128)(2,1)S(1)}, u32[]{:S(2)}, u32[]{:S(2)}) collective-permute-start(bf16[24,3200]{1,0:T(8,128)(2,1)S(1)} %get-tuple-element.141), channel_id=1, source_target_pairs={{0,24},{1,25},{2,26},{3,27},{4,28},{5,29},{6,30},{7,31},{8,0},{9,1... | collective-permute-start | bytes 460808 | tf_op jit(solution)/shard_map/ppermute | solution.py:514
  17.8 3.4 %collective-permute-done.2 = bf16[24,3200]{1,0:T(8,128)(2,1)S(1)} collective-permute-done((bf16[24,3200]{1,0:T(8,128)(2,1)S(1)}, bf16[24,3200]{1,0:T(8,128)(2,1)S(1)}, u32[]{:S(2)}, u32[]{:S(2)}) %collective-permute-start.2) | collective-permute-done | bytes 153632 | tf_op jit(solution)/shard_map/ppermute | solution.py:514
  21.2 13.7 %collective-permute-done.1 = bf16[24,3200]{1,0:T(8,128)(2,1)S(1)} collective-permute-done((bf16[24,3200]{1,0:T(8,128)(2,1)S(1)}, bf16[24,3200]{1,0:T(8,128)(2,1)S(1)}, u32[]{:S(2)}, u32[]{:S(2)}) %collective-permute-start.1) | collective-permute-done | bytes 153632 | tf_op jit(solution)/shard_map/ppermute | solution.py:514
  36.4 10.3 %collective-permute-done.3 = bf16[4,24,3200]{2,1,0:T(8,128)(2,1)S(1)} collective-permute-done((bf16[4,24,3200]{2,1,0:T(8,128)(2,1)S(1)}, bf16[4,24,3200]{2,1,0:T(8,128)(2,1)S(1)}, u32[]{:S(2)}, u32[]{:S(2)}) %collective-permute-start.3) | collective-permute-done | bytes 614432 | tf_op jit(solution)/shard_map/ppermute | solution.py:514
  47.5 16.2 %collective-permute-done.4.mine1 = bf16[2,4,24,3200]{3,2,1,0:T(8,128)(2,1)S(1)} collective-permute-done((bf16[2,4,24,3200]{3,2,1,0:T(8,128)(2,1)S(1)}, bf16[2,4,24,3200]{3,2,1,0:T(8,128)(2,1)S(1)}, u32[]{:S(2)}, u32[]{:S(2)}) %collective-permute-start.4) | collective-permute-done | bytes 1228832 | tf_op jit(solution)/shard_map/ppermute | solution.py:514
  63.6 3.4 %collective-permute-start.6 = (bf16[2,4,24,3200]{3,2,1,0:T(8,128)(2,1)S(1)}, bf16[2,4,24,3200]{3,2,1,0:T(8,128)(2,1)}, u32[]{:S(2)}, u32[]{:S(2)}) collective-permute-start(bf16[2,4,24,3200]{3,2,1,0:T(8,128)(2,1)S(1)} %collective-permute-done.4.mine1), channel_id=1, source_target_pairs={{0,1},{1,0},{2,3},{3,2},{4,5},{5,4},{6,7},{7,6},{8,9},{9,8},{10,11... | collective-permute-start | bytes 3686408 | tf_op jit(solution)/shard_map/ppermute | solution.py:514
  71.0 20.3 %attn_forward.1 = (bf16[1024,768]{1,0:T(8,128)(2,1)}, bf16[1024,2304]{1,0:T(8,128)(2,1)}, bf16[8,6,128,256]{3,2,1,0:T(8,128)(2,1)}, bf16[1024,768]{1,0:T(8,128)(...) custom-call(s32[4]{0:T(128)S(1)} %pad_add_fusion.place, ...), custom_call_target="tpu_custom_call" | custom-call | flops 16000000000 | bytes 20000000 | tf_op jit(solution)/shard_map/attn_forward/pallas_call | solution.py:172
  91.3 13.1 %all-gather.2.cloned.1.call-done.fc.out = bf16[32,8,24,768]{3,2,1,0:T(8,128)(2,1)} async-done(((bf16[1,8,24,768]{3,2,1,0:T(8,128)(2,1)}), bf16[32,8,24,768]{3,2,1,0:T(8,128)(2,1)}) %all-gather.2.cloned.1.call-update) | async-done | bytes 9437200 | tf_op jit(solution)/shard_map/all_gather | solution.py:646
  105.8 21.8 %ffn.2 = (f32[1024,768]{1,0:T(8,128)}, f32[1024,768]{1,0:T(8,128)}, f32[1,1536]{1,0:T(1,128)S(1)}, bf16[2,2,4,4,24,768]{5,4,3,2,1,0:T(8,128)(2,1)S(1)}, bf16[2,2,4,4,24,768]{5,4,3,2,1,0:T(8,128)(2,1)}) custom-call(s32[4]{0:T(128)S(1)} %pad_add_fusion.place, bf16[1024,768]{1,0:T(8,128)(2,1)S(1)} %copy-done.8, bf16[1024,768]{1,0:T(8,128)(2,1)S(1)} %bitcast.300, ...), custom_call_target="tpu_custom_call" | custom-call | flops 15000000512 | bytes 20000000 | tf_op jit(solution)/shard_map/ffn/pallas_call | solution.py:269
  128.0 22.2 %ffn.3 = (f32[1024,768]{1,0:T(8,128)}, f32[1024,768]{1,0:T(8,128)}, f32[1,1536]{1,0:T(1,128)S(1)}, bf16[2,2,4,4,24,768]{5,4,3,2,1,0:T(8,128)(2,1)S(1)}, bf16[2,2,4,4,24,768]{5,4,3,2,1,0:T(8,128)(2,1)}) custom-call(s32[4]{0:T(128)S(1)} %pad_add_fusion.place, bf16[1024,768]{1,0:T(8,128)(2,1)S(1)} %copy-done.8, bf16[1024,768]{1,0:T(8,128)(2,1)S(1)} %bitcast.301, ...), custom_call_target="tpu_custom_call" | custom-call | flops 15000000512 | bytes 20000000 | tf_op jit(solution)/shard_map/ffn/pallas_call | solution.py:269
  152.3 2.6 collective-permute-done.7
  157.3 12.0 %attn_backward.2 = (bf16[1024,768]{1,0:T(8,128)(2,1)}, f32[1024,768]{1,0:T(8,128)}, f32[8,1,768]{2,1,0:T(1,128)S(1)}, bf16[1024,768]{1,0:T(8,128)(2,1)S(1)}, bf1...) custom-call(bf16[1024,768]{1,0:T(8,128)(2,1)S(1)} %bitcast.298, bf16[8,1,768]{2,1,0:T(2,128)(2,1)S(1)} %copy.64.time, ...), custom_call_target="tpu_custom_call" | custom-call | flops 6000000000 | bytes 10000000 | tf_op jit(solution)/shard_map/attn_backward/pallas_call | solution.py:391
  172.2 26.3 %attn_backward.3 = (bf16[1024,768]{1,0:T(8,128)(2,1)}, f32[1024,768]{1,0:T(8,128)}, f32[8,1,768]{2,1,0:T(1,128)S(1)}, bf16[1024,768]{1,0:T(8,128)(2,1)S(1)}, bf1...) custom-call(bf16[1024,768]{1,0:T(8,128)(2,1)S(1)} %bitcast.299, ...), custom_call_target="tpu_custom_call", output_to_operand_aliasing={{0}: (12, {}), {1}: (13, {}), {2}: (14, {}), {3}: (15, {}),... | custom-call | flops 17999998976 | bytes 30000000 | tf_op jit(solution)/shard_map/attn_backward/pallas_call | solution.py:391
  198.6 2.5 fusion.2
  203.1 4.6 %weight_grad.2 = (bf16[2,2,4,24,1536]{4,3,2,1,0:T(8,128)(2,1)S(1)}, bf16[2,2,4,24,1536]{4,3,2,1,0:T(8,128)(2,1)S(1)}) custom-call(s32[4]{0:T(128)S(1)} %pad_add_fusion.place, bf16[1024,768]{1,0:T(8,128)(2,1)S(1)} %copy-done.2, bf16[1024,2304]{1,0:T(8,128)(2,1)} %get-tuple-element.99.refs_1_), custom_call_target="tpu_custom_call" | custom-call | flops 2500000000 | bytes 8000000 | tf_op jit(solution)/shard_map/weight_grad/pallas_call | solution.py:492
  207.8 4.9 %weight_grad.3 = (bf16[2,2,4,24,1664]{4,3,2,1,0:T(8,128)(2,1)S(1)}, bf16[2,2,4,24,1664]{4,3,2,1,0:T(8,128)(2,1)S(1)}) custom-call(s32[4]{0:T(128)S(1)} %pad_add_fusion.place, bf16[1024,768]{1,0:T(8,128)(2,1)S(1)} %copy-done.2, bf16[1024,2304]{1,0:T(8,128)(2,1)} %get-tuple-element.99.refs_1_, bf16[1024,768]{1,0:T(8,128)(2,1)S(1)} %copy-done.3, ...), custom_call_target="tpu_custom_call" | custom-call | flops 2500000000 | bytes 8000000 | tf_op jit(solution)/shard_map/weight_grad/pallas_call | solution.py:492
  214.5 1.9 collective-permute-start.24
  216.5 1.9 collective-permute-start.25
  220.3 6.1 %collective-permute-done.27 = bf16[4,4,24,768]{3,2,1,0:T(8,128)(2,1)S(1)} collective-permute-done((bf16[4,4,24,768]{3,2,1,0:T(8,128)(2,1)}, bf16[4,4,24,768]{3,2,1,0:T(8,128)(2,1)S(1)}, u32[]{:S(2)}, u32[]{:S(2)}) %collective-permute-start.27) | collective-permute-done | bytes 589856 | tf_op jit(solution)/shard_map/ppermute | solution.py:514
  228.5 3.5 %collective-permute-done.25 = bf16[4,24,768]{2,1,0:T(8,128)(2,1)S(1)} collective-permute-done((bf16[4,24,768]{2,1,0:T(8,128)(2,1)S(1)}, bf16[4,24,768]{2,1,0:T(8,128)(2,1)S(1)}, u32[]{:S(2)}, u32[]{:S(2)}) %collective-permute-start.25) | collective-permute-done | bytes 147488 | tf_op jit(solution)/shard_map/ppermute | solution.py:514
  234.9 2.2 collective-permute-start.20
  237.3 4.0 %collective-permute-done.29 = bf16[4,24,768]{2,1,0:T(8,128)(2,1)S(1)} collective-permute-done((bf16[4,24,768]{2,1,0:T(8,128)(2,1)S(1)}, bf16[4,24,768]{2,1,0:T(8,128)(2,1)S(1)}, u32[]{:S(2)}, u32[]{:S(2)}) %collective-permute-start.29) | collective-permute-done | bytes 147488 | tf_op jit(solution)/shard_map/ppermute | solution.py:514
  242.7 3.6 %collective-permute-start.23 = (bf16[24,1536]{1,0:T(8,128)(2,1)S(1)}, bf16[24,1536]{1,0:T(8,128)(2,1)S(1)}, u32[]{:S(2)}, u32[]{:S(2)}) collective-permute-start(bf16[24,1536]{1,0:T(8,128)(2,1)S(1)} %get-tuple-element.130), channel_id=1, source_target_pairs={{0,8},{1,9},{2,10},{3,11},{4,12},{5,13},{6,14},{7,15},{8,16},{9,17... | collective-permute-start | bytes 221192 | tf_op jit(solution)/shard_map/ppermute | solution.py:514
  250.3 2.8 %collective-permute-done.22 = bf16[24,1536]{1,0:T(8,128)(2,1)S(1)} collective-permute-done((bf16[24,1536]{1,0:T(8,128)(2,1)S(1)}, bf16[24,1536]{1,0:T(8,128)(2,1)S(1)}, u32[]{:S(2)}, u32[]{:S(2)}) %collective-permute-start.22) | collective-permute-done | bytes 73760 | tf_op jit(solution)/shard_map/ppermute | solution.py:514
  (145 shorter events, 51.8 us)
Async XLA Ops:
  7.2 97.3 %all-gather.2.cloned.1.call-start = ((), (), s32[]{:S(2)}) async-start(), calls=%async_computation | async-start | bytes 9732096 | tf_op jit(solution)/shard_map/all_gather | solution.py:646
  11.6 9.5 %collective-permute-start.2 = (bf16[24,3200]{1,0:T(8,128)(2,1)S(1)}, bf16[24,3200]{1,0:T(8,128)(2,1)S(1)}, u32[]{:S(2)}, u32[]{:S(2)}) collective-permute-start(bf16[24,3200]{1,0:T(8,128)(2,1)S(1)} %get-tuple-element.141), channel_id=1, source_target_pairs={{0,24},{1,25},{2,26},{3,27},{4,28},{5,29},{6,30},{7,31},{8,0},{9,1... | collective-permute-start | bytes 460808 | tf_op jit(solution)/shard_map/ppermute | solution.py:514
  16.7 18.1 %collective-permute-start.1 = (bf16[24,3200]{1,0:T(8,128)(2,1)S(1)}, bf16[24,3200]{1,0:T(8,128)(2,1)S(1)}, u32[]{:S(2)}, u32[]{:S(2)}) collective-permute-start(bf16[24,3200]{1,0:T(8,128)(2,1)S(1)} %get-tuple-element.141), channel_id=1, source_target_pairs={{0,16},{1,17},{2,18},{3,19},{4,20},{5,21},{6,22},{7,23},{8,24},{9,... | collective-permute-start | bytes 460808 | tf_op jit(solution)/shard_map/ppermute | solution.py:514
  16.7 18.1 %collective-permute-start = (bf16[24,3200]{1,0:T(8,128)(2,1)S(1)}, bf16[24,3200]{1,0:T(8,128)(2,1)S(1)}, u32[]{:S(2)}, u32[]{:S(2)}) collective-permute-start(bf16[24,3200]{1,0:T(8,128)(2,1)S(1)} %get-tuple-element.141), channel_id=1, source_target_pairs={{0,8},{1,9},{2,10},{3,11},{4,12},{5,13},{6,14},{7,15},{8,16},{9,17... | collective-permute-start | bytes 460808 | tf_op jit(solution)/shard_map/ppermute | solution.py:514
  35.0 11.7 %collective-permute-start.3 = (bf16[4,24,3200]{2,1,0:T(8,128)(2,1)S(1)}, bf16[4,24,3200]{2,1,0:T(8,128)(2,1)S(1)}, u32[]{:S(2)}, u32[]{:S(2)}) collective-permute-start(bf16[4,24,3200]{2,1,0:T(8,128)(2,1)S(1)} %get-tuple-element.133), channel_id=1, source_target_pairs={{0,2},{1,5},{2,0},{3,7},{4,6},{5,1},{6,4},{7,3},{8,10},{9,13},{10,... | collective-permute-start | bytes 1843208 | tf_op jit(solution)/shard_map/ppermute | solution.py:514
  46.8 16.8 %collective-permute-start.4 = (bf16[2,4,24,3200]{3,2,1,0:T(8,128)(2,1)S(1)}, bf16[2,4,24,3200]{3,2,1,0:T(8,128)(2,1)S(1)}, u32[]{:S(2)}, u32[]{:S(2)}) collective-permute-start(bf16[2,4,24,3200]{3,2,1,0:T(8,128)(2,1)S(1)} %pad_maximum_fusion.mine0), channel_id=1, source_target_pairs={{0,4},{1,3},{2,6},{3,1},{4,0},{5,7},{6,2},{7,5},{8,12},{9,11},{10,... | collective-permute-start | bytes 3686408 | tf_op jit(solution)/shard_map/ppermute | solution.py:514
  47.5 20.7 %collective-permute-start.5 = (bf16[2,4,24,3200]{3,2,1,0:T(8,128)(2,1)S(1)}, bf16[2,4,24,3200]{3,2,1,0:T(8,128)(2,1)}, u32[]{:S(2)}, u32[]{:S(2)}) collective-permute-start(bf16[2,4,24,3200]{3,2,1,0:T(8,128)(2,1)S(1)} %pad_maximum_fusion.mine0), channel_id=1, source_target_pairs={{0,1},{1,0},{2,3},{3,2},{4,5},{5,4},{6,7},{7,6},{8,9},{9,8},{10,11... | collective-permute-start | bytes 3686408 | tf_op jit(solution)/shard_map/ppermute | solution.py:514
  127.7 22.8 %collective-permute-start.8 = (bf16[2,2,4,4,24,768]{5,4,3,2,1,0:T(8,128)(2,1)}, bf16[2,2,4,4,24,768]{5,4,3,2,1,0:T(8,128)(2,1)S(1)}, u32[]{:S(2)}, u32[]{:S(2)}) collective-permute-start(bf16[2,2,4,4,24,768]{5,4,3,2,1,0:T(8,128)(2,1)} %get-tuple-element.75), channel_id=1, source_target_pairs={{0,1},{1,0},{2,3},{3,2},{4,5},{5,4},{6,7},{7,6},{8,9},{9,8},{10,11... | collective-permute-start | bytes 7077896 | tf_op jit(solution)/shard_map/ppermute | solution.py:514
  150.8 18.5 %collective-permute-start.9 = (bf16[2,4,4,24,768]{4,3,2,1,0:T(8,128)(2,1)S(1)}, bf16[2,4,4,24,768]{4,3,2,1,0:T(8,128)(2,1)}, u32[]{:S(2)}, u32[]{:S(2)}) collective-permute-start(bf16[2,4,4,24,768]{4,3,2,1,0:T(8,128)(2,1)S(1)} %fusion.1), channel_id=1, source_target_pairs={{0,4},{1,3},{2,6},{3,1},{4,0},{5,7},{6,2},{7,5},{8,12},{9,11},{10,... | collective-permute-start | bytes 3538952 | tf_op jit(solution)/shard_map/ppermute | solution.py:514
  155.3 43.2 %collective-permute-start.10 = (bf16[2,4,4,24,768]{4,3,2,1,0:T(8,128)(2,1)S(1)}, bf16[2,4,4,24,768]{4,3,2,1,0:T(8,128)(2,1)}, u32[]{:S(2)}, u32[]{:S(2)}) collective-permute-start(bf16[2,4,4,24,768]{4,3,2,1,0:T(8,128)(2,1)S(1)} %fusion), channel_id=1, source_target_pairs={{0,4},{1,3},{2,6},{3,1},{4,0},{5,7},{6,2},{7,5},{8,12},{9,11},{10,... | collective-permute-start | bytes 3538952 | tf_op jit(solution)/shard_map/ppermute | solution.py:514
  170.8 30.4 %collective-permute-start.11 = (bf16[4,4,24,768]{3,2,1,0:T(8,128)(2,1)S(1)}, bf16[4,4,24,768]{3,2,1,0:T(8,128)(2,1)S(1)}, u32[]{:S(2)}, u32[]{:S(2)}) collective-permute-start(bf16[4,4,24,768]{3,2,1,0:T(8,128)(2,1)S(1)} %fusion.3), channel_id=1, source_target_pairs={{0,2},{1,5},{2,0},{3,7},{4,6},{5,1},{6,4},{7,3},{8,10},{9,13},{10,... | collective-permute-start | bytes 1769480 | tf_op jit(solution)/shard_map/ppermute | solution.py:514
  207.7 8.8 %collective-permute-start.18 = (bf16[2,2,4,24,1536]{4,3,2,1,0:T(8,128)(2,1)S(1)}, bf16[2,2,4,24,1536]{4,3,2,1,0:T(8,128)(2,1)S(1)}, u32[]{:S(2)}, u32[]{:S(2)}) collective-permute-start(bf16[2,2,4,24,1536]{4,3,2,1,0:T(8,128)(2,1)S(1)} %get-tuple-element.111), channel_id=1, source_target_pairs={{0,1},{1,0},{2,3},{3,2},{4,5},{5,4},{6,7},{7,6},{8,9},{9,8},{10,11... | collective-permute-start | bytes 3538952 | tf_op jit(solution)/shard_map/ppermute | solution.py:514
  213.3 13.2 %collective-permute-start.27 = (bf16[4,4,24,768]{3,2,1,0:T(8,128)(2,1)}, bf16[4,4,24,768]{3,2,1,0:T(8,128)(2,1)S(1)}, u32[]{:S(2)}, u32[]{:S(2)}) collective-permute-start(bf16[4,4,24,768]{3,2,1,0:T(8,128)(2,1)} %fusion.2), channel_id=1, source_target_pairs={{0,2},{1,5},{2,0},{3,7},{4,6},{5,1},{6,4},{7,3},{8,10},{9,13},{10,... | collective-permute-start | bytes 1769480 | tf_op jit(solution)/shard_map/ppermute | solution.py:514
  214.5 17.5 %collective-permute-start.24 = (bf16[4,24,768]{2,1,0:T(8,128)(2,1)S(1)}, bf16[4,24,768]{2,1,0:T(8,128)(2,1)S(1)}, u32[]{:S(2)}, u32[]{:S(2)}) collective-permute-start(bf16[4,24,768]{2,1,0:T(8,128)(2,1)S(1)} %get-tuple-element.122), channel_id=1, source_target_pairs={{0,24},{1,25},{2,26},{3,27},{4,28},{5,29},{6,30},{7,31},{8,0},{9,1... | collective-permute-start | bytes 442376 | tf_op jit(solution)/shard_map/ppermute | solution.py:514
  216.4 11.5 %collective-permute-start.26 = (bf16[4,24,768]{2,1,0:T(8,128)(2,1)S(1)}, bf16[4,24,768]{2,1,0:T(8,128)(2,1)S(1)}, u32[]{:S(2)}, u32[]{:S(2)}) collective-permute-start(bf16[4,24,768]{2,1,0:T(8,128)(2,1)S(1)} %get-tuple-element.121), channel_id=1, source_target_pairs={{0,8},{1,9},{2,10},{3,11},{4,12},{5,13},{6,14},{7,15},{8,16},{9,17... | collective-permute-start | bytes 442376 | tf_op jit(solution)/shard_map/ppermute | solution.py:514
  216.5 15.5 %collective-permute-start.25 = (bf16[4,24,768]{2,1,0:T(8,128)(2,1)S(1)}, bf16[4,24,768]{2,1,0:T(8,128)(2,1)S(1)}, u32[]{:S(2)}, u32[]{:S(2)}) collective-permute-start(bf16[4,24,768]{2,1,0:T(8,128)(2,1)S(1)} %get-tuple-element.120), channel_id=1, source_target_pairs={{0,16},{1,17},{2,18},{3,19},{4,20},{5,21},{6,22},{7,23},{8,24},{9,... | collective-permute-start | bytes 442376 | tf_op jit(solution)/shard_map/ppermute | solution.py:514
  218.6 16.1 %collective-permute-start.19 = (bf16[2,4,24,1536]{3,2,1,0:T(8,128)(2,1)S(1)}, bf16[2,4,24,1536]{3,2,1,0:T(8,128)(2,1)S(1)}, u32[]{:S(2)}, u32[]{:S(2)}) collective-permute-start(bf16[2,4,24,1536]{3,2,1,0:T(8,128)(2,1)S(1)} %fusion.6), channel_id=1, source_target_pairs={{0,4},{1,3},{2,6},{3,1},{4,0},{5,7},{6,2},{7,5},{8,12},{9,11},{10,... | collective-permute-start | bytes 1769480 | tf_op jit(solution)/shard_map/ppermute | solution.py:514
  226.4 10.7 %collective-permute-start.13 = (bf16[2,4,24,1664]{3,2,1,0:T(8,128)(2,1)S(1)}, bf16[2,4,24,1664]{3,2,1,0:T(8,128)(2,1)S(1)}, u32[]{:S(2)}, u32[]{:S(2)}) collective-permute-start(bf16[2,4,24,1664]{3,2,1,0:T(8,128)(2,1)S(1)} %fusion.4), channel_id=1, source_target_pairs={{0,4},{1,3},{2,6},{3,1},{4,0},{5,7},{6,2},{7,5},{8,12},{9,11},{10,... | collective-permute-start | bytes 1916936 | tf_op jit(solution)/shard_map/ppermute | solution.py:514
  227.9 9.4 %collective-permute-start.30 = (bf16[4,24,768]{2,1,0:T(8,128)(2,1)S(1)}, bf16[4,24,768]{2,1,0:T(8,128)(2,1)S(1)}, u32[]{:S(2)}, u32[]{:S(2)}) collective-permute-start(bf16[4,24,768]{2,1,0:T(8,128)(2,1)S(1)} %get-tuple-element.124), channel_id=1, source_target_pairs={{0,8},{1,9},{2,10},{3,11},{4,12},{5,13},{6,14},{7,15},{8,16},{9,17... | collective-permute-start | bytes 442376 | tf_op jit(solution)/shard_map/ppermute | solution.py:514
  232.0 9.4 %collective-permute-start.29 = (bf16[4,24,768]{2,1,0:T(8,128)(2,1)S(1)}, bf16[4,24,768]{2,1,0:T(8,128)(2,1)S(1)}, u32[]{:S(2)}, u32[]{:S(2)}) collective-permute-start(bf16[4,24,768]{2,1,0:T(8,128)(2,1)S(1)} %get-tuple-element.125), channel_id=1, source_target_pairs={{0,16},{1,17},{2,18},{3,19},{4,20},{5,21},{6,22},{7,23},{8,24},{9,... | collective-permute-start | bytes 442376 | tf_op jit(solution)/shard_map/ppermute | solution.py:514
  232.0 9.4 %collective-permute-start.28 = (bf16[4,24,768]{2,1,0:T(8,128)(2,1)S(1)}, bf16[4,24,768]{2,1,0:T(8,128)(2,1)S(1)}, u32[]{:S(2)}, u32[]{:S(2)}) collective-permute-start(bf16[4,24,768]{2,1,0:T(8,128)(2,1)S(1)} %get-tuple-element.123), channel_id=1, source_target_pairs={{0,24},{1,25},{2,26},{3,27},{4,28},{5,29},{6,30},{7,31},{8,0},{9,1... | collective-permute-start | bytes 442376 | tf_op jit(solution)/shard_map/ppermute | solution.py:514
  237.2 17.1 %collective-permute-start.14 = (bf16[4,24,1664]{2,1,0:T(8,128)(2,1)S(1)}, bf16[4,24,1664]{2,1,0:T(8,128)(2,1)S(1)}, u32[]{:S(2)}, u32[]{:S(2)}) collective-permute-start(bf16[4,24,1664]{2,1,0:T(8,128)(2,1)S(1)} %fusion.5), channel_id=1, source_target_pairs={{0,2},{1,5},{2,0},{3,7},{4,6},{5,1},{6,4},{7,3},{8,10},{9,13},{10,... | collective-permute-start | bytes 958472 | tf_op jit(solution)/shard_map/ppermute | solution.py:514
  255.2 7.8 %collective-permute-start.17 = (bf16[24,1664]{1,0:T(8,128)(2,1)}, bf16[24,1664]{1,0:T(8,128)(2,1)}, u32[]{:S(2)}, u32[]{:S(2)}) collective-permute-start(bf16[24,1664]{1,0:T(8,128)(2,1)} %get-tuple-element.127), channel_id=1, source_target_pairs={{0,8},{1,9},{2,10},{3,11},{4,12},{5,13},{6,14},{7,15},{8,16},{9,17... | collective-permute-start | bytes 239624 | tf_op jit(solution)/shard_map/ppermute | solution.py:514
  256.7 7.8 %collective-permute-start.16 = (bf16[24,1664]{1,0:T(8,128)(2,1)}, bf16[24,1664]{1,0:T(8,128)(2,1)}, u32[]{:S(2)}, u32[]{:S(2)}) collective-permute-start(bf16[24,1664]{1,0:T(8,128)(2,1)} %get-tuple-element.128), channel_id=1, source_target_pairs={{0,16},{1,17},{2,18},{3,19},{4,20},{5,21},{6,22},{7,23},{8,24},{9,... | collective-permute-start | bytes 239624 | tf_op jit(solution)/shard_map/ppermute | solution.py:514
  (35 other events, 266.7 us)
Sparse Core Ops, SparseCore 0:
  11.5 92.8 all-gather.1

commit v3 on v2

--- a/solution.py
+++ b/solution.py
@@ -72,11 +72,11 @@
     send[(second, first, deep) + tail] = jnp.where(mine, odd, even)
 
 
-def pick(place, parts, z, y, x):
+def pick(place, parts, z, y, x, tail=()):
     mine0, mine1, other0, other1 = parts
     first, second, deep = slots(place, z, y, x)
-    mine = jnp.where(first == 0, mine0[second, deep], mine1[second, deep])
-    other = jnp.where(second == 0, other0[first, deep], other1[first, deep])
+    mine = jnp.where(first == 0, mine0[(second, deep) + tail], mine1[(second, deep) + tail])
+    other = jnp.where(second == 0, other0[(first, deep) + tail], other1[(first, deep) + tail])
     even = place[3] == 0
     return jnp.where(even, mine, other), jnp.where(even, other, mine)
 
@@ -145,15 +145,15 @@
             q = qkv[sl, c : c + 2 * HD] * jnp.asarray(HD**-0.5, BF16)
             k = head_pair(qkv[sl, width + c : width + c + 2 * HD])
             v = head_pair(qkv[sl, 2 * width + c : 2 * width + c + 2 * HD])
-            s = dot(q, k, 1, 1)
+            s = dot(k, q, 1, 1)
             halves = []
             for h in range(2):
-                sh = s[:, h * size : (h + 1) * size] + mask
-                e = jnp.exp(sh - jnp.max(sh, axis=-1, keepdims=True))
-                halves.append((e / jnp.sum(e, axis=-1, keepdims=True)).astype(BF16))
-            pr = jnp.concatenate(halves, axis=1)
+                sh = s[h * size : (h + 1) * size] + mask
+                e = jnp.exp(sh - jnp.max(sh, axis=0, keepdims=True))
+                halves.append((e * (1.0 / jnp.sum(e, axis=0, keepdims=True))).astype(BF16))
+            pr = jnp.concatenate(halves, axis=0)
             probs[r, p] = pr
-            att[sl, c : c + 2 * HD] = dot(pr, v, 1, 0).astype(BF16)
+            att[sl, c : c + 2 * HD] = dot(pr, v, 0, 0).astype(BF16)
     hidden = x + dot(att[...], weights[:, 3 * width : 4 * width], 1, 0) + vec[4:5, :]
     hid[...] = hidden
     nhat2, _ = normalise(hidden)
@@ -182,7 +182,7 @@
         out_specs=[
             tile(width),
             tile(3 * width),
-            pl.BlockSpec((rows, pairs, size, 2 * size), lambda i: (i, 0, 0, 0)),
+            pl.BlockSpec((rows, pairs, 2 * size, size), lambda i: (i, 0, 0, 0)),
             tile(width),
             tile(width),
             tile(width),
@@ -193,7 +193,7 @@
         out_shape=[
             jax.ShapeDtypeStruct((toks, width), BF16),
             jax.ShapeDtypeStruct((toks, 3 * width), BF16),
-            jax.ShapeDtypeStruct((row_count, pairs, size, 2 * size), BF16),
+            jax.ShapeDtypeStruct((row_count, pairs, 2 * size, size), BF16),
             jax.ShapeDtypeStruct((toks, width), BF16),
             jax.ShapeDtypeStruct((toks, width), F32),
             jax.ShapeDtypeStruct((toks, width), BF16),
@@ -207,7 +207,9 @@
     )(place, tok, time, seg, *gathered)
 
 
-def ffn_body(place, n2, cot, fc, out, bfc, acc_out, acc_dn2, dbfc, keep, send, fc_s, out_s, act_s, dpre_s, *, tm, sub, half):
+def ffn_body(
+    place, n2, cot, mine0, mine1, other0, other1, bfc, sum_out, sum_dn2, dbfc, keep, send, acc_out, acc_dn2, fc_s, out_s, act_s, dpre_s, *, tm, sub, half
+):
     step = pl.program_id(0)
 
     @pl.when(step == 0)
@@ -215,8 +217,20 @@
         acc_out[...] = jnp.zeros_like(acc_out)
         acc_dn2[...] = jnp.zeros_like(acc_dn2)
 
-    fc_s[...] = merge_rows(fc[:, 0])
-    out_s[...] = merge_rows(out[...].reshape((-1,) + out.shape[2:]))
+    gathered = (mine0, mine1, other0, other1)
+    blocks, rows = 2, mine0.shape[-2]
+    for z in range(Z):
+        for y in range(Y):
+            for x in range(X):
+                both = pick(place, gathered, z, y, x, (step,))
+                at = ((z * Y + y) * X + x) * CORES * rows
+                fc_s[at : at + CORES * rows, :] = merge_rows(jnp.stack(both))
+    for z in range(Z // blocks):
+        for y in range(Y):
+            for x in range(X):
+                both = pick(place, gathered, step * (Z // blocks) + z, y, x, (slice(blocks, 2 * blocks),))
+                at = ((z * Y + y) * X + x) * CORES * blocks * rows
+                out_s[at : at + CORES * blocks * rows, :] = merge_rows(jnp.concatenate(both, axis=0))
     chunk = fc_s.shape[1]
     for part in range(chunk // sub):
         cols = slice(part * sub, (part + 1) * sub)
@@ -236,9 +250,14 @@
             acc_out[sl, :] += dot(act, out_s[cols, :], 1, 0)
             acc_dn2[sl, :] += dot(d_pre, fc_s[:, cols], 1, 1)
         dbfc[:, cols] = db
+
+    @pl.when(step == pl.num_programs(0) - 1)
+    def _():
+        sum_out[...] = acc_out[...].astype(BF16)
+        sum_dn2[...] = acc_dn2[...].astype(BF16)
+
     grad = dot(act_s[...], cot[...], 0, 0)
-    blocks, rows = out.shape[1:3]
-    planes = out.shape[0] // (Y * X * CORES)
+    planes = Z // blocks
     for z in range(planes):
         for y in range(Y):
             for x in range(X):
@@ -257,9 +276,9 @@
                 put_blocks(place, z, y, x, even, odd, keep, send, (step,))
 
 
-def ffn(place, n2, cot, gathered, bfc, half, tm=512, sub=256):
+def ffn(place, n2, cot, gathered, bfc, half, tm=512, sub=768):
     toks, width = n2.shape
-    pieces, _, rows, _ = gathered.shape
+    rows = width // PIECES
     blocks = 2
     count = 2 * blocks
     once = pl.Buffered(buffer_count=1)
@@ -273,8 +292,9 @@
             pl.BlockSpec(memory_space=pltpu.SMEM),
             full((toks, width)),
             full((toks, width)),
-            pl.BlockSpec((pieces, 1, rows, width), lambda j: (0, count * half + j, 0, 0)),
-            pl.BlockSpec((pieces // blocks, blocks, rows, width), lambda j: (j, 2 * half + 1, 0, 0)),
+        ]
+        + [full(g.shape) for g in gathered]
+        + [
             pl.BlockSpec((2, width), lambda j: (0, j)),
         ],
         out_specs=[
@@ -285,13 +305,15 @@
             whole(parted),
         ],
         out_shape=[
-            jax.ShapeDtypeStruct((toks, width), F32),
-            jax.ShapeDtypeStruct((toks, width), F32),
+            jax.ShapeDtypeStruct((toks, width), BF16),
+            jax.ShapeDtypeStruct((toks, width), BF16),
             jax.ShapeDtypeStruct((1, blocks * width), F32),
             jax.ShapeDtypeStruct(parted, BF16),
             jax.ShapeDtypeStruct(parted, BF16),
         ],
         scratch_shapes=[
+            pltpu.VMEM((toks, width), F32),
+            pltpu.VMEM((toks, width), F32),
             pltpu.VMEM((width, width), BF16),
             pltpu.VMEM((width, width), BF16),
             pltpu.VMEM((toks, width), BF16),
@@ -300,7 +322,7 @@
         compiler_params=pltpu.CompilerParams(vmem_limit_bytes=VMEM_LIMIT),
         cost_estimate=pl.CostEstimate(flops=15 * 10**9, bytes_accessed=20 * 10**6, transcendentals=3 * 10**6),
         name="ffn",
-    )(place, n2, cot, gathered, gathered, bfc)
+    )(place, n2, cot, *gathered, bfc)
 
 
 def attn_backward_body(
@@ -315,9 +337,9 @@
         sums[...] = jnp.zeros_like(sums)
 
     hidden = hid[...]
-    layer_out[...] = (hidden + (out0[...] + out1[...]) + vec[7:8, :]).astype(BF16)
+    layer_out[...] = (hidden + (out0[...].astype(F32) + out1[...].astype(F32)) + vec[7:8, :]).astype(BF16)
     nhat, inv = normalise(hidden)
-    dn2 = dn20[...] + dn21[...]
+    dn2 = dn20[...].astype(F32) + dn21[...].astype(F32)
     cotangent = cot[...].astype(F32)
     q = dn2 * vec[5:6, :]
     mean_q = jnp.mean(q, axis=-1, keepdims=True)
@@ -341,21 +363,16 @@
             v = head_pair(qkv[sl, 2 * width + c : 2 * width + c + 2 * HD])
             dm = d_mixed[sl, c : c + 2 * HD]
             pr = probs[r, p]
-            dp = dot(dm, v, 1, 1)
-            pf = pr.astype(F32)
-            prod = dp * pf
-            ds = jnp.concatenate(
-                [
-                    prod[:, h * size : (h + 1) * size]
-                    - pf[:, h * size : (h + 1) * size]
-                    * jnp.sum(prod[:, h * size : (h + 1) * size], axis=-1, keepdims=True)
-                    for h in range(2)
-                ],
-                axis=1,
-            ).astype(BF16)
-            dv = own_lanes(dot(pr, dm, 0, 0))
-            dk = own_lanes(dot(ds, qb, 0, 0))
-            dq = dot(ds, k, 1, 0) * HD**-0.5
+            dp = dot(v, dm, 1, 1)
+            halves = []
+            for h in range(2):
+                pf = pr[h * size : (h + 1) * size].astype(F32)
+                dph = dp[h * size : (h + 1) * size]
+                halves.append((pf * (dph - jnp.sum(dph * pf, axis=0, keepdims=True))).astype(BF16))
+            ds = jnp.concatenate(halves, axis=0)
+            dv = own_lanes(dot(pr, dm, 1, 0))
+            dk = own_lanes(dot(ds, qb, 1, 0))
+            dq = dot(ds, k, 0, 0) * HD**-0.5
             dqkv[sl, c : c + 2 * HD] = dq.astype(BF16)
             dqkv[sl, width + c : width + c + 2 * HD] = dk.astype(BF16)
             dqkv[sl, 2 * width + c : 2 * width + c + 2 * HD] = dv.astype(BF16)
@@ -380,7 +397,7 @@
 
 
 def attn_backward(tok, time, hid, outs, dn2s, cot, qkv, probs, weights, vec, base, steps, before=(), rows=2):
-    row_count, pairs, size, _ = probs.shape
+    row_count, pairs, _, size = probs.shape
     width = hid.shape[1]
     tm = rows * size
     toks = row_count * size
@@ -395,7 +412,7 @@
         + [tile(width)] * 6
         + [
             tile(3 * width),
-            pl.BlockSpec((rows, pairs, size, 2 * size), lambda i: (i + base, 0, 0, 0)),
+            pl.BlockSpec((rows, pairs, 2 * size, size), lambda i: (i + base, 0, 0, 0)),
             full(weights.shape),
             full(vec.shape),
         ]
@@ -435,13 +452,13 @@
     return jnp.where(lane < cut, block, 0.0)
 
 
-def weight_grad_body(place, *refs, columns, with_vectors):
-    keep, send = refs[-2:]
-    rows = keep.shape[3]
-    width = refs[0].shape[1]
+def weight_grad_body(place, n1, dqkv, att, dbr, sums0, sums1, dbfc0, dbfc1, keep0, send0, keep1, send1):
+    rows = keep0.shape[3]
+    width = n1.shape[1]
     step = pl.program_id(0)
 
-    def emit(grad, tail):
+    def emit(grad, keep, send, at_column):
+        tail = (slice(None), slice(at_column, at_column + grad.shape[1]))
         for z in range(Z):
             for y in range(Y):
                 for x in range(X):
@@ -450,60 +467,59 @@
                     odd = grad[at + rows : at + 2 * rows].astype(BF16)
                     put_blocks(place, z, y, x, even, odd, keep, send, tail)
 
-    for k in range(columns):
+    for k in range(2):
 
         @pl.when(step == k)
         def _(k=k):
-            emit(dot(refs[0][...], refs[1][...], 0, 0), (slice(None), slice(k * width, (k + 1) * width)))
-
-    if with_vectors:
-
-        @pl.when(step == columns)
-        def _():
-            att, dbr, sums0, sums1, dbfc0, dbfc1 = refs[2:8]
-            emit(dot(att[...], dbr[...], 0, 0), (slice(None), slice(columns * width, (columns + 1) * width)))
-            vectors = sums0[...] + sums1[...]
-            pad = jnp.zeros((6, dbfc0.shape[1]), F32)
-            hidden = jnp.concatenate([dbfc0[...], dbfc1[...], pad], axis=0)
-
-            def block(piece):
-                early = collect(hidden, rows, 2 * rows, 0, piece)
-                late = collect(hidden, rows, 2 * rows, rows, piece)
-                top = collect(vectors, rows, rows, 0, piece)
-                rest = [early[:2], late[:2], jnp.zeros((rows - 12, 128), F32)]
-                return jnp.concatenate([top] + rest, axis=0).astype(BF16)
-
-            for z in range(Z):
-                for y in range(Y):
-                    for x in range(X):
-                        piece = ((z * Y + y) * X + x) * CORES
-                        tail = (slice(None), slice((columns + 1) * width, (columns + 1) * width + 128))
-                        put_blocks(place, z, y, x, block(piece), block(piece + 1), keep, send, tail)
-
-
-def weight_grad(place, n1, dqkv, first, columns, extra=()):
+            emit(dot(n1[...], dqkv[...], 0, 0), keep0, send0, k * width)
+
+    @pl.when(step == 2)
+    def _():
+        emit(dot(n1[...], dqkv[...], 0, 0), keep1, send1, 0)
+
+    @pl.when(step == 3)
+    def _():
+        emit(dot(att[...], dbr[...], 0, 0), keep1, send1, width)
+        vectors = sums0[...] + sums1[...]
+        pad = jnp.zeros((6, dbfc0.shape[1]), F32)
+        hidden = jnp.concatenate([dbfc0[...], dbfc1[...], pad], axis=0)
+
+        def block(piece):
+            early = collect(hidden, rows, 2 * rows, 0, piece)
+            late = collect(hidden, rows, 2 * rows, rows, piece)
+            top = collect(vectors, rows, rows, 0, piece)
+            rest = [early[:2], late[:2], jnp.zeros((rows - 12, 128), F32)]
+            return jnp.concatenate([top] + rest, axis=0).astype(BF16)
+
+        tail = (slice(None), slice(2 * width, 2 * width + 128))
+        for z in range(Z):
+            for y in range(Y):
+                for x in range(X):
+                    piece = ((z * Y + y) * X + x) * CORES
+                    put_blocks(place, z, y, x, block(piece), block(piece + 1), keep1, send1, tail)
+
+
+def weight_grad(place, n1, dqkv, att, dbr, sums0, sums1, dbfc0, dbfc1):
     toks, width = n1.shape
     rows = width // PIECES
     once = pl.Buffered(buffer_count=1)
     full = lambda a: pl.BlockSpec(a.shape, lambda j: (0, 0), pipeline_mode=once)
-    parted = (Y, X, Z, rows, columns * width + (width + 128 if extra else 0))
-    whole = pl.BlockSpec(parted, lambda j: (0,) * 5)
-    shape = jax.ShapeDtypeStruct(parted, BF16)
+    shapes = [(Y, X, Z, rows, columns) for columns in (2 * width, 2 * width + 128) for _ in range(2)]
     return pl.pallas_call(
-        functools.partial(weight_grad_body, columns=columns, with_vectors=bool(extra)),
-        grid=(columns + bool(extra),),
+        weight_grad_body,
+        grid=(4,),
         in_specs=[
             pl.BlockSpec(memory_space=pltpu.SMEM),
             full(n1),
-            pl.BlockSpec((toks, width), lambda j: (0, first + jnp.minimum(j, columns - 1))),
+            pl.BlockSpec((toks, width), lambda j: (0, jnp.minimum(j, 2))),
         ]
-        + [full(e) for e in extra],
-        out_specs=[whole, whole],
-        out_shape=[shape, shape],
+        + [full(e) for e in (att, dbr, sums0, sums1, dbfc0, dbfc1)],
+        out_specs=[pl.BlockSpec(shape, lambda j: (0,) * 5) for shape in shapes],
+        out_shape=[jax.ShapeDtypeStruct(shape, BF16) for shape in shapes],
         compiler_params=pltpu.CompilerParams(vmem_limit_bytes=VMEM_LIMIT),
-        cost_estimate=pl.CostEstimate(flops=25 * 10**8, bytes_accessed=8 * 10**6, transcendentals=0),
+        cost_estimate=pl.CostEstimate(flops=5 * 10**9, bytes_accessed=16 * 10**6, transcendentals=0),
         name="weight_grad",
-    )(place, n1, dqkv, *extra)
+    )(place, n1, dqkv, att, dbr, sums0, sums1, dbfc0, dbfc1)
 
 
 def flip(position):
@@ -524,19 +540,29 @@
 
 class CubeGather:
     def __init__(self, block):
-        self.ready, self.step, self.mine, self.parts = block, 0, None, None
+        self.ready, self.came, self.step, self.parts = block, None, 0, None
 
     def send(self):
         if self.step == 0:
-            ring = [exchange(self.ready, lambda i, k=k: (i + 8 * k) % PIECES) for k in range(1, Z)]
-            self.ready = jnp.stack([self.ready] + ring)
+            self.came = [exchange(self.ready, lambda i, k=k: (i + 8 * k) % PIECES) for k in range(1, Z)]
         elif self.step == 1:
-            self.ready = jnp.stack([self.ready, exchange(self.ready, plane_partner("second"))])
+            self.came = [exchange(self.ready, plane_partner("second"))]
         elif self.step == 2:
-            self.ready = (self.ready, exchange(self.ready, plane_partner("first")))
+            self.came = [exchange(self.ready, plane_partner("first"))]
+        self.step += 1
+
+    def take(self):
+        if self.step < 3:
+            self.ready = jnp.stack([self.ready] + list(self.came))
         else:
-            self.parts = self.ready + tuple(exchange(half, flip(1)) for half in self.ready)
-        self.step += 1
+            self.parts = (self.ready, self.came[0])
+
+    def share(self):
+        self.parts = self.parts + tuple(exchange(half, flip(1)) for half in self.parts)
+
+
+def meet(*things):
+    return lax.optimization_barrier(things)
 
 
 class CubeSum:
@@ -581,11 +607,12 @@
     return values
 
 
-def cut_any(every):
-    every = every.reshape((Z, Y, X, CORES, every.shape[0] // PIECES) + every.shape[1:])
+def cut_any(blocks):
+    every = blocks.reshape((Z, Y, X, CORES) + blocks.shape[1:])
     deep = jnp.array([0, 3, 2, 1])
-    even = jnp.transpose(every[:, :, :, 0], (1, 2, 0, 3, 4))[:, :, deep]
-    odd = jnp.transpose(every[:, :, :, 1], (2, 1, 0, 3, 4))[:, :, deep]
+    rest = tuple(range(3, every.ndim - 1))
+    even = jnp.transpose(every[:, :, :, 0], (1, 2, 0) + rest)[:, :, deep]
+    odd = jnp.transpose(every[:, :, :, 1], (2, 1, 0) + rest)[:, :, deep]
     return even[0], even[1], odd[0], odd[1]
 
 
@@ -643,11 +670,27 @@
         ffn_block = jnp.concatenate(
             [ffn_fc(w_fc).transpose(0, 2, 1, 3), w_out.reshape(halves, blocks, own, width)], axis=1
         )
-        ffn_full = lax.all_gather(ffn_block.reshape(-1, own, width), "dp", axis=0)
         small = jnp.pad(small, ((0, own - small.shape[0]), (0, 128 - own)))
         attn_gather = CubeGather(jnp.concatenate([w_qkv, w_proj, small], axis=1))
-        for _ in range(4):
-            attn_gather.send()
+        early, late = CubeGather(ffn_block[0]), CubeGather(ffn_block[1])
+        attn_gather.send()
+        early.send()
+        attn_gather.came, late.ready = meet(attn_gather.came, late.ready)
+        attn_gather.take()
+        attn_gather.send()
+        late.send()
+        attn_gather.came, early.came = meet(attn_gather.came, early.came)
+        attn_gather.take()
+        early.take()
+        attn_gather.send()
+        early.send()
+        attn_gather.came, early.came, late.came = meet(attn_gather.came, early.came, late.came)
+        attn_gather.take()
+        attn_gather.share()
+        early.take()
+        late.take()
+        early.send()
+        late.send()
         attn_full = attn_gather.parts
     else:
         whole = lambda w: lax.all_gather(w, "dp", axis=0, tiled=True)
@@ -658,60 +701,77 @@
             [vectors.reshape(8, PIECES, cut).transpose(1, 0, 2), hidden_bias[:, jnp.array([0, 2, 1, 3])]], axis=1
         )
         small = jnp.pad(small, ((0, 0), (0, cut - small.shape[1]), (0, 128 - cut))).reshape(width, 128)
-        attn_full = cut_any(jnp.concatenate([whole(w_qkv), whole(w_proj), small], axis=1))
+        attn_full = jnp.concatenate([whole(w_qkv), whole(w_proj), small], axis=1)
+        attn_full = cut_any(attn_full.reshape(PIECES, cut, -1))
         fc_full = ffn_fc(whole(w_fc)).reshape(halves, PIECES, cut, blocks, width).transpose(1, 0, 3, 2, 4)
         out_full = whole(w_out).reshape(PIECES, halves, blocks, cut, width)
-        ffn_full = jnp.concatenate([fc_full, out_full], axis=2).reshape(PIECES, -1, cut, width)
+        ffn_full = jnp.concatenate([fc_full, out_full], axis=2)
+        early, late = [cut_any(ffn_full[:, h].reshape(PIECES, -1, cut, width)) for h in range(halves)]
 
     flat = tokens.reshape(toks, width)
     times = time_embed.reshape(row_count, 1, width)
     segments = segment_ids.reshape(row_count, 1, row_len)
     cot = cotangent.reshape(toks, width)
+    if cube:
+        (segments,) = hold(late.ready, *hold(early.ready, segments))
     n1, qkv, probs, att, hid, n2, attn_w, vec, bfc = attn_forward(place, flat, times, segments, attn_full)
-
-    out0, dn20, dbfc0, *grads0 = ffn(place, n2, cot, ffn_full, bfc, 0)
+    if cube:
+        n2, early.came, late.came = meet(n2, early.came, late.came)
+        early.take()
+        early.share()
+        late.take()
+        late.send()
+        (n2,) = hold(late.ready, n2)
+        early = early.parts
+    out0, dn20, dbfc0, *grads0 = ffn(place, n2, cot, early, bfc, 0)
     sum0 = CubeSum(*grads0)
     if cube:
+        out0, late.came, sum0.ahead = meet(out0, late.came, sum0.ahead)
+        late.take()
+        late.share()
         sum0.send()
-    bfc, out0 = lax.optimization_barrier((bfc, out0))
-    out1, dn21, dbfc1, *grads1 = ffn(place, n2, cot, ffn_full, bfc, 1)
+        sum0.send()
+        (n2,) = hold(sum0.ahead, n2)
+        late = late.parts
+    out1, dn21, dbfc1, *grads1 = ffn(place, n2, cot, late, bfc, 1)
     sum1 = CubeSum(*grads1)
     backward = lambda hid, base, steps, before: attn_backward(
         flat, times, hid, (out0, out1), (dn20, dn21), cot, qkv, probs, attn_w, vec, base, steps, before
     )
     steps = row_count // 2
     if cube:
+        out1, sum1.ahead, sum0.first = meet(out1, sum1.ahead, sum0.first)
+        sum1.send()
         sum0.send()
-        sum1.send()
         (hid,) = hold(sum0.ahead, hid)
     *before, sums0 = backward(hid, 0, 1, ())
     if cube:
+        sums0, sum0.second, sum1.came = meet(sums0, sum0.second, sum1.came)
+        sum0.send()
         sum1.send()
-        sum0.send()
-        (hid,) = hold(sum1.ahead, *hold(sum0.ahead, hid))
+        (hid,) = hold(sum1.ahead, *hold(sum0.ahead[0], hid))
     layer_out, d_tokens, d_time, dbr, dqkv, sums1 = backward(hid, 1, steps - 1, before)
     if cube:
-        sum0.send()
+        dqkv, sum0.rest, sum1.first = meet(dqkv, sum0.rest, sum1.first)
         sum1.send()
-        (dqkv,) = hold(sum1.ahead, *hold(sum0.ahead[0], dqkv))
-    attn0 = CubeSum(*weight_grad(place, n1, dqkv, 0, 2))
+        (dqkv,) = hold(sum1.ahead, dqkv)
+    grads = weight_grad(place, n1, dqkv, att, dbr, sums0, sums1, dbfc0, dbfc1)
+    attn0, attn1 = CubeSum(*grads[:2]), CubeSum(*grads[2:])
     if cube:
-        attn0.send()
-        attn0.keep, dbr = lax.optimization_barrier((attn0.keep, dbr))
-    attn1 = CubeSum(*weight_grad(place, n1, dqkv, 2, 1, (att, dbr, sums0, sums1, dbfc0, dbfc1)))
-    if cube:
+        attn0.ahead, attn1.ahead, sum1.second = meet(attn0.ahead, attn1.ahead, sum1.second)
         attn0.send()
         attn1.send()
+        attn0.send()
         attn1.send()
-        sum1.second, *sum0.rest = hold(attn1.ahead, sum1.second, *sum0.rest)
+        (sum1.second,) = hold(attn1.ahead, sum1.second)
         sum1.send()
         attn0.send()
         attn1.send()
-        sum1.rest = hold(attn1.ahead, *sum1.rest)
         attn0.send()
         attn1.send()
+        sum1.rest = hold(attn1.ahead[0], *sum1.rest)
+        attn0.rest = hold(attn1.ahead[0], *attn0.rest)
         own_ffn = jnp.stack([sum0.total(), sum1.total()])
-        (own_ffn,) = hold(attn1.ahead[0], own_ffn)
         own_attn = jnp.concatenate([attn0.total(), attn1.total()], axis=1)
         own_out = own_ffn[:, blocks:].reshape(ratio * own, width)
         own_fc = own_ffn[:, :blocks].transpose(2, 0, 1, 3).reshape(own, halves, PIECES, blocks * own)

time: 278 us -> 248 us (0.89)
  between operations: 14.7 us -> 1.42 us
  waiting for transfers between devices: 80.9 us -> 68.2 us
  Pallas kernels: 112 us -> 104 us
  starting transfers between devices: 37.9 us -> 44 us
  local copies, waits for them, and re-layouts: 13.9 us -> 9.61 us
    all_gather x1 -> x0, waiting for transfers between devices: 13.1 us -> none  [on_device(): ffn_full = lax.all_gather(ffn_block.reshape(-1, own, width), 'dp', axis=0)]
    pallas_call x2, Pallas kernels: 38.3 us -> 31.6 us  [attn_backward(): pl.pallas_call(functools.partial(attn_backward_body, rows=rows), grid=(st...]
    ppermute x31 -> x45, starting transfers between devices: 37.9 us -> 44 us  [exchange(): return lax.ppermute(array, 'dp', [(i, partner(i)) for i in range(PIECES)])]
    unnamed x55 -> x45, local copies, waits for them, and re-layouts: 5.1 us -> 0.98 us
    pallas_call x2 -> x1, Pallas kernels: 9.49 us -> 8.86 us  [weight_grad(): pl.pallas_call(weight_grad_body, grid=(4,), in_specs=[pl.BlockSpec(memory...]
    ppermute x31 -> x45, waiting for transfers between devices: 67.8 us -> 68.2 us  [exchange(): return lax.ppermute(array, 'dp', [(i, partner(i)) for i in range(PIECES)])]
  transfers between devices with their start and end apart: 32 -> 45, of which waited for: 14 -> 18; matrix products, arithmetic and copies ran while one was open for 5% -> 7% of each run, Pallas kernels for 31% -> 43%
where the time goes in v3:
time: 248 us; the launch traced here: 244 us
  Pallas kernels  104 us (42%)
  waiting for transfers between devices  68.2 us (28%)
  starting transfers between devices  44 us (18%)
  other arithmetic  17 us (7%)
  local copies, waits for them, and re-layouts  9.61 us (4%)
    ppermute x45, waiting for transfers between devices, exchange(): return lax.ppermute(array, 'dp', [(i, partner(i)) for i in range(PIECES)])  68.2 us
    pallas_call x2, Pallas kernels, ffn(): pl.pallas_call(functools.partial(ffn_body, tm=tm, sub=sub, half=half), gr...  44.8 us
    ppermute x45, starting transfers between devices, exchange(): return lax.ppermute(array, 'dp', [(i, partner(i)) for i in range(PIECES)])  44 us
    pallas_call x2, Pallas kernels, attn_backward(): pl.pallas_call(functools.partial(attn_backward_body, rows=rows), grid=(st...  31.6 us
    pallas_call x1, Pallas kernels, attn_forward(): pl.pallas_call(functools.partial(attn_forward_body, rows=rows), grid=(row...  18.6 us
    pallas_call x1, Pallas kernels, weight_grad(): pl.pallas_call(weight_grad_body, grid=(4,), in_specs=[pl.BlockSpec(memory...  8.86 us
  transfers between devices with their start and end apart: 45, of which 18 were waited for; matrix products, arithmetic and copies ran while one was open for 7% of the time, Pallas kernels for 43%

profile of v3, /device:TPU:0, one launch (start us, length us, event | category | flops | bytes accessed | tf_op | source)
XLA Modules:
  0.0 244.2 jit_solution(2333962566019458051)
XLA Ops:
  3.3 5.1 %collective-permute-start.2 = (bf16[24,3200]{1,0:T(8,128)(2,1)S(1)}, bf16[24,3200]{1,0:T(8,128)(2,1)S(1)}, u32[]{:S(2)}, u32[]{:S(2)}) collective-permute-start(bf16[24,3200]{1,0:T(8,128)(2,1)S(1)} %get-tuple-element.209), channel_id=1, source_target_pairs={{0,24},{1,25},{2,26},{3,27},{4,28},{5,29},{6,30},{7,31},{8,0},{9,1... | collective-permute-start | bytes 460808 | tf_op jit(solution)/shard_map/ppermute | solution.py:530
  12.9 8.6 %collective-permute-done.1 = bf16[24,3200]{1,0:T(8,128)(2,1)S(1)} collective-permute-done((bf16[24,3200]{1,0:T(8,128)(2,1)S(1)}, bf16[24,3200]{1,0:T(8,128)(2,1)S(1)}, u32[]{:S(2)}, u32[]{:S(2)}) %collective-permute-start.1) | collective-permute-done | bytes 153632 | tf_op jit(solution)/shard_map/ppermute | solution.py:530
  25.9 2.0 collective-permute-start.4
  29.0 9.4 %collective-permute-done.5 = bf16[4,24,768]{2,1,0:T(8,128)(2,1)S(1)} collective-permute-done((bf16[4,24,768]{2,1,0:T(8,128)(2,1)S(1)}, bf16[4,24,768]{2,1,0:T(8,128)(2,1)S(1)}, u32[]{:S(2)}, u32[]{:S(2)}) %collective-permute-start.5) | collective-permute-done | bytes 147488 | tf_op jit(solution)/shard_map/ppermute | solution.py:530
  41.8 2.0 collective-permute-start.9
  43.9 2.8 %collective-permute-done.11 = bf16[4,24,768]{2,1,0:T(8,128)(2,1)S(1)} collective-permute-done((bf16[4,24,768]{2,1,0:T(8,128)(2,1)S(1)}, bf16[4,24,768]{2,1,0:T(8,128)(2,1)S(1)}, u32[]{:S(2)}, u32[]{:S(2)}) %collective-permute-start.11) | collective-permute-done | bytes 147488 | tf_op jit(solution)/shard_map/ppermute | solution.py:530
  46.6 8.1 %collective-permute-done.10 = bf16[4,24,768]{2,1,0:T(8,128)(2,1)S(1)} collective-permute-done((bf16[4,24,768]{2,1,0:T(8,128)(2,1)S(1)}, bf16[4,24,768]{2,1,0:T(8,128)(2,1)S(1)}, u32[]{:S(2)}, u32[]{:S(2)}) %collective-permute-start.10) | collective-permute-done | bytes 147488 | tf_op jit(solution)/shard_map/ppermute | solution.py:530
  55.5 5.9 %collective-permute-done.7.mine1 = bf16[2,4,24,3200]{3,2,1,0:T(8,128)(2,1)S(1)} collective-permute-done((bf16[2,4,24,3200]{3,2,1,0:T(8,128)(2,1)S(1)}, bf16[2,4,24,3200]{3,2,1,0:T(8,128)(2,1)S(1)}, u32[]{:S(2)}, u32[]{:S(2)}) %collective-permute-start.7) | collective-permute-done | bytes 1228832 | tf_op jit(solution)/shard_map/ppermute | solution.py:530
  64.5 18.6 %attn_forward.1 = (bf16[1024,768]{1,0:T(8,128)(2,1)}, bf16[1024,2304]{1,0:T(8,128)(2,1)}, bf16[8,6,256,128]{3,2,1,0:T(8,128)(2,1)}, bf16[1024,768]{1,0:T(8,128)(...) custom-call(s32[4]{0:T(128)S(1)} %pad_add_fusion.place, ...), custom_call_target="tpu_custom_call" | custom-call | flops 16000000000 | bytes 20000000 | tf_op jit(solution)/shard_map/attn_forward/pallas_call | solution.py:172
  83.1 2.1 collective-permute-done.14.mine1
  85.7 2.4 collective-permute-done.17.other1
  88.1 22.6 %ffn.2 = (bf16[1024,768]{1,0:T(8,128)(2,1)}, bf16[1024,768]{1,0:T(8,128)(2,1)}, f32[1,1536]{1,0:T(1,128)S(1)}, bf16[2,2,4,4,24,768]{5,4,3,2,1,0:T(8,128)(2,1)}, bf16[2,2,4,4,24,768]{5,4,3,2,1,0:T(8,128)(2,1)}) custom-call(s32[4]{0:T(128)S(1)} %pad_add_fusion.place, bf16[1024,768]{1,0:T(8,128)(2,1)} %get-tuple-element.124.n2, bf16[1024,768]{1,0:T(8,128)(2,1)} %bitcast.292, ...), custom_call_target="tpu_custom_call" | custom-call | flops 15000000512 | bytes 20000000 | tf_op jit(solution)/shard_map/ffn/pallas_call | solution.py:288
  111.4 6.2 %collective-permute-done.19 = bf16[2,2,4,4,24,768]{5,4,3,2,1,0:T(8,128)(2,1)S(1)} collective-permute-done((bf16[2,2,4,4,24,768]{5,4,3,2,1,0:T(8,128)(2,1)}, bf16[2,2,4,4,24,768]{5,4,3,2,1,0:T(8,128)(2,1)S(1)}, u32[]{:S(2)}, u32[]{:S(2)}) %collective-permute-start.19) | collective-permute-done | bytes 2359328 | tf_op jit(solution)/shard_map/ppermute | solution.py:530
  117.5 2.4 fusion
  120.2 22.2 %ffn.3 = (bf16[1024,768]{1,0:T(8,128)(2,1)}, bf16[1024,768]{1,0:T(8,128)(2,1)}, f32[1,1536]{1,0:T(1,128)S(1)}, bf16[2,2,4,4,24,768]{5,4,3,2,1,0:T(8,128)(2,1)}, bf16[2,2,4,4,24,768]{5,4,3,2,1,0:T(8,128)(2,1)}) custom-call(s32[4]{0:T(128)S(1)} %pad_add_fusion.place, bf16[1024,768]{1,0:T(8,128)(2,1)} %get-tuple-element.124.n2, bf16[1024,768]{1,0:T(8,128)(2,1)} %bitcast.293, ...), custom_call_target="tpu_custom_call" | custom-call | flops 15000000512 | bytes 20000000 | tf_op jit(solution)/shard_map/ffn/pallas_call | solution.py:288
  145.5 10.3 %attn_backward.2 = (bf16[1024,768]{1,0:T(8,128)(2,1)}, f32[1024,768]{1,0:T(8,128)}, f32[8,1,768]{2,1,0:T(1,128)S(1)}, bf16[1024,768]{1,0:T(8,128)(2,1)S(1)}, bf1...) custom-call(bf16[1024,768]{1,0:T(8,128)(2,1)S(1)} %bitcast.287, bf16[8,1,768]{2,1,0:T(2,128)(2,1)S(1)} %copy.48.time, ...), custom_call_target="tpu_custom_call" | custom-call | flops 6000000000 | bytes 10000000 | tf_op jit(solution)/shard_map/attn_backward/pallas_call | solution.py:408
  157.7 2.0 collective-permute-start.27
  163.2 21.3 %attn_backward.3 = (bf16[1024,768]{1,0:T(8,128)(2,1)}, f32[1024,768]{1,0:T(8,128)}, f32[8,1,768]{2,1,0:T(1,128)S(1)}, bf16[1024,768]{1,0:T(8,128)(2,1)S(1)}, bf1...) custom-call(bf16[1024,768]{1,0:T(8,128)(2,1)S(1)} %bitcast.288, ...), custom_call_target="tpu_custom_call", output_to_operand_aliasing={{0}: (12, {}), {1}: (13, {}), {2}: (14, {}), {3}: (15, {}),... | custom-call | flops 17999998976 | bytes 30000000 | tf_op jit(solution)/shard_map/attn_backward/pallas_call | solution.py:408
  186.2 8.9 %weight_grad.1 = (bf16[2,2,4,24,1536]{4,3,2,1,0:T(8,128)(2,1)S(1)}, bf16[2,2,4,24,1536]{4,3,2,1,0:T(8,128)(2,1)S(1)}, bf16[2,2,4,24,1664]{4,3,2,1,0:T(8,128)(2,1)S(1)}, bf16[2,2,4,24,1664]{4,3,2,1,0:T(8,128)(2,1)S(1)}) custom-call(s32[4]{0:T(128)S(1)} %pad_add_fusion.place, bf16[1024,768]{1,0:T(8,128)(2,1)} %get-tuple-element.154.n1, ...), custom_call_target="tpu_custom_call" | custom-call | flops 5000000000 | bytes 16000000 | tf_op jit(solution)/shard_map/weight_grad/pallas_call | solution.py:508
  205.3 2.8 %collective-permute-done.37 = bf16[2,4,24,1536]{3,2,1,0:T(8,128)(2,1)S(1)} collective-permute-done((bf16[2,4,24,1536]{3,2,1,0:T(8,128)(2,1)S(1)}, bf16[2,4,24,1536]{3,2,1,0:T(8,128)(2,1)S(1)}, u32[]{:S(2)}, u32[]{:S(2)}) %collective-permute-start.37) | collective-permute-done | bytes 589856 | tf_op jit(solution)/shard_map/ppermute | solution.py:530
  209.3 8.8 %collective-permute-done.31 = bf16[2,4,24,1664]{3,2,1,0:T(8,128)(2,1)S(1)} collective-permute-done((bf16[2,4,24,1664]{3,2,1,0:T(8,128)(2,1)S(1)}, bf16[2,4,24,1664]{3,2,1,0:T(8,128)(2,1)S(1)}, u32[]{:S(2)}, u32[]{:S(2)}) %collective-permute-start.31) | collective-permute-done | bytes 639008 | tf_op jit(solution)/shard_map/ppermute | solution.py:530
  221.5 3.8 %collective-permute-done.32 = bf16[4,24,1664]{2,1,0:T(8,128)(2,1)S(1)} collective-permute-done((bf16[4,24,1664]{2,1,0:T(8,128)(2,1)S(1)}, bf16[4,24,1664]{2,1,0:T(8,128)(2,1)S(1)}, u32[]{:S(2)}, u32[]{:S(2)}) %collective-permute-start.32) | collective-permute-done | bytes 319520 | tf_op jit(solution)/shard_map/ppermute | solution.py:530
  229.0 2.3 collective-permute-done.40
  231.5 3.1 %collective-permute-start.34 = (bf16[24,1664]{1,0:T(8,128)(2,1)}, bf16[24,1664]{1,0:T(8,128)(2,1)}, u32[]{:S(2)}, u32[]{:S(2)}) collective-permute-start(bf16[24,1664]{1,0:T(8,128)(2,1)} %get-tuple-element.190), channel_id=1, source_target_pairs={{0,16},{1,17},{2,18},{3,19},{4,20},{5,21},{6,22},{7,23},{8,24},{9,... | collective-permute-start | bytes 239624 | tf_op jit(solution)/shard_map/ppermute | solution.py:530
  (161 shorter events, 59.1 us)
Async XLA Ops:
  8.4 13.0 %collective-permute-start.1 = (bf16[24,3200]{1,0:T(8,128)(2,1)S(1)}, bf16[24,3200]{1,0:T(8,128)(2,1)S(1)}, u32[]{:S(2)}, u32[]{:S(2)}) collective-permute-start(bf16[24,3200]{1,0:T(8,128)(2,1)S(1)} %get-tuple-element.209), channel_id=1, source_target_pairs={{0,16},{1,17},{2,18},{3,19},{4,20},{5,21},{6,22},{7,23},{8,24},{9,... | collective-permute-start | bytes 460808 | tf_op jit(solution)/shard_map/ppermute | solution.py:530
  8.4 13.0 %collective-permute-start = (bf16[24,3200]{1,0:T(8,128)(2,1)S(1)}, bf16[24,3200]{1,0:T(8,128)(2,1)S(1)}, u32[]{:S(2)}, u32[]{:S(2)}) collective-permute-start(bf16[24,3200]{1,0:T(8,128)(2,1)S(1)} %get-tuple-element.209), channel_id=1, source_target_pairs={{0,8},{1,9},{2,10},{3,11},{4,12},{5,13},{6,14},{7,15},{8,16},{9,17... | collective-permute-start | bytes 460808 | tf_op jit(solution)/shard_map/ppermute | solution.py:530
  21.6 16.8 %collective-permute-start.3 = (bf16[4,24,3200]{2,1,0:T(8,128)(2,1)S(1)}, bf16[4,24,3200]{2,1,0:T(8,128)(2,1)S(1)}, u32[]{:S(2)}, u32[]{:S(2)}) collective-permute-start(bf16[4,24,3200]{2,1,0:T(8,128)(2,1)S(1)} %get-tuple-element.195), channel_id=1, source_target_pairs={{0,2},{1,5},{2,0},{3,7},{4,6},{5,1},{6,4},{7,3},{8,10},{9,13},{10,... | collective-permute-start | bytes 1843208 | tf_op jit(solution)/shard_map/ppermute | solution.py:530
  24.4 14.0 %collective-permute-start.5 = (bf16[4,24,768]{2,1,0:T(8,128)(2,1)S(1)}, bf16[4,24,768]{2,1,0:T(8,128)(2,1)S(1)}, u32[]{:S(2)}, u32[]{:S(2)}) collective-permute-start(bf16[4,24,768]{2,1,0:T(8,128)(2,1)S(1)} %bitcast.299), channel_id=1, source_target_pairs={{0,16},{1,17},{2,18},{3,19},{4,20},{5,21},{6,22},{7,23},{8,24},{9,... | collective-permute-start | bytes 442376 | tf_op jit(solution)/shard_map/ppermute | solution.py:530
  38.5 22.9 %collective-permute-start.7 = (bf16[2,4,24,3200]{3,2,1,0:T(8,128)(2,1)S(1)}, bf16[2,4,24,3200]{3,2,1,0:T(8,128)(2,1)S(1)}, u32[]{:S(2)}, u32[]{:S(2)}) collective-permute-start(bf16[2,4,24,3200]{3,2,1,0:T(8,128)(2,1)S(1)} %pad_maximum_fusion.mine0), channel_id=1, source_target_pairs={{0,4},{1,3},{2,6},{3,1},{4,0},{5,7},{6,2},{7,5},{8,12},{9,11},{10,... | collective-permute-start | bytes 3686408 | tf_op jit(solution)/shard_map/ppermute | solution.py:530
  39.2 16.3 %collective-permute-start.8 = (bf16[4,4,24,768]{3,2,1,0:T(8,128)(2,1)S(1)}, bf16[4,4,24,768]{3,2,1,0:T(8,128)(2,1)S(1)}, u32[]{:S(2)}, u32[]{:S(2)}) collective-permute-start(bf16[4,4,24,768]{3,2,1,0:T(8,128)(2,1)S(1)} %get-tuple-element.201), channel_id=1, source_target_pairs={{0,2},{1,5},{2,0},{3,7},{4,6},{5,1},{6,4},{7,3},{8,10},{9,13},{10,... | collective-permute-start | bytes 1769480 | tf_op jit(solution)/shard_map/ppermute | solution.py:530
  40.8 14.0 %collective-permute-start.10 = (bf16[4,24,768]{2,1,0:T(8,128)(2,1)S(1)}, bf16[4,24,768]{2,1,0:T(8,128)(2,1)S(1)}, u32[]{:S(2)}, u32[]{:S(2)}) collective-permute-start(bf16[4,24,768]{2,1,0:T(8,128)(2,1)S(1)} %get-tuple-element.99), channel_id=1, source_target_pairs={{0,16},{1,17},{2,18},{3,19},{4,20},{5,21},{6,22},{7,23},{8,24},{9,... | collective-permute-start | bytes 442376 | tf_op jit(solution)/shard_map/ppermute | solution.py:530
  41.8 12.9 %collective-permute-start.9 = (bf16[4,24,768]{2,1,0:T(8,128)(2,1)S(1)}, bf16[4,24,768]{2,1,0:T(8,128)(2,1)S(1)}, u32[]{:S(2)}, u32[]{:S(2)}) collective-permute-start(bf16[4,24,768]{2,1,0:T(8,128)(2,1)S(1)} %get-tuple-element.99), channel_id=1, source_target_pairs={{0,8},{1,9},{2,10},{3,11},{4,12},{5,13},{6,14},{7,15},{8,16},{9,17... | collective-permute-start | bytes 442376 | tf_op jit(solution)/shard_map/ppermute | solution.py:530
  46.6 17.5 %collective-permute-start.12 = (bf16[2,4,24,3200]{3,2,1,0:T(8,128)(2,1)S(1)}, bf16[2,4,24,3200]{3,2,1,0:T(8,128)(2,1)}, u32[]{:S(2)}, u32[]{:S(2)}) collective-permute-start(bf16[2,4,24,3200]{3,2,1,0:T(8,128)(2,1)S(1)} %pad_maximum_fusion.mine0), channel_id=1, source_target_pairs={{0,1},{1,0},{2,3},{3,2},{4,5},{5,4},{6,7},{7,6},{8,9},{9,8},{10,11... | collective-permute-start | bytes 3686408 | tf_op jit(solution)/shard_map/ppermute | solution.py:530
  62.9 22.8 %collective-permute-start.16 = (bf16[2,4,4,24,768]{4,3,2,1,0:T(8,128)(2,1)S(1)}, bf16[2,4,4,24,768]{4,3,2,1,0:T(8,128)(2,1)S(1)}, u32[]{:S(2)}, u32[]{:S(2)}) collective-permute-start(bf16[2,4,4,24,768]{4,3,2,1,0:T(8,128)(2,1)S(1)} %pad_maximum_fusion.1.mine0), channel_id=1, source_target_pairs={{0,1},{1,0},{2,3},{3,2},{4,5},{5,4},{6,7},{7,6},{8,9},{9,8},{10,11... | collective-permute-start | bytes 3538952 | tf_op jit(solution)/shard_map/ppermute | solution.py:530
  63.4 21.8 %collective-permute-start.14 = (bf16[2,4,4,24,768]{4,3,2,1,0:T(8,128)(2,1)S(1)}, bf16[2,4,4,24,768]{4,3,2,1,0:T(8,128)(2,1)S(1)}, u32[]{:S(2)}, u32[]{:S(2)}) collective-permute-start(bf16[2,4,4,24,768]{4,3,2,1,0:T(8,128)(2,1)S(1)} %pad_maximum_fusion.1.mine0), channel_id=1, source_target_pairs={{0,4},{1,3},{2,6},{3,1},{4,0},{5,7},{6,2},{7,5},{8,12},{9,11},{10,... | collective-permute-start | bytes 3538952 | tf_op jit(solution)/shard_map/ppermute | solution.py:530
  63.8 19.4 %collective-permute-start.15 = (bf16[4,4,24,768]{3,2,1,0:T(8,128)(2,1)S(1)}, bf16[4,4,24,768]{3,2,1,0:T(8,128)(2,1)S(1)}, u32[]{:S(2)}, u32[]{:S(2)}) collective-permute-start(bf16[4,4,24,768]{3,2,1,0:T(8,128)(2,1)S(1)} %get-tuple-element.199), channel_id=1, source_target_pairs={{0,2},{1,5},{2,0},{3,7},{4,6},{5,1},{6,4},{7,3},{8,10},{9,13},{10,... | collective-permute-start | bytes 1769480 | tf_op jit(solution)/shard_map/ppermute | solution.py:530
  85.3 25.3 %collective-permute-start.18 = (bf16[2,4,4,24,768]{4,3,2,1,0:T(8,128)(2,1)S(1)}, bf16[2,4,4,24,768]{4,3,2,1,0:T(8,128)(2,1)S(1)}, u32[]{:S(2)}, u32[]{:S(2)}) collective-permute-start(bf16[2,4,4,24,768]{4,3,2,1,0:T(8,128)(2,1)S(1)} %pad_maximum_fusion.2.mine0), channel_id=1, source_target_pairs={{0,4},{1,3},{2,6},{3,1},{4,0},{5,7},{6,2},{7,5},{8,12},{9,11},{10,... | collective-permute-start | bytes 3538952 | tf_op jit(solution)/shard_map/ppermute | solution.py:530
  120.0 22.5 %collective-permute-start.22 = (bf16[2,4,4,24,768]{4,3,2,1,0:T(8,128)(2,1)S(1)}, bf16[2,4,4,24,768]{4,3,2,1,0:T(8,128)(2,1)}, u32[]{:S(2)}, u32[]{:S(2)}) collective-permute-start(bf16[2,4,4,24,768]{4,3,2,1,0:T(8,128)(2,1)S(1)} %fusion), channel_id=1, source_target_pairs={{0,4},{1,3},{2,6},{3,1},{4,0},{5,7},{6,2},{7,5},{8,12},{9,11},{10,... | collective-permute-start | bytes 3538952 | tf_op jit(solution)/shard_map/ppermute | solution.py:530
  142.5 13.3 %collective-permute-start.24 = (bf16[2,2,4,4,24,768]{5,4,3,2,1,0:T(8,128)(2,1)}, bf16[2,2,4,4,24,768]{5,4,3,2,1,0:T(8,128)(2,1)S(1)}, u32[]{:S(2)}, u32[]{:S(2)}) collective-permute-start(bf16[2,2,4,4,24,768]{5,4,3,2,1,0:T(8,128)(2,1)} %get-tuple-element.141), channel_id=1, source_target_pairs={{0,1},{1,0},{2,3},{3,2},{4,5},{5,4},{6,7},{7,6},{8,9},{9,8},{10,11... | collective-permute-start | bytes 7077896 | tf_op jit(solution)/shard_map/ppermute | solution.py:530
  157.6 26.9 %collective-permute-start.25 = (bf16[4,24,768]{2,1,0:T(8,128)(2,1)S(1)}, bf16[4,24,768]{2,1,0:T(8,128)(2,1)S(1)}, u32[]{:S(2)}, u32[]{:S(2)}) collective-permute-start(bf16[4,24,768]{2,1,0:T(8,128)(2,1)S(1)} %get-tuple-element.187), channel_id=1, source_target_pairs={{0,24},{1,25},{2,26},{3,27},{4,28},{5,29},{6,30},{7,31},{8,0},{9,1... | collective-permute-start | bytes 442376 | tf_op jit(solution)/shard_map/ppermute | solution.py:530
  157.7 26.8 %collective-permute-start.27 = (bf16[4,24,768]{2,1,0:T(8,128)(2,1)S(1)}, bf16[4,24,768]{2,1,0:T(8,128)(2,1)S(1)}, u32[]{:S(2)}, u32[]{:S(2)}) collective-permute-start(bf16[4,24,768]{2,1,0:T(8,128)(2,1)S(1)} %get-tuple-element.185), channel_id=1, source_target_pairs={{0,8},{1,9},{2,10},{3,11},{4,12},{5,13},{6,14},{7,15},{8,16},{9,17... | collective-permute-start | bytes 442376 | tf_op jit(solution)/shard_map/ppermute | solution.py:530
  159.7 24.8 %collective-permute-start.26 = (bf16[4,24,768]{2,1,0:T(8,128)(2,1)S(1)}, bf16[4,24,768]{2,1,0:T(8,128)(2,1)S(1)}, u32[]{:S(2)}, u32[]{:S(2)}) collective-permute-start(bf16[4,24,768]{2,1,0:T(8,128)(2,1)S(1)} %get-tuple-element.186), channel_id=1, source_target_pairs={{0,16},{1,17},{2,18},{3,19},{4,20},{5,21},{6,22},{7,23},{8,24},{9,... | collective-permute-start | bytes 442376 | tf_op jit(solution)/shard_map/ppermute | solution.py:530
  161.9 22.7 %collective-permute-start.28 = (bf16[2,4,4,24,768]{4,3,2,1,0:T(8,128)(2,1)S(1)}, bf16[2,4,4,24,768]{4,3,2,1,0:T(8,128)(2,1)S(1)}, u32[]{:S(2)}, u32[]{:S(2)}) collective-permute-start(bf16[2,4,4,24,768]{4,3,2,1,0:T(8,128)(2,1)S(1)} %fusion.1), channel_id=1, source_target_pairs={{0,4},{1,3},{2,6},{3,1},{4,0},{5,7},{6,2},{7,5},{8,12},{9,11},{10,... | collective-permute-start | bytes 3538952 | tf_op jit(solution)/shard_map/ppermute | solution.py:530
  200.0 18.1 %collective-permute-start.31 = (bf16[2,4,24,1664]{3,2,1,0:T(8,128)(2,1)S(1)}, bf16[2,4,24,1664]{3,2,1,0:T(8,128)(2,1)S(1)}, u32[]{:S(2)}, u32[]{:S(2)}) collective-permute-start(bf16[2,4,24,1664]{3,2,1,0:T(8,128)(2,1)S(1)} %fusion.4), channel_id=1, source_target_pairs={{0,4},{1,3},{2,6},{3,1},{4,0},{5,7},{6,2},{7,5},{8,12},{9,11},{10,... | collective-permute-start | bytes 1916936 | tf_op jit(solution)/shard_map/ppermute | solution.py:530
  202.1 26.9 %collective-permute-start.42 = (bf16[4,24,768]{2,1,0:T(8,128)(2,1)S(1)}, bf16[4,24,768]{2,1,0:T(8,128)(2,1)S(1)}, u32[]{:S(2)}, u32[]{:S(2)}) collective-permute-start(bf16[4,24,768]{2,1,0:T(8,128)(2,1)S(1)} %get-tuple-element.182), channel_id=1, source_target_pairs={{0,24},{1,25},{2,26},{3,27},{4,28},{5,29},{6,30},{7,31},{8,0},{9,1... | collective-permute-start | bytes 442376 | tf_op jit(solution)/shard_map/ppermute | solution.py:530
  203.1 17.3 %collective-permute-start.44 = (bf16[4,24,768]{2,1,0:T(8,128)(2,1)S(1)}, bf16[4,24,768]{2,1,0:T(8,128)(2,1)S(1)}, u32[]{:S(2)}, u32[]{:S(2)}) collective-permute-start(bf16[4,24,768]{2,1,0:T(8,128)(2,1)S(1)} %get-tuple-element.183), channel_id=1, source_target_pairs={{0,8},{1,9},{2,10},{3,11},{4,12},{5,13},{6,14},{7,15},{8,16},{9,17... | collective-permute-start | bytes 442376 | tf_op jit(solution)/shard_map/ppermute | solution.py:530
  204.2 22.9 %collective-permute-start.43 = (bf16[4,24,768]{2,1,0:T(8,128)(2,1)S(1)}, bf16[4,24,768]{2,1,0:T(8,128)(2,1)S(1)}, u32[]{:S(2)}, u32[]{:S(2)}) collective-permute-start(bf16[4,24,768]{2,1,0:T(8,128)(2,1)S(1)} %get-tuple-element.184), channel_id=1, source_target_pairs={{0,16},{1,17},{2,18},{3,19},{4,20},{5,21},{6,22},{7,23},{8,24},{9,... | collective-permute-start | bytes 442376 | tf_op jit(solution)/shard_map/ppermute | solution.py:530
  227.1 13.2 %collective-permute-start.33 = (bf16[24,1664]{1,0:T(8,128)(2,1)}, bf16[24,1664]{1,0:T(8,128)(2,1)}, u32[]{:S(2)}, u32[]{:S(2)}) collective-permute-start(bf16[24,1664]{1,0:T(8,128)(2,1)} %get-tuple-element.188), channel_id=1, source_target_pairs={{0,24},{1,25},{2,26},{3,27},{4,28},{5,29},{6,30},{7,31},{8,0},{9,1... | collective-permute-start | bytes 239624 | tf_op jit(solution)/shard_map/ppermute | solution.py:530
  (43 other events, 418.5 us)
